TPU v7x, 32 devices: a whole 2x2x4 slice. The times are simulated.
32 devices in a mesh: dp: 2 (over x), expert: 16 (over z, y, core).
Axes of the slice: x: 2, y: 2, z: 4, core: 2. Of those that a mesh axis runs over, the one named last changes fastest.
Arguments:
- tokens: bfloat16 [2, 32, 64, 2048], P(None, ('dp', 'expert')), may hold values from -6 to 6
- cotangent: bfloat16 [2, 32, 64, 2048], P(None, ('dp', 'expert')), may hold values from -6 to 6
- routes: int32 [2, 32, 64, 6], P(None, ('dp', 'expert')), may hold values from 0 to 15, all different within a row; in each aligned block of 64 rows (0 to 63, 64 to 127, ..., all dimensions but the last counted through in order) at most 32 rows name the same one
- segments: int32 [2, 32, 64], P(None, ('dp', 'expert')), may hold values from 0 to 2, never falling along the last dimension, each value on 1 to 32 neighbouring positions
- attn_gain: bfloat16 [2048], P(('dp', 'expert')), may hold values from 0.5 to 1.5
- q_weight: bfloat16 [2048, 3072], P(('dp', 'expert')), may hold values from -0.125 to 0.125
- kv_down: bfloat16 [2048, 576], P(('dp', 'expert')), may hold values from -0.125 to 0.125
- kv_gain: bfloat16 [512], P(('dp', 'expert')), may hold values from 0.5 to 1.5
- kv_up: bfloat16 [512, 4096], P(('dp', 'expert')), may hold values from -0.25 to 0.25
- out_weight: bfloat16 [2048, 2048], P(('dp', 'expert')), may hold values from -0.5 to 0.5
- ffn_gain: bfloat16 [2048], P(('dp', 'expert')), may hold values from 0.5 to 1.5
- router: bfloat16 [2048, 16], P(('dp', 'expert')), may hold values from -0.0625 to 0.0625
- shared_gate: bfloat16 [2048, 2816], P(('dp', 'expert')), may hold values from -0.125 to 0.125
- shared_up: bfloat16 [2048, 2816], P(('dp', 'expert')), may hold values from -0.125 to 0.125
- shared_down: bfloat16 [2816, 2048], P(('dp', 'expert')), may hold values from -0.15625 to 0.15625
- expert_gate: bfloat16 [16, 2048, 1408], P('expert', 'dp'), may hold values from -0.125 to 0.125
- expert_up: bfloat16 [16, 2048, 1408], P('expert', 'dp'), may hold values from -0.125 to 0.125
- expert_down: bfloat16 [16, 1408, 2048], P('expert', None, 'dp'), may hold values from -0.625 to 0.625
Outputs:
- out: bfloat16 [2, 32, 64, 2048], P(None, ('dp', 'expert'))
- tokens_grad: bfloat16 [2, 32, 64, 2048], P(None, ('dp', 'expert'))
- attn_gain_grad: float32 [2048], P(('dp', 'expert'))
- q_weight_grad: float32 [2048, 3072], P(('dp', 'expert'))
- kv_down_grad: float32 [2048, 576], P(('dp', 'expert'))
- kv_gain_grad: float32 [512], P(('dp', 'expert'))
- kv_up_grad: float32 [512, 4096], P(('dp', 'expert'))
- out_weight_grad: float32 [2048, 2048], P(('dp', 'expert'))
- ffn_gain_grad: float32 [2048], P(('dp', 'expert'))
- router_grad: float32 [2048, 16], P(('dp', 'expert'))
- shared_gate_grad: float32 [2048, 2816], P(('dp', 'expert'))
- shared_up_grad: float32 [2048, 2816], P(('dp', 'expert'))
- shared_down_grad: float32 [2816, 2048], P(('dp', 'expert'))
- expert_gate_grad: float32 [16, 2048, 1408], P('expert', 'dp')
- expert_up_grad: float32 [16, 2048, 1408], P('expert', 'dp')
- expert_down_grad: float32 [16, 1408, 2048], P('expert', None, 'dp')
Inputs may be any that keep to these rules, and one draw needn't show every extreme that they name: A token's 6 routes are different experts. Within one sequence of one micro-batch no expert is named by more than 32 positions, a bound that some block reaches. `segments`: segment numbers never fall along a sequence.
All inputs are finite; a program needn't handle non-finite values.
Results may differ from a plain program's by a relative error of at most 0.019.
Values may be sent and summed in bfloat16 or wider, within the bound.
A program may use at most 384 MiB of HBM per device.

v0:
```python
import functools

import jax
import jax.numpy as jnp
from jax import lax
from jax.experimental import pallas as pl
from jax.experimental.pallas import tpu as pltpu
from jax.sharding import PartitionSpec as P

D = 2048
HEADS = 16
NOPE = 128
ROPE = 64
VDIM = 128
RANK = 512
TOP = 6
SEQ = 64
MICRO = 2

EPSILON = 1e-06
ROPE_BASE = 10000.0
MASKED = -1e30
BF = jnp.bfloat16
F32 = jnp.float32

MESH_ID = pl.DeviceIdType.MESH


class Grid:
    def __init__(self, mesh):
        self.experts = mesh.shape["expert"]
        self.size = {"p": mesh.shape["dp"], "r": self.experts // 8, "q": 4}
        self.devices = self.size["p"] * self.experts

    def here(self):
        e = lax.axis_index("expert")
        r_size = self.size["r"]
        return {
            "p": lax.axis_index("dp"),
            "q": lax.div(e, 2 * r_size),
            "r": lax.rem(lax.div(e, 2), r_size),
            "c": lax.rem(e, 2),
        }

    def shift(self, at, offsets):
        moved = dict(at)
        for axis, step in offsets.items():
            if step:
                moved[axis] = lax.rem(at[axis] + step, self.size[axis])
        return moved

    def expert_of(self, at):
        return at["q"] * (2 * self.size["r"]) + at["r"] * 2 + at["c"]

    def number(self, at):
        return at["p"] * self.experts + self.expert_of(at)

    def mesh_id(self, at):
        return (at["p"], self.expert_of(at))

    def partners(self, at):
        found = [{**at, "c": 1 - at["c"]}]
        for axis in "pr":
            found += [self.shift(at, {axis: step}) for step in range(1, self.size[axis])]
        return found


def greet(grid, at):
    barrier = pltpu.get_barrier_semaphore()
    partners = grid.partners(at)
    for partner in partners:
        pl.semaphore_signal(barrier, inc=1, device_id=grid.mesh_id(partner), device_id_type=MESH_ID)
    others = len(partners)
    for step in (-1, 1):
        on_line = jnp.logical_and(at["q"] + step >= 0, at["q"] + step < grid.size["q"])
        others = others + on_line.astype(jnp.int32)

        @pl.when(on_line)
        def _():
            other = grid.mesh_id({**at, "q": at["q"] + step})
            pl.semaphore_signal(barrier, inc=1, device_id=other, device_id_type=MESH_ID)

    pl.semaphore_wait(barrier, others)


ALONG = (0, -1, 1, -2, 2, -3, 3)


def gather_kernel(grid, arrays, items, *refs):
    count = len(items)
    ins, outs = refs[:arrays], refs[arrays : 2 * arrays]
    send_sem, recv_sem, core_send, core_recv, own_sem = refs[2 * arrays :]
    at = grid.here()
    sibling = {**at, "c": 1 - at["c"]}
    q_size = grid.size["q"]
    greet(grid, at)
    pending = []
    own_copies = []
    me = grid.number(at)
    for a in range(arrays):
        own = pltpu.make_async_copy(ins[a], outs[a].at[me], own_sem.at[a])
        own.start()
        own_copies.append(own)

    def spans(axis):
        return ALONG if axis == "q" else tuple(range(grid.size[axis]))

    def inside(step):
        return jnp.logical_and(at["q"] + step >= 0, at["q"] + step < q_size)

    def guarded(step, action):
        if step:
            pl.when(inside(step))(action)
        else:
            action()

    def q_part(i, offset):
        return offset[items[i][3].index("q")]

    def slot(i, offset):
        number = 0
        for axis, part in zip(items[i][3], offset):
            number = number * len(spans(axis)) + spans(axis).index(part)
        return number

    def block_of(i, offset, base):
        moved = dict(base)
        for axis, part in zip(items[i][3], offset):
            if part:
                moved[axis] = (
                    base[axis] + part
                    if axis == "q"
                    else lax.rem(base[axis] + part, grid.size[axis])
                )
        return grid.number(moved)

    def views(i, offset, base):
        a, first, width, order = items[i]
        columns = pl.ds(first, width)
        view = outs[a].at[block_of(i, offset, base), :, columns]
        return (ins[a].at[:, columns] if offset == (0, 0, 0) else view), view

    def send(i, offset, landed, target_step, cond_step):
        number = len(pending)

        def copy():
            source, view = views(i, offset, at)
            return pltpu.make_async_remote_copy(
                src_ref=source,
                dst_ref=view,
                send_sem=send_sem.at[number],
                recv_sem=recv_sem.at[i, slot(i, landed)],
                device_id=grid.mesh_id(target_step()),
                device_id_type=MESH_ID,
            )

        guarded(cond_step, lambda: copy().start())
        pending.append((q_part(i, offset), cond_step, copy))

    def forward(i, offset, stage):
        axis = items[i][3][stage]
        if axis == "q":
            part = offset[stage]
            for step in (1, -1) if part == 0 else (1,) if part < 0 else (-1,):
                if abs(part - step) < q_size:
                    landed = offset[:stage] + (part - step,) + offset[stage + 1 :]
                    send(i, offset, landed, lambda step=step: {**at, "q": at["q"] + step}, step)
            return
        for step in range(1, grid.size[axis]):
            part = (offset[stage] - step) % grid.size[axis]
            landed = offset[:stage] + (part,) + offset[stage + 1 :]
            send(i, offset, landed, lambda step=step: grid.shift(at, {axis: step}), 0)

    def across(i, offset):
        def copy():
            source, view = views(i, offset, at)
            return pltpu.make_async_remote_copy(
                src_ref=source,
                dst_ref=view,
                send_sem=core_send.at[i, slot(i, offset)],
                recv_sem=core_recv.at[i, slot(i, offset)],
                device_id=grid.mesh_id(sibling),
                device_id_type=MESH_ID,
            )

        copy().start()
        pending.append((q_part(i, offset), 0, copy))

    def landed_at(i, offset, base, sem):
        view = views(i, offset, base)[1]
        pltpu.make_async_copy(view, view, sem.at[i, slot(i, offset)]).wait()

    def take(i, offset, stage):
        def action():
            landed_at(i, offset, at, recv_sem)
            if items[i][3][stage] == "q":
                forward(i, offset, stage)
            for later in range(stage + 1, 3):
                forward(i, offset, later)
            across(i, offset)

        guarded(q_part(i, offset), action)

    for i in range(count):
        for stage in range(3):
            forward(i, (0, 0, 0), stage)
        across(i, (0, 0, 0))
    ranges = [[spans(axis) for axis in item[3]] for item in items]
    todo = []
    for i in range(count):
        for u in ranges[i][0]:
            for v in ranges[i][1]:
                for w in ranges[i][2]:
                    stage = 2 if w else 1 if v else 0
                    if u or v or w:
                        todo.append((stage, abs(u), abs(v), abs(w), i, (u, v, w)))
    for stage, _, _, _, i, offset in sorted(todo):
        take(i, offset, stage)
    for own in own_copies:
        own.wait()
    for i in range(count):
        for u in ranges[i][0]:
            for v in ranges[i][1]:
                for w in ranges[i][2]:
                    offset = (u, v, w)
                    guarded(
                        q_part(i, offset),
                        functools.partial(landed_at, i, offset, sibling, core_recv),
                    )
    for q_step, cond_step, copy in pending:
        guarded(q_step, functools.partial(guarded, cond_step, lambda: copy().wait_send()))


def gather_all(grid, arrays, items, collective_id):
    count = len(items)
    slots = grid.devices // 2 // 4 * len(ALONG)
    return pl.pallas_call(
        functools.partial(gather_kernel, grid, len(arrays), items),
        out_shape=[jax.ShapeDtypeStruct((grid.devices,) + a.shape, a.dtype) for a in arrays],
        in_specs=[pl.BlockSpec(memory_space=pl.ANY)] * len(arrays),
        out_specs=[pl.BlockSpec(memory_space=pl.ANY)] * len(arrays),
        scratch_shapes=[
            pltpu.SemaphoreType.DMA((count * slots * 2,)),
            pltpu.SemaphoreType.DMA((count, slots)),
            pltpu.SemaphoreType.DMA((count, slots)),
            pltpu.SemaphoreType.DMA((count, slots)),
            pltpu.SemaphoreType.DMA((len(arrays),)),
        ],
        compiler_params=pltpu.CompilerParams(collective_id=collective_id, has_side_effects=True),
        name="gather_all",
    )(*arrays)


def add_rows(target, *parts):
    rows = target.shape[0]
    step = min(16, rows)

    @pl.loop(0, rows // step)
    def _(k):
        block = pl.ds(pl.multiple_of(k * step, step), step)
        total = parts[0][block, :].astype(jnp.float32)
        for part in parts[1:]:
            total = total + part[block, :].astype(jnp.float32)
        target[block, :] = total.astype(target.dtype)


DEPTH = 2
AHEAD = 6


def scatter_kernel(grid, arrays, items, *refs):
    count = len(items)
    ins, outs = refs[:arrays], refs[arrays : 2 * arrays]
    held, crossed = refs[2 * arrays : 3 * arrays], refs[3 * arrays : 4 * arrays]
    landing = refs[4 * arrays : 4 * arrays + 3 * count]
    load_sem, core_send, core_recv, send_sem, recv_sem, line_send, line_recv = refs[
        4 * arrays + 3 * count :
    ]
    at = grid.here()
    sibling = {**at, "c": 1 - at["c"]}
    size = grid.size
    q_size = size["q"]
    greet(grid, at)

    def flat(block):
        p, r, t = block
        return (p * size["r"] + r) * q_size + t

    def owner(base, block):
        p, r, t = block
        return grid.number({**grid.shift(base, {"p": p, "r": r}), "q": t})

    targets = []
    for t in range(q_size // 2):
        targets += [t, q_size - 1 - t]
    blocks = []
    for t in targets:
        near = [(p, r, t) for p in range(size["p"]) for r in range(size["r"])]
        blocks += sorted(near, key=lambda b: -(b[0] > 0) - (b[1] > 0))

    def load(a, block):
        return pltpu.make_async_copy(
            ins[a].at[owner(at, block)], held[a].at[flat(block)], load_sem.at[a, flat(block)]
        )

    def across(a, block):
        return pltpu.make_async_remote_copy(
            src_ref=ins[a].at[owner(sibling, block)],
            dst_ref=crossed[a].at[flat(block)],
            send_sem=core_send.at[a, flat(block)],
            recv_sem=core_recv.at[a, flat(block)],
            device_id=grid.mesh_id(sibling),
            device_id_type=MESH_ID,
        )

    def begin(number):
        if number < len(blocks):
            for a in range(arrays):
                across(a, blocks[number]).start()
                load(a, blocks[number]).start()

    merged = [0]

    def merge_to(block):
        while merged[0] <= blocks.index(block):
            now = blocks[merged[0]]
            for a in range(arrays):
                load(a, now).wait()
                across(a, now).wait_recv()
                view = held[a].at[flat(now)]
                add_rows(view, view, crossed[a].at[flat(now)])
            begin(merged[0] + AHEAD)
            merged[0] += 1

    def held_view(i, block):
        return held[items[i][0]].at[flat(block), :, pl.ds(items[i][1], items[i][2])]

    def block_at(i, first, second, t):
        part = dict(zip(items[i][3], (first, second)))
        return (part["p"], part["r"], t)

    pending = []

    def send(i, stage, steps, t):
        n1, n2 = (size[axis] for axis in items[i][3])
        step = steps[stage]
        slot = ((steps[0] - 1) * n2 + steps[1]) * q_size + t if stage == 0 else (steps[1] - 1) * q_size + t
        sem = slot if stage == 0 else (n1 - 1) * n2 * q_size + slot
        copy = pltpu.make_async_remote_copy(
            src_ref=held_view(i, block_at(i, *steps, t)),
            dst_ref=landing[3 * i + stage].at[slot],
            send_sem=send_sem.at[i, sem],
            recv_sem=recv_sem.at[i, sem],
            device_id=grid.mesh_id(grid.shift(at, {items[i][3][stage]: step})),
            device_id_type=MESH_ID,
        )
        return copy

    def start(i, stage, steps, t):
        copy = send(i, stage, steps, t)
        copy.start()
        pending.append(copy)

    def receive(i, stage, steps, t):
        send(i, stage, steps, t).wait_recv()
        into = (0, steps[1]) if stage == 0 else (0, 0)
        n2 = size[items[i][3][1]]
        slot = ((steps[0] - 1) * n2 + steps[1]) * q_size + t if stage == 0 else (steps[1] - 1) * q_size + t
        view = held_view(i, block_at(i, *into, t))
        add_rows(view, view, landing[3 * i + stage].at[slot])

    def line(i, t, step):
        side = 0 if step > 0 else 1
        return pltpu.make_async_remote_copy(
            src_ref=held_view(i, (0, 0, t)),
            dst_ref=landing[3 * i + 2].at[side * q_size + t],
            send_sem=line_send.at[i, t],
            recv_sem=line_recv.at[i, side * q_size + t],
            device_id=grid.mesh_id({**at, "q": at["q"] + step}),
            device_id_type=MESH_ID,
        )

    def from_line(i, t, step):
        line(i, t, step).wait_recv()
        side = 0 if step > 0 else 1
        view = held_view(i, (0, 0, t))
        add_rows(view, view, landing[3 * i + 2].at[side * q_size + t])

    def along(t):
        q = at["q"]
        for i in range(count):
            if t > 0:

                @pl.when(jnp.logical_and(q > 0, q <= t))
                def _():
                    from_line(i, t, 1)

                @pl.when(q < t)
                def _():
                    line(i, t, 1).start()

            if t < q_size - 1:

                @pl.when(jnp.logical_and(q < q_size - 1, q >= t))
                def _():
                    from_line(i, t, -1)

                @pl.when(q > t)
                def _():
                    line(i, t, -1).start()

    ticks = []
    for t in targets:
        for far in (True, False):
            turn = []
            for i in range(count):
                n1, n2 = (size[axis] for axis in items[i][3])
                for second in range(1, n2) if far else (0,):
                    for first in range(1, n1):
                        turn.append((i, (first, second), t))
            ticks.append((turn, None if far else t))

    def handle(k):
        turn, done = ticks[k]
        for i, steps, t in turn:
            merge_to(block_at(i, 0, steps[1], t))
            receive(i, 0, steps, t)
            if steps[1] and steps[0] == size[items[i][3][0]] - 1:
                start(i, 1, (0, steps[1]), t)

    def close(t):
        for i in range(count):
            for second in range(1, size[items[i][3][1]]):
                receive(i, 1, (0, second), t)

    for number in range(AHEAD):
        begin(number)
    finished = []
    for k in range(len(ticks) + DEPTH):
        if k < len(ticks):
            for i, steps, t in ticks[k][0]:
                merge_to(block_at(i, *steps, t))
                start(i, 0, steps, t)
        if k >= DEPTH:
            handle(k - DEPTH)
            if ticks[k - DEPTH][1] is not None:
                finished.append(ticks[k - DEPTH][1])
                if len(finished) > 1:
                    close(finished[-2])
                    along(finished[-2])
    close(finished[-1])
    along(finished[-1])
    for a in range(arrays):
        add_rows(outs[a], held[a].at[at["q"]])
    for block in blocks:
        for a in range(arrays):
            across(a, block).wait_send()
    for copy in pending:
        copy.wait_send()
    for t in range(q_size):
        for i in range(count):

            @pl.when(at["q"] < t)
            def _():
                line(i, t, 1).wait_send()

            @pl.when(at["q"] > t)
            def _():
                line(i, t, -1).wait_send()


def sum_scattered(grid, arrays, items, collective_id, dtype=jnp.float32):
    count = len(items)
    chips = grid.devices // 2
    q_size = grid.size["q"]
    scratch = [pltpu.VMEM((chips,) + a.shape[1:], a.dtype) for a in arrays] * 2
    most = 0
    for a, _, width, order in items:
        n1, n2 = (grid.size[axis] for axis in order)
        shares = ((n1 - 1) * n2 * q_size, (n2 - 1) * q_size, 2 * q_size)
        most = max(most, shares[0] + shares[1])
        for share in shares:
            scratch.append(pltpu.VMEM((share, arrays[a].shape[1], width), arrays[a].dtype))
    return pl.pallas_call(
        functools.partial(scatter_kernel, grid, len(arrays), items),
        out_shape=[jax.ShapeDtypeStruct(a.shape[1:], dtype) for a in arrays],
        in_specs=[pl.BlockSpec(memory_space=pl.ANY)] * len(arrays),
        out_specs=[pl.BlockSpec(memory_space=pltpu.VMEM)] * len(arrays),
        scratch_shapes=scratch
        + [
            pltpu.SemaphoreType.DMA((len(arrays), chips)),
            pltpu.SemaphoreType.DMA((len(arrays), chips)),
            pltpu.SemaphoreType.DMA((len(arrays), chips)),
            pltpu.SemaphoreType.DMA((count, most)),
            pltpu.SemaphoreType.DMA((count, most)),
            pltpu.SemaphoreType.DMA((count, q_size)),
            pltpu.SemaphoreType.DMA((count, 2 * q_size)),
        ],
        compiler_params=pltpu.CompilerParams(
            collective_id=collective_id, has_side_effects=True, vmem_limit_bytes=60 * 2**20
        ),
        name="sum_scattered",
    )(*arrays)


def normalize(values, gain_row):
    scale_rows = lax.rsqrt(jnp.mean(values * values, -1, keepdims=True) + EPSILON)
    return (values * scale_rows * gain_row, scale_rows)


def normalize_back(values, scale_rows, gain_row, gradient):
    weighted = gradient * gain_row
    gain_grad = jnp.sum(gradient * values * scale_rows, 0)
    inner_mean = jnp.mean(weighted * values, -1, keepdims=True)
    return (
        scale_rows * weighted - values * scale_rows * scale_rows * scale_rows * inner_mean,
        gain_grad,
    )


def rope_tables(length, width):
    half_width = width // 2
    frequency = ROPE_BASE ** (-2.0 * jnp.arange(half_width, dtype=jnp.float32) / width)
    angles = jnp.arange(length, dtype=jnp.float32)[:, None] * frequency[None, :]
    return (jnp.cos(angles), jnp.sin(angles))


def rotate(values, cosine, sine_table):
    half_width = values.shape[-1] // 2
    front_half = values[..., :half_width]
    back_half = values[..., half_width:]
    return jnp.concatenate(
        [
            front_half * cosine - back_half * sine_table,
            back_half * cosine + front_half * sine_table,
        ],
        -1,
    )


def unrotate(gradient, cosine, sine_table):
    half_width = gradient.shape[-1] // 2
    front_half = gradient[..., :half_width]
    back_half = gradient[..., half_width:]
    return jnp.concatenate(
        [
            front_half * cosine + back_half * sine_table,
            back_half * cosine - front_half * sine_table,
        ],
        -1,
    )


def capacity_for(expert_count):
    return min(SEQ, ((4 * SEQ * TOP + 3 * expert_count - 1) // (3 * expert_count) + 7) // 8 * 8)


def silu_parts(pre_act):
    sigma_rows = jax.nn.sigmoid(pre_act)
    return (pre_act * sigma_rows, sigma_rows * (1.0 + pre_act * (1.0 - sigma_rows)))


def attention_mask(segment_row):
    places = jnp.arange(segment_row.shape[0], dtype=jnp.int32)
    return (places[:, None] >= places[None, :]) & (segment_row[:, None] == segment_row[None, :])


def dot(left, right):
    return jnp.dot(left, right, preferred_element_type=F32)


def dot_t(left, right):
    return lax.dot_general(left, right, (((1,), (1,)), ((), ())), preferred_element_type=F32)


def t_dot(left, right):
    return lax.dot_general(left, right, (((0,), (0,)), ((), ())), preferred_element_type=F32)


def pack(parts, rows):
    flat = jnp.concatenate([part.reshape(rows, -1) for part in parts], 1)
    width = -(-flat.shape[1] // 2048) * 2048
    flat = jnp.pad(flat, ((0, 0), (0, width - flat.shape[1])))
    return flat.reshape(rows, width // 128, 128)


def unpack(block, shapes):
    rows = block.shape[0]
    flat = block.reshape(rows, -1)
    parts, first = [], 0
    for shape in shapes:
        size = 1
        for extent in shape:
            size *= extent
        parts.append(flat[:, first : first + size].reshape((rows,) + shape))
        first += size
    return parts


def swap_windows(pieces, axis_size):
    me = lax.axis_index("dp")
    got = [pieces(me)]
    for step in range(1, axis_size):
        peer = lax.rem(me + step, axis_size)
        perm = [(k, (k + step) % axis_size) for k in range(axis_size)]
        got.append(lax.ppermute(pieces(peer), "dp", perm))
    return got


def in_order(got):
    me = lax.axis_index("dp")
    count = len(got)
    ordered = []
    for k in range(count):
        value = got[0]
        for step in range(1, count):
            value = jnp.where(lax.rem(me - k + count, count) == step, got[step], value)
        ordered.append(value)
    return ordered


def attention_forward(rows, segments, weights, tables):
    attn_gain, q_weight, kv_down, kv_gain, kv_up, out_weight, ffn_gain, router = weights
    cosine, sine_table = tables
    count = rows.shape[0]
    inputs = rows.astype(F32)
    normed_f, scale_one = normalize(inputs, attn_gain)
    normed = normed_f.astype(BF)
    q_raw = dot(normed, q_weight).reshape(MICRO, SEQ, HEADS, NOPE + ROPE)
    turn = (cosine[:, None, :], sine_table[:, None, :])
    queries = jnp.concatenate([q_raw[..., :NOPE], rotate(q_raw[..., NOPE:], *turn)], -1).astype(BF)
    kv_raw = dot(normed, kv_down)
    latent_f, scale_latent = normalize(kv_raw[:, :RANK], kv_gain)
    latent = latent_f.astype(BF)
    key_rope = rotate(kv_raw[:, RANK:].reshape(MICRO, SEQ, ROPE), cosine, sine_table)
    kv_full = dot(latent, kv_up).reshape(MICRO, SEQ, HEADS, NOPE + VDIM)
    shared_key = jnp.broadcast_to(key_rope[:, :, None, :], (MICRO, SEQ, HEADS, ROPE))
    key_rows = jnp.concatenate([kv_full[..., :NOPE], shared_key], -1).astype(BF)
    value_rows = kv_full[..., NOPE:].astype(BF)
    allowed = jax.vmap(attention_mask)(segments)[:, None]
    scores = jnp.einsum("mqhe,mkhe->mhqk", queries, key_rows, preferred_element_type=F32)
    scores = jnp.where(allowed, scores * (NOPE + ROPE) ** (-0.5), MASKED)
    powers = jnp.exp(scores - jnp.max(scores, -1, keepdims=True))
    softmax_rows = powers / jnp.sum(powers, -1, keepdims=True)
    probability = softmax_rows.astype(BF)
    attended = (
        jnp.einsum("mhqk,mkhe->mqhe", probability, value_rows, preferred_element_type=F32)
        .reshape(count, HEADS * VDIM)
        .astype(BF)
    )
    residual = inputs + dot(attended, out_weight)
    hidden_f, scale_two = normalize(residual, ffn_gain)
    hidden = hidden_f.astype(BF)
    saved = (
        inputs, scale_one, normed, queries, kv_raw, scale_latent, latent, key_rows, value_rows,
        softmax_rows, probability, attended, residual, scale_two,
    )
    return hidden, saved


def attention_backward(grad_out, hidden_grad, saved, weights, tables):
    attn_gain, q_weight, kv_down, kv_gain, kv_up, out_weight, ffn_gain, router = weights
    cosine, sine_table = tables
    (
        inputs, scale_one, normed, queries, kv_raw, scale_latent, latent, key_rows, value_rows,
        softmax_rows, probability, attended, residual, scale_two,
    ) = saved
    count = inputs.shape[0]
    turn = (cosine[:, None, :], sine_table[:, None, :])
    residual_part, ffn_gain_grad = normalize_back(residual, scale_two, ffn_gain, hidden_grad)
    residual_grad = grad_out + residual_part
    mixed_grad = residual_grad.astype(BF)
    out_weight_grad = t_dot(attended, mixed_grad)
    attended_grad = dot_t(mixed_grad, out_weight).astype(BF).reshape(MICRO, SEQ, HEADS, VDIM)
    value_grad = jnp.einsum(
        "mhqk,mqhe->mkhe", probability, attended_grad, preferred_element_type=F32
    )
    probs_grad = jnp.einsum(
        "mqhe,mkhe->mhqk", attended_grad, value_rows, preferred_element_type=F32
    )
    inner = jnp.sum(softmax_rows * probs_grad, -1, keepdims=True)
    score_grad = (softmax_rows * (probs_grad - inner)).astype(BF)
    score_scale = (NOPE + ROPE) ** (-0.5)
    query_grad = score_scale * jnp.einsum(
        "mhqk,mkhe->mqhe", score_grad, key_rows, preferred_element_type=F32
    )
    keys_grad = score_scale * jnp.einsum(
        "mhqk,mqhe->mkhe", score_grad, queries, preferred_element_type=F32
    )
    q_raw_grad = (
        jnp.concatenate([query_grad[..., :NOPE], unrotate(query_grad[..., NOPE:], *turn)], -1)
        .reshape(count, HEADS * (NOPE + ROPE))
        .astype(BF)
    )
    q_weight_grad = t_dot(normed, q_raw_grad)
    kv_full_grad = (
        jnp.concatenate([keys_grad[..., :NOPE], value_grad], -1)
        .reshape(count, HEADS * (NOPE + VDIM))
        .astype(BF)
    )
    kv_up_grad = t_dot(latent, kv_full_grad)
    latent_grad = dot_t(kv_full_grad, kv_up)
    latent_part, kv_gain_grad = normalize_back(
        kv_raw[:, :RANK], scale_latent, kv_gain, latent_grad
    )
    rope_grad = unrotate(jnp.sum(keys_grad[..., NOPE:], 2), cosine, sine_table)
    kv_raw_grad = jnp.concatenate([latent_part, rope_grad.reshape(count, ROPE)], -1).astype(BF)
    kv_down_grad = t_dot(normed, kv_raw_grad)
    normed_grad = dot_t(q_raw_grad, q_weight) + dot_t(kv_raw_grad, kv_down)
    input_part, attn_gain_grad = normalize_back(inputs, scale_one, attn_gain, normed_grad)
    tokens_grad = residual_grad + input_part
    return tokens_grad, (
        attn_gain_grad, q_weight_grad, kv_down_grad, kv_gain_grad, kv_up_grad, out_weight_grad,
        ffn_gain_grad,
    )


def experts_step(hidden_all, grad_all, gates, weights, expert_grads):
    gate_part, up_part, down_part, shared_in, shared_down = weights
    devices, tokens, _ = hidden_all.shape
    blocks = devices * tokens // SEQ
    capacity = capacity_for(gates.shape[1])
    expert = lax.axis_index("expert")
    hidden = hidden_all.reshape(blocks, SEQ, D)
    grad = grad_all.reshape(blocks, SEQ, D)
    share = lax.dynamic_index_in_dim(gates, expert, 1, keepdims=False).reshape(blocks, SEQ)
    chosen = share >= 0
    place = jnp.cumsum(chosen.astype(jnp.int32), 1) - 1
    slots = jnp.arange(capacity, dtype=jnp.int32)
    picks = (chosen[:, None, :] & (place[:, None, :] == slots[None, :, None])).astype(BF)
    share_rows = jnp.sum(picks.astype(F32) * share[:, None, :], -1).reshape(-1, 1)
    rows = jnp.einsum("bst,btd->bsd", picks, hidden).reshape(-1, D)
    grad_rows = jnp.einsum("bst,btd->bsd", picks, grad).reshape(-1, D)
    a_pre = dot(rows, gate_part)
    b_pre = dot(rows, up_part)
    act, slope = silu_parts(a_pre)
    inner_f = act * b_pre
    inner = inner_f.astype(BF)
    flow = dot_t(grad_rows, down_part)
    gate_grad_rows = jnp.sum(inner.astype(F32) * flow, -1).reshape(blocks, capacity)
    inner_grad = flow * share_rows
    a_grad = (inner_grad * b_pre * slope).astype(BF)
    b_grad = (inner_grad * act).astype(BF)
    row_grad = (dot_t(a_grad, gate_part) + dot_t(b_grad, up_part)).astype(BF)
    gate_grad = jnp.einsum("bst,bs->bt", picks.astype(F32), gate_grad_rows, precision=lax.Precision.HIGHEST)
    scaled = (inner.astype(F32) * share_rows).astype(BF)
    expert_out = dot(scaled, down_part).astype(BF)
    new_grads = (t_dot(rows, a_grad), t_dot(rows, b_grad), t_dot(scaled, grad_rows))
    if expert_grads is not None:
        new_grads = tuple(x + y for x, y in zip(expert_grads[0], new_grads))

    half = shared_in.shape[1] // 2
    hidden_flat = hidden.reshape(-1, D)
    grad_flat = grad.reshape(-1, D)
    shared_pre = dot(hidden_flat, shared_in)
    shared_act, shared_slope = silu_parts(shared_pre[:, :half])
    shared_b = shared_pre[:, half:]
    shared_inner = (shared_act * shared_b).astype(BF)
    shared_flow = dot_t(grad_flat, shared_down)
    shared_grad = jnp.concatenate(
        [shared_flow * shared_b * shared_slope, shared_flow * shared_act], 1
    ).astype(BF)
    hidden_part = jnp.einsum(
        "bst,bsd->btd", picks, row_grad.reshape(blocks, capacity, D), preferred_element_type=F32
    ) + dot_t(shared_grad, shared_in).reshape(blocks, SEQ, D)
    out_part = jnp.einsum(
        "bst,bsd->btd", picks, expert_out.reshape(blocks, capacity, D), preferred_element_type=F32
    ) + dot(shared_inner, shared_down).reshape(blocks, SEQ, D)
    shared_grads = (t_dot(hidden_flat, shared_grad), t_dot(shared_inner, grad_flat))
    if expert_grads is not None:
        shared_grads = tuple(x + y for x, y in zip(expert_grads[1], shared_grads))
    shape = (devices, tokens, D)
    mine = (jnp.arange(gates.shape[1], dtype=jnp.int32) == expert)[None, :, None]
    gate_grad = jnp.where(mine, gate_grad.reshape(devices, 1, tokens), 0.0)
    return (
        out_part.astype(BF).reshape(shape),
        hidden_part.astype(BF).reshape(shape),
        gate_grad,
        (new_grads, shared_grads),
    )


def body(
    grid,
    tokens,
    cotangent,
    routes,
    segments,
    attn_gain,
    q_weight,
    kv_down,
    kv_gain,
    kv_up,
    out_weight,
    ffn_gain,
    router,
    shared_gate,
    shared_up,
    shared_down,
    expert_gate,
    expert_up,
    expert_down,
):
    devices = grid.devices
    dp_size = grid.size["p"]
    experts = router.shape[1]
    tables = rope_tables(SEQ, ROPE)
    me_dp = lax.axis_index("dp")
    count = MICRO * SEQ
    eff = expert_gate.shape[2]

    window = -(-eff // (128 * dp_size)) * 128
    starts = [min(k * window, eff - window) for k in range(dp_size)]

    def start_of(peer):
        return jnp.minimum(peer * window, eff - window)

    def columns_for(array):
        return lambda peer: lax.dynamic_slice_in_dim(array[0], start_of(peer), window, 1)

    def rows_for(array):
        return lambda peer: lax.dynamic_slice_in_dim(array[0], start_of(peer), window, 0)

    gate_part = jnp.concatenate(in_order(swap_windows(columns_for(expert_gate), dp_size)), 0)
    up_part = jnp.concatenate(in_order(swap_windows(columns_for(expert_up), dp_size)), 0)
    down_part = jnp.concatenate(in_order(swap_windows(rows_for(expert_down), dp_size)), 1)
    fresh = jnp.arange(window, dtype=jnp.int32) + start_of(me_dp) >= me_dp * window
    gate_part = jnp.where(fresh[None, :], gate_part, 0)
    up_part = jnp.where(fresh[None, :], up_part, 0)
    down_part = jnp.where(fresh[:, None], down_part, 0)

    share = shared_gate.shape[1] // devices
    both = jnp.concatenate(
        [shared_gate.reshape(-1, devices, share), shared_up.reshape(-1, devices, share)], 2
    )
    shared_in = lax.all_to_all(
        both.transpose(1, 0, 2), ("dp", "expert"), split_axis=0, concat_axis=0, tiled=True
    ).reshape(D, 2 * share)

    small_shapes = (attn_gain.shape, ffn_gain.shape, kv_gain.shape, router.shape)
    small = pack([attn_gain[None], ffn_gain[None], kv_gain[None], router[None]], 1)[0]
    up_shape = kv_up.shape
    kv_up_sent = kv_up if up_shape[0] % 16 == 0 else kv_up.reshape(16, -1)
    first, second = ("q", "r", "p"), ("q", "p", "r")
    got = gather_all(
        grid,
        [q_weight, kv_down, kv_up_sent, out_weight, small],
        [
            (0, 0, q_weight.shape[1], first),
            (3, 0, out_weight.shape[1], second),
            (2, 0, kv_up_sent.shape[1], second),
            (1, 0, kv_down.shape[1], second),
            (4, 0, 128, first),
        ],
        0,
    )
    gains = unpack(got[4], small_shapes)
    weights = (
        gains[0].reshape(-1).astype(F32),
        got[0].reshape(D, -1),
        got[1].reshape(D, -1),
        gains[2].reshape(-1).astype(F32),
        got[2].reshape(RANK, -1),
        got[3].reshape(-1, D),
        gains[1].reshape(-1).astype(F32),
        gains[3].reshape(D, experts),
    )
    router_full = weights[7]

    token_rows = tokens.reshape(count, D)
    grad_out = cotangent.reshape(count, D)
    route_rows = routes.reshape(count, TOP)
    hidden, saved = attention_forward(token_rows, segments.reshape(MICRO, SEQ), weights, tables)
    logits = dot(hidden, router_full)
    choose = route_rows[:, :, None] == jnp.arange(experts, dtype=jnp.int32)[None, None, :]
    choose = choose.astype(F32)
    gate_share = jax.nn.softmax(jnp.sum(choose * logits[:, None, :], -1), -1)
    dense_share = jnp.sum(choose * gate_share[..., None], 1)
    dense_gates = jnp.where(jnp.sum(choose, 1) > 0, dense_share, -1.0)

    groups = 1 if devices * count <= 8192 else MICRO
    size = count // groups
    half = D // 2
    own_weights = (gate_part, up_part, down_part, shared_in, shared_down)
    outs, hidden_grads, gate_grads = [], [], []
    grads = None
    for g in range(groups):
        piece = slice(g * size, (g + 1) * size)
        sent = [hidden[piece], grad_out[piece], dense_gates[piece].T]
        if g > 0:
            *sent, hidden_grads[-1], outs[-1] = lax.optimization_barrier(
                (*sent, hidden_grads[-1], outs[-1])
            )
        hidden_all, grad_all, gates_all = gather_all(
            grid,
            sent,
            [
                (0, 0, half, first),
                (0, half, half, second),
                (1, 0, half, first),
                (1, half, half, second),
                (2, 0, size, first),
            ],
            1,
        )
        out_part, hidden_part, gate_part_grad, grads = experts_step(
            hidden_all, grad_all, gates_all, own_weights, grads
        )
        hidden_sum, gate_sum = sum_scattered(
            grid,
            [hidden_part, gate_part_grad],
            [(0, 0, half, ("p", "r")), (0, half, half, ("r", "p")), (1, 0, size, ("p", "r"))],
            2,
        )
        (out_sum,) = sum_scattered(
            grid, [out_part], [(0, 0, half, ("p", "r")), (0, half, half, ("r", "p"))], 3
        )
        hidden_grads.append(hidden_sum)
        gate_grads.append(gate_sum.T)
        outs.append(out_sum)
    hidden_sum = jnp.concatenate(hidden_grads, 0)
    gate_grad = jnp.concatenate(gate_grads, 0)
    result = saved[12] + jnp.concatenate(outs, 0)

    dense_share = jnp.maximum(dense_share, 0.0)
    inner = jnp.sum(dense_share * gate_grad, -1, keepdims=True)
    logit_grad = (dense_share * (gate_grad - inner)).astype(BF)
    router_grad = t_dot(hidden, logit_grad)
    hidden_grad = hidden_sum + dot_t(logit_grad, router_full)
    tokens_grad, (
        attn_gain_grad, q_weight_grad, kv_down_grad, kv_gain_grad, kv_up_grad, out_weight_grad,
        ffn_gain_grad,
    ) = attention_backward(grad_out.astype(F32), hidden_grad, saved, weights, tables)

    small_grads = pack(
        [
            attn_gain_grad.reshape(devices, -1),
            ffn_gain_grad.reshape(devices, -1),
            kv_gain_grad.reshape(devices, -1),
            router_grad.reshape(devices, -1),
        ],
        devices,
    )
    q_sum, down_sum, up_sum, out_weight_sum, small_sum = sum_scattered(
        grid,
        [
            q_weight_grad.astype(BF).reshape((devices,) + q_weight.shape),
            kv_down_grad.astype(BF).reshape((devices,) + kv_down.shape),
            kv_up_grad.astype(BF).reshape((devices,) + kv_up_sent.shape),
            out_weight_grad.astype(BF).reshape((devices,) + out_weight.shape),
            small_grads,
        ],
        [
            (0, 0, q_weight.shape[1], ("p", "r")),
            (3, 0, out_weight.shape[1], ("r", "p")),
            (2, 0, kv_up_sent.shape[1], ("r", "p")),
            (1, 0, kv_down.shape[1], ("r", "p")),
            (4, 0, 128, ("p", "r")),
        ],
        4,
    )
    small_sums = unpack(small_sum[None], small_shapes)

    (gate_grad_part, up_grad_part, down_grad_part), (shared_in_grad, shared_down_grad) = grads
    shared_back = lax.all_to_all(
        shared_in_grad.astype(BF).reshape(devices, -1, 2 * share),
        ("dp", "expert"), split_axis=0, concat_axis=0, tiled=True,
    ).astype(F32)
    shared_back = shared_back.transpose(1, 0, 2)
    shared_gate_grad = shared_back[:, :, :share].reshape(shared_gate.shape)
    shared_up_grad = shared_back[:, :, share:].reshape(shared_up.shape)

    def whole(part, axis, other, extent):
        def for_peer(peer):
            return lax.dynamic_slice_in_dim(part, peer * extent, extent, other)

        got_back = swap_windows(lambda peer: for_peer(peer).astype(BF), dp_size)
        got_back = [for_peer(me_dp)] + [piece.astype(F32) for piece in got_back[1:]]
        pieces = []
        for k, piece in enumerate(in_order(got_back)):
            skip = k * window - starts[k]
            pieces.append(lax.slice_in_dim(piece, skip, window, axis=axis))
        return jnp.concatenate(pieces, axis)[None]

    extent = expert_gate.shape[1]
    return (
        result.astype(BF).reshape(tokens.shape),
        tokens_grad.astype(BF).reshape(tokens.shape),
        small_sums[0].reshape(-1),
        q_sum,
        down_sum,
        small_sums[2].reshape(-1),
        up_sum.reshape(up_shape),
        out_weight_sum,
        small_sums[1].reshape(-1),
        small_sums[3].reshape(router.shape),
        shared_gate_grad,
        shared_up_grad,
        shared_down_grad,
        whole(gate_grad_part, 1, 0, extent),
        whole(up_grad_part, 1, 0, extent),
        whole(down_grad_part, 0, 1, extent),
    )


def solution(mesh):
    return jax.shard_map(
        functools.partial(body, Grid(mesh)),
        mesh=mesh,
        in_specs=(
            P(None, ("dp", "expert"), None, None),
            P(None, ("dp", "expert"), None, None),
            P(None, ("dp", "expert"), None, None),
            P(None, ("dp", "expert"), None),
            P(("dp", "expert")),
            P(("dp", "expert"), None),
            P(("dp", "expert"), None),
            P(("dp", "expert")),
            P(("dp", "expert"), None),
            P(("dp", "expert"), None),
            P(("dp", "expert")),
            P(("dp", "expert"), None),
            P(("dp", "expert"), None),
            P(("dp", "expert"), None),
            P(("dp", "expert"), None),
            P("expert", "dp", None),
            P("expert", "dp", None),
            P("expert", None, "dp"),
        ),
        out_specs=(
            P(None, ("dp", "expert"), None, None),
            P(None, ("dp", "expert"), None, None),
            P(("dp", "expert")),
            P(("dp", "expert"), None),
            P(("dp", "expert"), None),
            P(("dp", "expert")),
            P(("dp", "expert"), None),
            P(("dp", "expert"), None),
            P(("dp", "expert")),
            P(("dp", "expert"), None),
            P(("dp", "expert"), None),
            P(("dp", "expert"), None),
            P(("dp", "expert"), None),
            P("expert", "dp", None),
            P("expert", "dp", None),
            P("expert", None, "dp"),
        ),
        check_vma=False,
    )
```

profile of v0, /device:TPU:16, one launch (start us, length us, event | category | flops | bytes accessed | tf_op | source)
XLA Modules:
  0.0 1282.1 jit_solution(5058130987186996686)
XLA Ops:
  17.5 9.3 constant_dynamic-slice_fusion
  35.6 209.9 %gather_all.2 = (bf16[32,64,3072]{2,1,0:T(8,128)(2,1)}, bf16[32,64,576]{2,1,0:T(8,128)(2,1)}, bf16[32,16,4096]{2,1,0:T(8,128)(2,1)}, bf16[32,64,2048]{2,1,0:T(8,128)(2,1)}, bf16[32,16,128]{2,1,0:T(8,128)(2,1)}) custom-call(bf16[64,3072]{1,0:T(8,128)(2,1)} %refs_0_.1, bf16[64,576]{1,0:T(8,128)(2,1)} %refs_1_.1, bf16[16,4096]{1,0:T(8,128)(2,1)} %refs_2_.1, ...), custom_call_target="tpu_custom_call" | custom-call | tf_op jit(solution)/shard_map/gather_all/pallas_call | solution.py:237
  257.4 16.8 %copy.177 = bf16[3072,2048]{1,0:T(8,128)(2,1)} copy(bf16[3072,2048]{0,1:T(8,128)(2,1)} %bitcast.234) | data formatting | bytes 25165824 | tf_op jit(solution)/shard_map/dot_general | solution.py:569
  274.1 9.0 fusion.46
  285.8 6.4 copy.176
  310.2 148.2 %gather_all.3 = (bf16[32,128,2048]{2,1,0:T(8,128)(2,1)}, bf16[32,128,2048]{2,1,0:T(8,128)(2,1)}, f32[32,16,128]{2,1,0:T(8,128)}) custom-call(bf16[128,2048]{1,0:T(8,128)(2,1)} %copy-done.14, bf16[128,2048]{1,0:T(8,128)(2,1)} %bitcast.268, f32[16,128]{1,0:T(8,128)} %select_bitcast_fusion.refs_2_), custom_call_target="tpu_custom_call" | custom-call | tf_op jit(solution)/shard_map/gather_all/pallas_call | solution.py:237
  460.2 11.3 fusion.38
  471.5 11.3 fusion.42
  482.9 13.9 %fusion.104 = f32[4096,176]{0,1:T(8,128)} fusion(bf16[4096,2048]{1,0:T(8,128)(2,1)} %bitcast.226, bf16[2048,176]{1,0:T(8,128)(2,1)S(1)} %bitcast.257), kind=kOutput, calls=%fused_computation.227 | convolution fusion | flops 2952790016 | bytes 20381696 | tf_op jit(solution)/shard_map/dot_general | solution.py:569
  496.8 11.9 multiply_convert_fusion.4
  510.0 8.9 convolution_convert_fusion.5
  527.0 9.6 fusion.108
  536.6 13.2 %fusion.105 = f32[4096,2048]{1,0:T(8,128)} fusion(bf16[4096,88]{0,1:T(8,128)(2,1)S(1)} %get-tuple-element.148, bf16[88,2048]{1,0:T(8,128)(2,1)S(1)} %copy-done), kind=kOutput, calls=%fused_computation.228 | convolution fusion | flops 1476395008 | bytes 34635776 | tf_op jit(solution)/shard_map/dot_general | solution.py:569
  551.5 8.8 fusion.71
  561.9 8.8 fusion.72
  573.1 16.5 %fusion.2 = (f32[2048]{0:T(1024)S(1)}, bf16[2048,768]{0,1:T(8,128)(2,1)}, bf16[2048,768]{0,1:T(8,128)(2,1)}, bf16[2048,768]{0,1:T(8,128)(2,1)}) fusion(f32[2048,768]{0,1:T(8,128)} %fusion.71, f32[2048,768]{0,1:T(8,128)} %fusion.72, f32[2048]{0:T(1024)S(1)} %mul.653, bf16[2048,2048]{1,0:T(8,128)(2,1)} %bitcast.245, ...), kind=kOutput, calls=%fused_computation.10 | convolution fusion | flops 6480197632 | bytes 33571584 | tf_op jit(solution)/shard_map/dot_general | solution.py:573
  589.5 11.8 fusion.4
  601.3 9.4 convolution_convert_fusion.1
  610.8 8.5 fusion.110
  619.3 11.0 fusion.70
  631.1 11.7 fusion.109
  642.8 11.5 add_convert_fusion.2
  654.4 13.3 %fusion.36 = f32[64,64,2048]{2,1,0:T(8,128)} fusion(bf16[64,32,2048]{2,1,0:T(8,128)(2,1)S(1)} %bitcast.247, s32[64,64]{1,0:T(8,128)S(1)} %copy-done.26, pred[64,64]{1,0:T(8,128)(4,1)S(1)} %copy-done.59), kind=kOutput, calls=%fused_computation.112 | convolution fusion | flops 537133056 | bytes 41963520 | tf_op jit(solution)/shard_map/bst,bsd->btd/dot_general | solution.py:763
  668.5 17.3 %add_convert_fusion = bf16[64,64,2048]{2,1,0:T(8,128)(2,1)} fusion(f32[64,64,2048]{2,1,0:T(8,128)} %fusion.36, bf16[2048,176,1]{1,0,2:T(8,128)(2,1)S(1)} %bitcast.258, bf16[64,64,88]{2,1,0:T(8,128)(2,1)} %bitcast.266, bf16[64,64,88]{2,1,0:T(8,128)(2,1)S(1)} %bitcast.265), kind=kOutput, calls=%fused_computation.1 | convolution fusion | flops 2972450816 | bytes 52494336 | tf_op jit(solution)/shard_map/dot_general | solution.py:573
  685.8 122.4 %sum_scattered.4 = (f32[128,2048]{1,0:T(8,128)}, f32[16,128]{1,0:T(8,128)}) custom-call(bf16[32,128,2048]{2,1,0:T(8,128)(2,1)} %bitcast.229, f32[32,16,128]{2,1,0:T(8,128)} %broadcast_select_fusion.refs_1_), custom_call_target="tpu_custom_call" | custom-call | tf_op jit(solution)/shard_map/sum_scattered/pallas_call | solution.py:484
  812.8 21.2 %add_convert_fusion.1 = bf16[64,64,2048]{2,1,0:T(8,128)(2,1)} fusion(f32[64,64,2048]{2,1,0:T(8,128)} %bitcast.221, bf16[64,32,2048]{2,1,0:T(8,128)(2,1)} %bitcast.237, s32[64,64]{1,0:T(8,128)S(1)} %copy-done.26, pred[64,64]{1,0:T(8,128)(4,1)S(1)} %copy-done.59), kind=kOutput, calls=%fused_computation.2 | convolution fusion | flops 553910272 | bytes 58740736 | tf_op jit(solution)/shard_map/bst,bsd->btd/dot_general | solution.py:766
  833.9 121.9 %sum_scattered.3 = f32[128,2048]{1,0:T(8,128)} custom-call(bf16[32,128,2048]{2,1,0:T(8,128)(2,1)} %bitcast.228), custom_call_target="tpu_custom_call" | custom-call | tf_op jit(solution)/shard_map/sum_scattered/pallas_call | solution.py:484
  958.6 6.3 fusion.17
  1007.8 6.5 convolution_convert_fusion
  1014.3 9.0 fusion.106
  1033.1 190.8 %sum_scattered.5 = (f32[64,3072]{1,0:T(8,128)}, f32[64,576]{1,0:T(8,128)}, f32[16,4096]{1,0:T(8,128)}, f32[64,2048]{1,0:T(8,128)}, f32[16,128]{1,0:T(8,128)}) custom-call(bf16[32,64,3072]{2,1,0:T(8,128)(2,1)} %bitcast.230, bf16[32,64,576]{2,1,0:T(8,128)(2,1)} %bitcast.254, bf16[32,16,4096]{2,1,0:T(8,128)(2,1)} %bitcast.238, bf16[32,64,2048]{2,1,0:T(8,128)(2,1)} %bitcast.233, ...), custom_call_target="tpu_custom_call" | custom-call | tf_op jit(solution)/shard_map/sum_scattered/pallas_call | solution.py:484
  1245.8 6.2 copy.209
  (356 shorter events, 187.2 us)
Async XLA Ops:
  0.6 496.1 %copy-start = (bf16[88,2048]{1,0:T(8,128)(2,1)S(1)}, bf16[88,2048]{1,0:T(8,128)(2,1)}, u32[]{:S(2)}) copy-start(bf16[88,2048]{1,0:T(8,128)(2,1)} %param.32) | copy-start | bytes 1081348
  7.0 475.8 %all-to-all-start = ((bf16[32,64,176]{2,1,0:T(8,128)(2,1)}), bf16[32,64,176]{2,1,0:T(8,128)(2,1)S(1)}, u32[]{:S(2)}, u32[]{:S(2)}) async-start(bf16[32,64,176]{2,1,0:T(8,128)(2,1)} %maximum_bitcast_fusion.3), calls=%async_computation | async-start | bytes 2097152 | tf_op jit(solution)/shard_map/all_to_all | solution.py:836
  16.0 554.7 %collective-permute-start.2 = (bf16[768,1024]{1,0:T(8,128)(2,1)}, bf16[768,1024]{1,0:T(8,128)(2,1)}, u32[]{:S(2)}, u32[]{:S(2)}) collective-permute-start(bf16[768,1024]{1,0:T(8,128)(2,1)} %dynamic-slice_bitcast_fusion), channel_id=1, source_target_pairs={{0,16},{16,0},{1,17},{17,1},{2,18},{18,2},{3,19},{19,3},{4,20},{20... | collective-permute-start | bytes 4718600 | tf_op jit(solution)/shard_map/ppermute | solution.py:606
  26.8 219.8 %copy-start.5 = (bf16[2,1,64,2048]{3,2,1,0:T(8,128)(2,1)S(1)}, bf16[2,1,64,2048]{3,2,1,0:T(8,128)(2,1)}, u32[]{:S(2)}) copy-start(bf16[2,1,64,2048]{3,2,1,0:T(8,128)(2,1)} %param.18) | copy-start | bytes 1572868
  29.5 530.7 %collective-permute-start = (bf16[1024,768]{0,1:T(8,128)(2,1)}, bf16[1024,768]{0,1:T(8,128)(2,1)}, u32[]{:S(2)}, u32[]{:S(2)}) collective-permute-start(bf16[1024,768]{0,1:T(8,128)(2,1)} %bitcast.269), channel_id=1, source_target_pairs={{0,16},{16,0},{1,17},{17,1},{2,18},{18,2},{3,19},{19,3},{4,20},{20... | collective-permute-start | bytes 4718600 | tf_op jit(solution)/shard_map/ppermute | solution.py:606
  32.6 517.1 %collective-permute-start.1 = (bf16[1024,768]{0,1:T(8,128)(2,1)}, bf16[1024,768]{0,1:T(8,128)(2,1)}, u32[]{:S(2)}, u32[]{:S(2)}) collective-permute-start(bf16[1024,768]{0,1:T(8,128)(2,1)} %bitcast.270), channel_id=1, source_target_pairs={{0,16},{16,0},{1,17},{17,1},{2,18},{18,2},{3,19},{19,3},{4,20},{20... | collective-permute-start | bytes 4718600 | tf_op jit(solution)/shard_map/ppermute | solution.py:606
  247.7 26.4 %copy-start.8 = (bf16[2,1,64,2048]{3,2,1,0:T(8,128)(2,1)}, bf16[2,1,64,2048]{3,2,1,0:T(8,128)(2,1)S(1)}, u32[]{:S(2)}) copy-start(bf16[2,1,64,2048]{3,2,1,0:T(8,128)(2,1)S(1)} %fusion.29) | copy-start | bytes 1572868
  251.0 34.5 %copy-start.16 = (f32[128,576]{0,1:T(8,128)}, f32[128,576]{0,1:T(8,128)S(1)}, u32[]{:S(2)}) copy-start(f32[128,576]{0,1:T(8,128)S(1)} %fusion.102) | copy-start | bytes 884740
  251.3 34.1 %copy-start.53 = (f32[64,32]{1,0:T(8,128)}, f32[64,32]{1,0:T(8,128)S(1)}, u32[]{:S(2)}) copy-start(f32[64,32]{1,0:T(8,128)S(1)} %get-tuple-element.170) | copy-start | bytes 24580
  251.3 34.1 %copy-start.55 = (f32[64,32]{1,0:T(8,128)}, f32[64,32]{1,0:T(8,128)S(1)}, u32[]{:S(2)}) copy-start(f32[64,32]{1,0:T(8,128)S(1)} %get-tuple-element.171) | copy-start | bytes 24580
  256.7 28.8 %copy-start.73 = (f32[512]{0:T(512)}, f32[512]{0:T(512)S(1)}, u32[]{:S(2)}) copy-start(f32[512]{0:T(512)S(1)} %reshape.539) | copy-start | bytes 6148
  256.8 51.2 %copy-start.67 = (f32[2048]{0:T(1024)}, f32[2048]{0:T(1024)S(1)}, u32[]{:S(2)}) copy-start(f32[2048]{0:T(1024)S(1)} %reshape.540) | copy-start | bytes 24580
  257.2 51.9 %copy-start.20 = (bf16[2048,16]{1,0:T(8,128)(2,1)}, bf16[2048,16]{1,0:T(8,128)(2,1)S(1)}, u32[]{:S(2)}) copy-start(bf16[2048,16]{1,0:T(8,128)(2,1)S(1)} %reshape_reshape.12) | copy-start | bytes 196612
  257.3 28.3 %copy-start.76 = (f32[128]{0:T(128)}, f32[128]{0:T(128)S(1)}, u32[]{:S(2)}) copy-start(f32[128]{0:T(128)S(1)} %add_rsqrt_fusion.2) | copy-start | bytes 1540
  308.0 163.5 %copy-start.78 = (f32[128]{0:T(128)}, f32[128]{0:T(128)S(1)}, u32[]{:S(2)}) copy-start(f32[128]{0:T(128)S(1)} %add_rsqrt_fusion.1) | copy-start | bytes 1540
  309.6 161.9 %copy-start.69 = (f32[128,16]{0,1:T(8,128)}, f32[128,16]{0,1:T(8,128)S(1)}, u32[]{:S(2)}) copy-start(f32[128,16]{0,1:T(8,128)S(1)} %get-tuple-element.133) | copy-start | bytes 24580
  482.9 13.9 %copy-start.10 = (bf16[32,64,176]{2,1,0:T(8,128)(2,1)}, bf16[32,64,176]{2,1,0:T(8,128)(2,1)S(1)}, u32[]{:S(2)}) copy-start(bf16[32,64,176]{2,1,0:T(8,128)(2,1)S(1)} %all-to-all-done) | copy-start | bytes 2162692
  521.5 707.5 %all-to-all-start.1 = ((bf16[32,64,176]{2,1,0:T(8,128)(2,1)}), bf16[32,64,176]{2,1,0:T(8,128)(2,1)}, u32[]{:S(2)}, u32[]{:S(2)}) async-start(bf16[32,64,176]{2,1,0:T(8,128)(2,1)} %bitcast.67), calls=%async_computation.1 | async-start | bytes 2097152 | tf_op jit(solution)/shard_map/all_to_all | solution.py:965
  527.0 24.4 %slice-start = ((s8[8388608]{0:T(1024)(128)(4,1)}), s8[4194304]{0:T(1024)(128)(4,1)S(1)}, s32[]{:S(2)}) async-start(s8[8388608]{0:T(1024)(128)(4,1)} %bitcast.240), calls=%async_computation.2 | async-start | bytes 8388608
  536.6 14.8 %slice-start.1 = ((s8[8388608]{0:T(1024)(128)(4,1)}), s8[4194304]{0:T(1024)(128)(4,1)S(1)}, s32[]{:S(2)}) async-start(s8[8388608]{0:T(1024)(128)(4,1)} %bitcast.240), calls=%async_computation.3 | async-start | bytes 8388608
  654.3 14.1 %copy-start.11 = (bf16[32,64,176]{2,1,0:T(8,128)(2,1)S(1)}, bf16[32,64,176]{2,1,0:T(8,128)(2,1)}, u32[]{:S(2)}) copy-start(bf16[32,64,176]{2,1,0:T(8,128)(2,1)} %copy-done.10) | copy-start | bytes 2162692
  654.3 14.1 %copy-start.22 = (bf16[4096,88]{1,0:T(8,128)(2,1)S(1)}, bf16[4096,88]{1,0:T(8,128)(2,1)}, u32[]{:S(2)}) copy-start(bf16[4096,88]{1,0:T(8,128)(2,1)} %copy.189) | copy-start | bytes 2162692
  685.8 122.5 %copy-start.70 = (f32[128,16]{0,1:T(8,128)S(1)}, f32[128,16]{0,1:T(8,128)}, u32[]{:S(2)}) copy-start(f32[128,16]{0,1:T(8,128)} %copy-done.69) | copy-start | bytes 24580
  685.8 123.9 %copy-start.15 = (bf16[128,2048]{1,0:T(8,128)(2,1)S(1)}, bf16[128,2048]{1,0:T(8,128)(2,1)}, u32[]{:S(2)}) copy-start(bf16[128,2048]{1,0:T(8,128)(2,1)} %copy-done.14) | copy-start | bytes 1572868
  685.8 124.3 %copy-start.3 = (f32[128,2048]{1,0:T(8,128)S(1)}, f32[128,2048]{1,0:T(8,128)}, u32[]{:S(2)}) copy-start(f32[128,2048]{1,0:T(8,128)} %copy-done.2) | copy-start | bytes 3145732
  685.8 124.3 %copy-start.21 = (bf16[2048,16]{1,0:T(8,128)(2,1)S(1)}, bf16[2048,16]{1,0:T(8,128)(2,1)}, u32[]{:S(2)}) copy-start(bf16[2048,16]{1,0:T(8,128)(2,1)} %copy-done.20) | copy-start | bytes 196612
  685.8 124.3 %copy-start.68 = (f32[2048]{0:T(1024)S(1)}, f32[2048]{0:T(1024)}, u32[]{:S(2)}) copy-start(f32[2048]{0:T(1024)} %copy-done.67) | copy-start | bytes 24580
  685.8 124.3 %copy-start.79 = (f32[128]{0:T(128)S(1)}, f32[128]{0:T(128)}, u32[]{:S(2)}) copy-start(f32[128]{0:T(128)} %copy-done.78) | copy-start | bytes 1540
  833.9 121.9 %copy-start.29 = (bf16[2,1,64,2048]{3,2,1,0:T(8,128)(2,1)S(1)}, bf16[2,1,64,2048]{3,2,1,0:T(8,128)(2,1)}, u32[]{:S(2)}) copy-start(bf16[2,1,64,2048]{3,2,1,0:T(8,128)(2,1)} %param.19) | copy-start | bytes 1572868
  983.7 268.3 %collective-permute-start.5 = (bf16[768,1024]{1,0:T(8,128)(2,1)}, bf16[768,1024]{1,0:T(8,128)(2,1)}, u32[]{:S(2)}, u32[]{:S(2)}) collective-permute-start(bf16[768,1024]{1,0:T(8,128)(2,1)} %dynamic-slice_convert_fusion), channel_id=1, source_target_pairs={{0,16},{16,0},{1,17},{17,1},{2,18},{18,2},{3,19},{19,3},{4,20},{20... | collective-permute-start | bytes 4718600 | tf_op jit(solution)/shard_map/ppermute | solution.py:606
  992.0 264.3 %collective-permute-start.3 = (bf16[1024,768]{0,1:T(8,128)(2,1)}, bf16[1024,768]{0,1:T(8,128)(2,1)}, u32[]{:S(2)}, u32[]{:S(2)}) collective-permute-start(bf16[1024,768]{0,1:T(8,128)(2,1)} %dynamic-slice_convert_fusion.2), channel_id=1, source_target_pairs={{0,16},{16,0},{1,17},{17,1},{2,18},{18,2},{3,19},{19,3},{4,20},{20... | collective-permute-start | bytes 4718600 | tf_op jit(solution)/shard_map/ppermute | solution.py:606
  992.3 242.7 %collective-permute-start.4 = (bf16[1024,768]{0,1:T(8,128)(2,1)}, bf16[1024,768]{0,1:T(8,128)(2,1)}, u32[]{:S(2)}, u32[]{:S(2)}) collective-permute-start(bf16[1024,768]{0,1:T(8,128)(2,1)} %dynamic-slice_convert_fusion.1), channel_id=1, source_target_pairs={{0,16},{16,0},{1,17},{17,1},{2,18},{18,2},{3,19},{19,3},{4,20},{20... | collective-permute-start | bytes 4718600 | tf_op jit(solution)/shard_map/ppermute | solution.py:606
  (69 other events, 399.4 us)
where the time goes:
time: 1290 us; the launch traced here: 1280 us
  Pallas kernels  793 us (61%)
  matrix products  301 us (23%)
  local copies, waits for them, and re-layouts  111 us (9%)
  other arithmetic  56 us (4%)
  starting transfers between devices  18.6 us (1%)
    pallas_call x3, Pallas kernels, sum_scattered(): pl.pallas_call(functools.partial(scatter_kernel, grid, len(arrays), items...  435 us
    pallas_call x2, Pallas kernels, gather_all(): pl.pallas_call(functools.partial(gather_kernel, grid, len(arrays), items)...  358 us
    dot_general x10, matrix products, dot_t(): lax.dot_general(left, right, (((1,), (1,)), ((), ())), preferred_element_...  89.7 us
    dot_general x10, matrix products, dot(): return jnp.dot(left, right, preferred_element_type=F32)  74.9 us
    dot_general x10, matrix products, t_dot(): lax.dot_general(left, right, (((0,), (0,)), ((), ())), preferred_element_...  69.2 us
  transfers between devices with their start and end apart: 8, of which 0 were waited for; matrix products, arithmetic and copies ran while one was open for 34% of the time, Pallas kernels for 62%

commit v1 on v0

v1 whole, which is shorter than its diff:
```python
import functools

import jax
import jax.numpy as jnp
from jax import lax
from jax.experimental import pallas as pl
from jax.experimental.pallas import tpu as pltpu
from jax.sharding import PartitionSpec as P

D = 2048
HEADS = 16
NOPE = 128
ROPE = 64
VDIM = 128
RANK = 512
TOP = 6
SEQ = 64
MICRO = 2

EPSILON = 1e-06
ROPE_BASE = 10000.0
MASKED = -1e30
BF = jnp.bfloat16
F32 = jnp.float32

MESH_ID = pl.DeviceIdType.MESH


class Grid:
    def __init__(self, mesh):
        self.experts = mesh.shape["expert"]
        self.size = {"p": mesh.shape["dp"], "r": self.experts // 8, "q": 4}
        self.devices = self.size["p"] * self.experts

    def here(self):
        e = lax.axis_index("expert")
        r_size = self.size["r"]
        return {
            "p": lax.axis_index("dp"),
            "q": lax.div(e, 2 * r_size),
            "r": lax.rem(lax.div(e, 2), r_size),
            "c": lax.rem(e, 2),
        }

    def shift(self, at, offsets):
        moved = dict(at)
        for axis, step in offsets.items():
            if step:
                moved[axis] = lax.rem(at[axis] + step, self.size[axis])
        return moved

    def expert_of(self, at):
        return at["q"] * (2 * self.size["r"]) + at["r"] * 2 + at["c"]

    def number(self, at):
        return at["p"] * self.experts + self.expert_of(at)

    def mesh_id(self, at):
        return (at["p"], self.expert_of(at))

    def partners(self, at):
        found = [{**at, "c": 1 - at["c"]}]
        for axis, size in self.size.items():
            found += [self.shift(at, {axis: step}) for step in range(1, size)]
        return found


def greet(grid, at):
    barrier = pltpu.get_barrier_semaphore()
    partners = grid.partners(at)
    for partner in partners:
        pl.semaphore_signal(barrier, inc=1, device_id=grid.mesh_id(partner), device_id_type=MESH_ID)
    pl.semaphore_wait(barrier, len(partners))


ALONG = (0, -1, 1, -2, 2, -3, 3)


def span_of(grid, axis):
    return ALONG if axis == "q" else tuple(range(grid.size[axis]))


class Gather:
    def __init__(self, grid, arrays, items):
        count = len(items)
        slots = grid.devices // 2 // 4 * len(ALONG)
        self.grid, self.items = grid, items
        self.inputs = list(arrays)
        self.in_specs = [pl.BlockSpec(memory_space=pl.ANY)] * len(arrays)
        self.out_shapes = [
            jax.ShapeDtypeStruct((grid.devices,) + a.shape, a.dtype) for a in arrays
        ]
        self.out_specs = [pl.BlockSpec(memory_space=pl.ANY)] * len(arrays)
        self.scratch = [
            pltpu.SemaphoreType.DMA((count * slots * 2,)),
            pltpu.SemaphoreType.DMA((count, slots)),
            pltpu.SemaphoreType.DMA((count, slots)),
            pltpu.SemaphoreType.DMA((count, slots)),
            pltpu.SemaphoreType.DMA((len(arrays),)),
        ]

    def steps(self, at, ins, outs, scratch):
        grid, items = self.grid, self.items
        count = len(items)
        send_sem, recv_sem, core_send, core_recv, own_sem = scratch
        sibling = {**at, "c": 1 - at["c"]}
        q_size = grid.size["q"]
        pending = []
        me = grid.number(at)

        def inside(step):
            return jnp.logical_and(at["q"] + step >= 0, at["q"] + step < q_size)

        def guarded(step, action):
            if step:
                pl.when(inside(step))(action)
            else:
                action()

        def q_part(i, offset):
            return offset[items[i][3].index("q")]

        def slot(i, offset):
            number = 0
            for axis, part in zip(items[i][3], offset):
                span = span_of(grid, axis)
                number = number * len(span) + span.index(part)
            return number

        def block_of(i, offset, base):
            moved = dict(base)
            for axis, part in zip(items[i][3], offset):
                if part:
                    moved[axis] = (
                        base[axis] + part
                        if axis == "q"
                        else lax.rem(base[axis] + part, grid.size[axis])
                    )
            return grid.number(moved)

        def views(i, offset, base):
            a, first, width, order = items[i]
            columns = pl.ds(first, width)
            view = outs[a].at[block_of(i, offset, base), :, columns]
            return (ins[a].at[:, columns] if offset == (0, 0, 0) else view), view

        def send(i, offset, landed, target_step, cond_step):
            number = len(pending)

            def copy():
                source, view = views(i, offset, at)
                return pltpu.make_async_remote_copy(
                    src_ref=source,
                    dst_ref=view,
                    send_sem=send_sem.at[number],
                    recv_sem=recv_sem.at[i, slot(i, landed)],
                    device_id=grid.mesh_id(target_step()),
                    device_id_type=MESH_ID,
                )

            guarded(cond_step, lambda: copy().start())
            pending.append((q_part(i, offset), cond_step, copy))

        def forward(i, offset, stage):
            axis = items[i][3][stage]
            if axis == "q":
                part = offset[stage]
                for step in (1, -1) if part == 0 else (1,) if part < 0 else (-1,):
                    if abs(part - step) < q_size:
                        landed = offset[:stage] + (part - step,) + offset[stage + 1 :]
                        send(
                            i, offset, landed, lambda step=step: {**at, "q": at["q"] + step}, step
                        )
                return
            for step in range(1, grid.size[axis]):
                part = (offset[stage] - step) % grid.size[axis]
                landed = offset[:stage] + (part,) + offset[stage + 1 :]
                send(i, offset, landed, lambda step=step: grid.shift(at, {axis: step}), 0)

        def across(i, offset):
            def copy():
                source, view = views(i, offset, at)
                return pltpu.make_async_remote_copy(
                    src_ref=source,
                    dst_ref=view,
                    send_sem=core_send.at[i, slot(i, offset)],
                    recv_sem=core_recv.at[i, slot(i, offset)],
                    device_id=grid.mesh_id(sibling),
                    device_id_type=MESH_ID,
                )

            copy().start()
            pending.append((q_part(i, offset), 0, copy))

        def landed_at(i, offset, base, sem):
            view = views(i, offset, base)[1]
            pltpu.make_async_copy(view, view, sem.at[i, slot(i, offset)]).wait()

        def take(i, offset, stage):
            def action():
                landed_at(i, offset, at, recv_sem)
                if items[i][3][stage] == "q":
                    forward(i, offset, stage)
                for later in range(stage + 1, 3):
                    forward(i, offset, later)
                across(i, offset)

            guarded(q_part(i, offset), action)

        ranges = [[span_of(grid, axis) for axis in item[3]] for item in items]
        offsets = [
            (i, (u, v, w))
            for i in range(count)
            for u in ranges[i][0]
            for v in ranges[i][1]
            for w in ranges[i][2]
        ]
        todo = []
        for i, offset in offsets:
            if any(offset):
                stage = max(k for k in range(3) if offset[k])
                todo.append((stage,) + tuple(abs(part) for part in offset) + (i, offset))
        yield len(todo) + 1

        own_copies = []
        for a in range(len(ins)):
            own = pltpu.make_async_copy(ins[a], outs[a].at[me], own_sem.at[a])
            own.start()
            own_copies.append(own)
        for i in range(count):
            for stage in range(3):
                forward(i, (0, 0, 0), stage)
            across(i, (0, 0, 0))
        yield
        for stage, _, _, _, i, offset in sorted(todo):
            take(i, offset, stage)
            yield
        for own in own_copies:
            own.wait()
        for i, offset in offsets:
            guarded(
                q_part(i, offset), functools.partial(landed_at, i, offset, sibling, core_recv)
            )
        for q_step, cond_step, copy in pending:
            guarded(q_step, functools.partial(guarded, cond_step, lambda: copy().wait_send()))


def add_rows(target, *parts):
    rows = target.shape[0]
    step = min(16, rows)

    @pl.loop(0, rows // step)
    def _(k):
        block = pl.ds(pl.multiple_of(k * step, step), step)
        total = parts[0][block, :].astype(F32)
        for part in parts[1:]:
            total = total + part[block, :].astype(F32)
        target[block, :] = total.astype(target.dtype)


DEPTH = 2
AHEAD = 4


class Scatter:
    def __init__(self, grid, arrays, items, rounds):
        count = len(items)
        chips = grid.devices // 2
        q_size = grid.size["q"]
        self.grid, self.items, self.rounds = grid, items, rounds
        self.inputs = list(arrays)
        self.in_specs = [pl.BlockSpec(memory_space=pl.ANY)] * len(arrays)
        self.out_shapes = [jax.ShapeDtypeStruct(a.shape[1:], F32) for a in arrays]
        self.out_specs = [pl.BlockSpec(memory_space=pltpu.VMEM)] * len(arrays)
        scratch = [pltpu.VMEM((chips,) + a.shape[1:], a.dtype) for a in arrays]
        scratch += [pltpu.VMEM((2 * AHEAD,) + a.shape[1:], a.dtype) for a in arrays]
        most = 0
        for a, _, width, order in items:
            n1, n2 = (grid.size[axis] for axis in order)
            shares = ((n1 - 1) * n2 * q_size, (n2 - 1) * q_size, q_size)
            most = max(most, shares[0] + shares[1])
            for share in shares:
                scratch.append(pltpu.VMEM((share, arrays[a].shape[1], width), arrays[a].dtype))
        self.scratch = scratch + [
            pltpu.SemaphoreType.DMA((len(arrays), chips)),
            pltpu.SemaphoreType.DMA((len(arrays), chips)),
            pltpu.SemaphoreType.DMA((len(arrays), chips)),
            pltpu.SemaphoreType.DMA((count, most)),
            pltpu.SemaphoreType.DMA((count, most)),
            pltpu.SemaphoreType.DMA((count, q_size)),
            pltpu.SemaphoreType.DMA((count, q_size)),
        ]

    def steps(self, at, ins, outs, scratch):
        grid, items = self.grid, self.items
        count, arrays = len(items), len(ins)
        held, crossed = scratch[:arrays], scratch[arrays : 2 * arrays]
        landing = scratch[2 * arrays : 2 * arrays + 3 * count]
        load_sem, core_send, core_recv, send_sem, recv_sem, line_send, line_recv = scratch[
            2 * arrays + 3 * count :
        ]
        sibling = {**at, "c": 1 - at["c"]}
        size = grid.size
        q_size = size["q"]

        def flat(block):
            p, r, t = block
            return (p * size["r"] + r) * q_size + t

        def owner(base, block):
            p, r, t = block
            return grid.number({**grid.shift(base, {"p": p, "r": r}), "q": t})

        targets = []
        for t in range(q_size // 2):
            targets += [t, q_size - 1 - t]
        near_blocks = []
        for t in targets:
            near = [(p, r, t) for p in range(size["p"]) for r in range(size["r"])]
            near_blocks += sorted(near, key=lambda b: -(b[0] > 0) - (b[1] > 0))
        blocks = [(n, block) for n in range(len(self.rounds)) for block in near_blocks]
        round_of = {a: n for n, members in enumerate(self.rounds) for a in members}

        def load(a, block):
            return pltpu.make_async_copy(
                ins[a].at[owner(at, block)], held[a].at[flat(block)], load_sem.at[a, flat(block)]
            )

        def crossed_at(a, block):
            return crossed[a].at[near_blocks.index(block) % (2 * AHEAD)]

        def across(a, block):
            return pltpu.make_async_remote_copy(
                src_ref=ins[a].at[owner(sibling, block)],
                dst_ref=crossed_at(a, block),
                send_sem=core_send.at[a, flat(block)],
                recv_sem=core_recv.at[a, flat(block)],
                device_id=grid.mesh_id(sibling),
                device_id_type=MESH_ID,
            )

        def begin(number):
            if number < len(blocks):
                n, block = blocks[number]
                for a in self.rounds[n]:
                    across(a, block).start()
                    load(a, block).start()

        merged = [0]

        def merge_to(n, block):
            while merged[0] <= blocks.index((n, block)):
                turn, now = blocks[merged[0]]
                for a in self.rounds[turn]:
                    load(a, now).wait()
                    across(a, now).wait_recv()
                    view = held[a].at[flat(now)]
                    add_rows(view, view, crossed_at(a, now))
                begin(merged[0] + AHEAD)
                merged[0] += 1

        def held_view(i, block):
            return held[items[i][0]].at[flat(block), :, pl.ds(items[i][1], items[i][2])]

        def block_at(i, first, second, t):
            part = dict(zip(items[i][3], (first, second)))
            return (part["p"], part["r"], t)

        def landing_slot(i, stage, steps, t):
            n2 = size[items[i][3][1]]
            if stage == 0:
                return ((steps[0] - 1) * n2 + steps[1]) * q_size + t
            return (steps[1] - 1) * q_size + t

        pending = []

        def send(i, stage, steps, t):
            n1, n2 = (size[axis] for axis in items[i][3])
            slot = landing_slot(i, stage, steps, t)
            sem = slot if stage == 0 else (n1 - 1) * n2 * q_size + slot
            return pltpu.make_async_remote_copy(
                src_ref=held_view(i, block_at(i, *steps, t)),
                dst_ref=landing[3 * i + stage].at[slot],
                send_sem=send_sem.at[i, sem],
                recv_sem=recv_sem.at[i, sem],
                device_id=grid.mesh_id(grid.shift(at, {items[i][3][stage]: steps[stage]})),
                device_id_type=MESH_ID,
            )

        def start(i, stage, steps, t):
            copy = send(i, stage, steps, t)
            copy.start()
            pending.append(copy)

        def receive(i, stage, steps, t):
            send(i, stage, steps, t).wait_recv()
            into = (0, steps[1]) if stage == 0 else (0, 0)
            view = held_view(i, block_at(i, *into, t))
            add_rows(view, view, landing[3 * i + stage].at[landing_slot(i, stage, steps, t)])

        def line(i, t):
            return pltpu.make_async_remote_copy(
                src_ref=held_view(i, (0, 0, t)),
                dst_ref=landing[3 * i + 2].at[at["q"]],
                send_sem=line_send.at[i, t],
                recv_sem=line_recv.at[i, at["q"]],
                device_id=grid.mesh_id({**at, "q": t}),
                device_id_type=MESH_ID,
            )

        def close(i, t):
            for second in range(1, size[items[i][3][1]]):
                receive(i, 1, (0, second), t)
            pl.when(at["q"] != t)(lambda: line(i, t).start())

        def finish(i):
            a, first, width, _ = items[i]
            parts = [held[a].at[at["q"], :, pl.ds(first, width)]]
            for step in range(1, q_size):
                source = lax.rem(at["q"] + step, q_size)
                view = landing[3 * i + 2].at[source]
                pltpu.make_async_copy(view, view, line_recv.at[i, source]).wait()
                parts.append(view)
            add_rows(outs[a].at[:, pl.ds(first, width)], *parts)

        ticks = []
        for n, members in enumerate(self.rounds):
            mine = [i for i in range(count) if items[i][0] in members]
            for t in targets:
                for far in (True, False):
                    turn = []
                    for i in mine:
                        n1, n2 = (size[axis] for axis in items[i][3])
                        for second in range(1, n2) if far else (0,):
                            for first in range(1, n1):
                                turn.append((i, (first, second), t))
                    ticks.append((n, turn, None if far else (mine, t)))
        yield sum(2 * len(turn) for _, turn, _ in ticks) + q_size * count + count

        for number in range(AHEAD):
            begin(number)
        closing, finishing = [], []
        for k in range(len(ticks) + DEPTH):
            if k < len(ticks):
                n, turn, _ = ticks[k]
                for i, steps, t in turn:
                    merge_to(n, block_at(i, *steps, t))
                    start(i, 0, steps, t)
                    yield
            if k >= DEPTH:
                n, turn, done = ticks[k - DEPTH]
                for i, steps, t in turn:
                    merge_to(n, block_at(i, 0, steps[1], t))
                    receive(i, 0, steps, t)
                    if steps[1] and steps[0] == size[items[i][3][0]] - 1:
                        start(i, 1, (0, steps[1]), t)
                    yield
                if closing and done is None:
                    for i in closing[0][0]:
                        close(i, closing[0][1])
                        yield
                    if closing[0][1] == targets[-1]:
                        finishing.append(closing[0][0])
                    closing.pop()
                    if len(finishing) > 1:
                        for i in finishing.pop(0):
                            finish(i)
                            yield
                if done is not None:
                    closing.append(done)
        for mine, t in closing:
            for i in mine:
                close(i, t)
                yield
            finishing.append(mine)
        for mine in finishing:
            for i in mine:
                finish(i)
                yield
        for n, block in blocks:
            for a in self.rounds[n]:
                across(a, block).wait_send()
        for copy in pending:
            copy.wait_send()
        for i in range(count):
            for t in range(q_size):
                pl.when(at["q"] != t)(lambda: line(i, t).wait_send())


def together(grid, parts, collective_id, name):
    def kernel(*refs):
        at = grid.here()
        if collective_id is not None:
            greet(grid, at)
        ins, outs, scratch = [], [], []
        for list_of, key in ((ins, "inputs"), (outs, "out_shapes"), (scratch, "scratch")):
            for part in parts:
                count = len(getattr(part, key))
                list_of.append(refs[:count])
                refs = refs[count:]
        running = []
        for part, *its in zip(parts, ins, outs, scratch):
            steps = part.steps(at, *its)
            running.append([steps, next(steps), 0])
        while running:
            now = min(running, key=lambda entry: entry[2] / entry[1])
            now[2] += 1
            if next(now[0], "end") == "end":
                running.remove(now)

    outs = pl.pallas_call(
        kernel,
        out_shape=[shape for part in parts for shape in part.out_shapes],
        in_specs=[spec for part in parts for spec in part.in_specs],
        out_specs=[spec for part in parts for spec in part.out_specs],
        scratch_shapes=[entry for part in parts for entry in part.scratch],
        compiler_params=pltpu.CompilerParams(
            collective_id=collective_id,
            has_side_effects=collective_id is not None,
            vmem_limit_bytes=62 * 2**20,
        ),
        name=name,
    )(*[array for part in parts for array in part.inputs])
    split = []
    for part in parts:
        split.append(outs[: len(part.out_shapes)])
        outs = outs[len(part.out_shapes) :]
    return split


GROUP = 256


def tiles(extent, width):
    def wrap(action):
        width_now = min(width, extent)

        @pl.loop(0, extent // width_now)
        def _(k):
            action(pl.ds(pl.multiple_of(k * width_now, width_now), width_now))

    return wrap


class Experts:
    def __init__(self, hidden, grad, share, weights, capacity):
        gate, up, down, shared_in, shared_down = weights
        count = hidden.shape[0]
        window = gate.shape[1]
        self.supers = count // (2 * GROUP)
        self.slots = GROUP // SEQ * capacity
        self.capacity = capacity
        self.window = window
        rows = 2 * self.slots
        total = self.supers * rows
        groups = count // GROUP
        self.inputs = [hidden, grad, share, gate, up, down, shared_in, shared_down]
        hbm = pl.BlockSpec(memory_space=pl.ANY)
        vmem = pl.BlockSpec(memory_space=pltpu.VMEM)
        self.in_specs = [hbm, hbm] + [vmem] * 6
        shared_width = shared_in.shape[1]
        kept = [(rows, D), (rows, D), (rows, 2 * window), (rows, window)]
        kept += [(2 * GROUP, shared_width), (2 * GROUP, shared_width // 2)]
        self.out_shapes = [
            jax.ShapeDtypeStruct((count, D), BF),
            jax.ShapeDtypeStruct((count, D), BF),
            jax.ShapeDtypeStruct((groups, GROUP), F32),
        ] + [jax.ShapeDtypeStruct((self.supers * r, c), BF) for r, c in kept]
        self.out_specs = [hbm, hbm, vmem] + [hbm] * len(kept)
        self.scratch = (
            [pltpu.VMEM((2 * GROUP, D), BF)] * 2
            + [pltpu.VMEM((2, r, c), BF) for r, c in kept]
            + [pltpu.VMEM((2, GROUP, D), BF)] * 2
            + [pltpu.VMEM((rows, window), F32)] * 3
            + [pltpu.VMEM((rows, D), BF)] * 2
            + [
                pltpu.VMEM((groups, GROUP), F32),
                pltpu.VMEM((2, self.slots, GROUP), BF),
                pltpu.VMEM((2, GROUP, self.slots), BF),
                pltpu.VMEM((rows, 1), F32),
                pltpu.VMEM((rows, 1), F32),
                pltpu.VMEM((2 * GROUP, shared_width), F32),
                pltpu.SemaphoreType.DMA((2,)),
                pltpu.SemaphoreType.DMA((len(kept), 2)),
                pltpu.SemaphoreType.DMA((2, 2)),
            ]
        )

    def steps(self, at, ins, outs, scratch):
        hidden, grad, share, gate, up, down, shared_in, shared_down = ins
        hidden_out, out_out, gate_grad = outs[:3]
        kept_out = outs[3:]
        hidden_in, grad_in = scratch[:2]
        kept = scratch[2:8]
        parts = scratch[8:10]
        a_pre, b_pre, flow = scratch[10:13]
        row_grad, expert_out = scratch[13:15]
        keys, picks, picks_t, share_rows, gate_rows, shared_pre = scratch[15:21]
        load_sem, keep_sem, part_sem = scratch[21:]
        slots, window, supers = self.slots, self.window, self.supers
        rows = 2 * slots
        half = shared_in.shape[1] // 2
        yield supers * 12

        def load(k):
            piece = pl.ds(k * 2 * GROUP, 2 * GROUP)
            return (
                pltpu.make_async_copy(hidden.at[piece, :], hidden_in, load_sem.at[0]),
                pltpu.make_async_copy(grad.at[piece, :], grad_in, load_sem.at[1]),
            )

        def keep(n, k):
            extent = kept[n].shape[1]
            return pltpu.make_async_copy(
                kept[n].at[k % 2],
                kept_out[n].at[pl.ds(k * extent, extent), :],
                keep_sem.at[n, k % 2],
            )

        def put(n, k, j):
            target = (hidden_out, out_out)[n]
            piece = pl.ds((2 * k + j) * GROUP, GROUP)
            return pltpu.make_async_copy(parts[n].at[j], target.at[piece, :], part_sem.at[n, j])

        for copy in load(0):
            copy.start()
        row_of = lax.broadcasted_iota(jnp.int32, (GROUP, GROUP), 0)
        column_of = lax.broadcasted_iota(jnp.int32, (GROUP, GROUP), 1)
        same = lax.div(row_of, SEQ) == lax.div(column_of, SEQ)
        earlier = jnp.logical_and(same, row_of < column_of).astype(BF)
        chosen = (share[...] >= 0).astype(F32)
        place = jnp.dot(chosen.astype(BF), earlier, preferred_element_type=F32)
        sequence = lax.div(lax.broadcasted_iota(jnp.int32, place.shape, 1), SEQ).astype(F32)
        keys[...] = jnp.where(chosen > 0, place + sequence * self.capacity, -1.0)

        for k in range(supers):
            slot = k % 2
            rows_in, grad_rows, ab_grad, scaled, shared_grad, shared_inner = (
                buffer.at[slot] for buffer in kept
            )
            if k >= 2:
                for n in range(len(kept)):
                    keep(n, k - 2).wait()
            for j in range(2):
                key = keys[pl.ds(2 * k + j, 1), :]
                number = lax.broadcasted_iota(jnp.int32, (slots, GROUP), 0).astype(F32)
                pick = (number == key).astype(F32)
                picks[j] = pick.astype(BF)
                picks_t[j] = pick.T.astype(BF)
                weight = share[pl.ds(2 * k + j, 1), :]
                share_rows[pl.ds(j * slots, slots), :] = jnp.sum(
                    pick * weight, axis=1, keepdims=True
                )
            for copy in load(k):
                copy.wait()
            for source, target in ((hidden_in, rows_in), (grad_in, grad_rows)):
                for j in range(2):

                    @tiles(D, 512)
                    def _(columns):
                        target[pl.ds(j * slots, slots), columns] = jnp.dot(
                            picks[j],
                            source[pl.ds(j * GROUP, GROUP), columns],
                            preferred_element_type=F32,
                        ).astype(BF)

                yield
            for weight, target in ((gate, a_pre), (up, b_pre)):

                @tiles(window, 256)
                def _(columns):
                    target[:, columns] = jnp.dot(
                        rows_in[...], weight[:, columns], preferred_element_type=F32
                    )

                yield

            @tiles(window, 256)
            def _(columns):
                flow[:, columns] = dot_t(grad_rows[...], down[columns, :])

            yield

            @tiles(rows, 32)
            def _(block):
                a = a_pre[block, :]
                b = b_pre[block, :]
                u = flow[block, :]
                weight = share_rows[block, :]
                sigma = jax.nn.sigmoid(a)
                act = a * sigma
                inner = (act * b).astype(BF).astype(F32)
                gate_rows[block, :] = jnp.sum(inner * u, axis=1, keepdims=True)
                scaled[block, :] = (inner * weight).astype(BF)
                u = u * weight
                ab_grad[block, pl.ds(0, window)] = (
                    u * b * (sigma * (1.0 + a * (1.0 - sigma)))
                ).astype(BF)
                ab_grad[block, pl.ds(window, window)] = (u * act).astype(BF)

            for j in range(2):
                pick = picks[j].astype(F32)
                gate_grad[pl.ds(2 * k + j, 1), :] = jnp.sum(
                    pick * gate_rows[pl.ds(j * slots, slots), :], axis=0, keepdims=True
                )
            yield

            @tiles(D, 256)
            def _(columns):
                row_grad[:, columns] = (
                    dot_t(ab_grad[:, pl.ds(0, window)], gate[columns, :])
                    + dot_t(ab_grad[:, pl.ds(window, window)], up[columns, :])
                ).astype(BF)

            yield

            @tiles(D, 512)
            def _(columns):
                expert_out[:, columns] = jnp.dot(
                    scaled[...], down[:, columns], preferred_element_type=F32
                ).astype(BF)

            yield

            @tiles(2 * GROUP, GROUP)
            def _(block):
                shared_pre[block, :] = jnp.dot(
                    hidden_in[block, :], shared_in[...], preferred_element_type=F32
                )

            yield

            @tiles(2 * GROUP, GROUP)
            def _(block):
                u = dot_t(grad_in[block, :], shared_down[...])
                a = shared_pre[block, pl.ds(0, half)]
                b = shared_pre[block, pl.ds(half, half)]
                sigma = jax.nn.sigmoid(a)
                act = a * sigma
                shared_inner[block, :] = (act * b).astype(BF)
                shared_grad[block, pl.ds(0, half)] = (
                    u * b * (sigma * (1.0 + a * (1.0 - sigma)))
                ).astype(BF)
                shared_grad[block, pl.ds(half, half)] = (u * act).astype(BF)

            for n in range(len(kept)):
                keep(n, k).start()
            if k + 1 < supers:
                for copy in load(k + 1):
                    copy.start()
            yield
            for j in range(2):
                if k:
                    put(0, k - 1, j).wait()

                @tiles(D, 256)
                def _(columns):
                    parts[0][j, :, columns] = (
                        jnp.dot(
                            picks_t[j],
                            row_grad[pl.ds(j * slots, slots), columns],
                            preferred_element_type=F32,
                        )
                        + dot_t(shared_grad[pl.ds(j * GROUP, GROUP), :], shared_in[columns, :])
                    ).astype(BF)

                put(0, k, j).start()
            yield
            for j in range(2):
                if k:
                    put(1, k - 1, j).wait()

                @tiles(D, 256)
                def _(columns):
                    parts[1][j, :, columns] = (
                        jnp.dot(
                            picks_t[j],
                            expert_out[pl.ds(j * slots, slots), columns],
                            preferred_element_type=F32,
                        )
                        + jnp.dot(
                            shared_inner[pl.ds(j * GROUP, GROUP), :],
                            shared_down[:, columns],
                            preferred_element_type=F32,
                        )
                    ).astype(BF)

                put(1, k, j).start()
            yield
        for k in range(max(0, supers - 2), supers):
            for n in range(len(kept)):
                keep(n, k).wait()
        for n in range(2):
            for j in range(2):
                put(n, supers - 1, j).wait()


def gather_all(grid, arrays, items, collective_id):
    return together(grid, [Gather(grid, arrays, items)], collective_id, "gather_all")[0]


def sum_scattered(grid, arrays, items, rounds, collective_id):
    part = Scatter(grid, arrays, items, rounds)
    return together(grid, [part], collective_id, "sum_scattered")[0]


def normalize(values, gain_row):
    scale_rows = lax.rsqrt(jnp.mean(values * values, -1, keepdims=True) + EPSILON)
    return (values * scale_rows * gain_row, scale_rows)


def normalize_back(values, scale_rows, gain_row, gradient):
    weighted = gradient * gain_row
    gain_grad = jnp.sum(gradient * values * scale_rows, 0)
    inner_mean = jnp.mean(weighted * values, -1, keepdims=True)
    return (
        scale_rows * weighted - values * scale_rows * scale_rows * scale_rows * inner_mean,
        gain_grad,
    )


def rope_tables(length, width):
    half_width = width // 2
    frequency = ROPE_BASE ** (-2.0 * jnp.arange(half_width, dtype=jnp.float32) / width)
    angles = jnp.arange(length, dtype=jnp.float32)[:, None] * frequency[None, :]
    return (jnp.cos(angles), jnp.sin(angles))


def rotate(values, cosine, sine_table):
    half_width = values.shape[-1] // 2
    front_half = values[..., :half_width]
    back_half = values[..., half_width:]
    return jnp.concatenate(
        [
            front_half * cosine - back_half * sine_table,
            back_half * cosine + front_half * sine_table,
        ],
        -1,
    )


def unrotate(gradient, cosine, sine_table):
    half_width = gradient.shape[-1] // 2
    front_half = gradient[..., :half_width]
    back_half = gradient[..., half_width:]
    return jnp.concatenate(
        [
            front_half * cosine + back_half * sine_table,
            back_half * cosine - front_half * sine_table,
        ],
        -1,
    )


def capacity_for(expert_count):
    return min(SEQ, ((4 * SEQ * TOP + 3 * expert_count - 1) // (3 * expert_count) + 7) // 8 * 8)


def silu_parts(pre_act):
    sigma_rows = jax.nn.sigmoid(pre_act)
    return (pre_act * sigma_rows, sigma_rows * (1.0 + pre_act * (1.0 - sigma_rows)))


def attention_mask(segment_row):
    places = jnp.arange(segment_row.shape[0], dtype=jnp.int32)
    return (places[:, None] >= places[None, :]) & (segment_row[:, None] == segment_row[None, :])


def dot(left, right):
    return jnp.dot(left, right, preferred_element_type=F32)


def dot_t(left, right):
    return lax.dot_general(left, right, (((1,), (1,)), ((), ())), preferred_element_type=F32)


def t_dot(left, right):
    return lax.dot_general(left, right, (((0,), (0,)), ((), ())), preferred_element_type=F32)


def pack(parts, rows):
    flat = jnp.concatenate([part.reshape(rows, -1) for part in parts], 1)
    width = -(-flat.shape[1] // 2048) * 2048
    flat = jnp.pad(flat, ((0, 0), (0, width - flat.shape[1])))
    return flat.reshape(rows, width // 128, 128)


def unpack(block, shapes):
    rows = block.shape[0]
    flat = block.reshape(rows, -1)
    parts, first = [], 0
    for shape in shapes:
        size = 1
        for extent in shape:
            size *= extent
        parts.append(flat[:, first : first + size].reshape((rows,) + shape))
        first += size
    return parts


def swap_windows(pieces, axis_size):
    me = lax.axis_index("dp")
    got = [pieces(me)]
    for step in range(1, axis_size):
        peer = lax.rem(me + step, axis_size)
        perm = [(k, (k + step) % axis_size) for k in range(axis_size)]
        got.append(lax.ppermute(pieces(peer), "dp", perm))
    return got


def in_order(got):
    me = lax.axis_index("dp")
    count = len(got)
    ordered = []
    for k in range(count):
        value = got[0]
        for step in range(1, count):
            value = jnp.where(lax.rem(me - k + count, count) == step, got[step], value)
        ordered.append(value)
    return ordered


def attention_forward(rows, segments, weights, tables):
    attn_gain, q_weight, kv_down, kv_gain, kv_up, out_weight, ffn_gain, router = weights
    cosine, sine_table = tables
    count = rows.shape[0]
    inputs = rows.astype(F32)
    normed_f, scale_one = normalize(inputs, attn_gain)
    normed = normed_f.astype(BF)
    q_raw = dot(normed, q_weight).reshape(MICRO, SEQ, HEADS, NOPE + ROPE)
    turn = (cosine[:, None, :], sine_table[:, None, :])
    queries = jnp.concatenate([q_raw[..., :NOPE], rotate(q_raw[..., NOPE:], *turn)], -1).astype(BF)
    kv_raw = dot(normed, kv_down)
    latent_f, scale_latent = normalize(kv_raw[:, :RANK], kv_gain)
    latent = latent_f.astype(BF)
    key_rope = rotate(kv_raw[:, RANK:].reshape(MICRO, SEQ, ROPE), cosine, sine_table)
    kv_full = dot(latent, kv_up).reshape(MICRO, SEQ, HEADS, NOPE + VDIM)
    shared_key = jnp.broadcast_to(key_rope[:, :, None, :], (MICRO, SEQ, HEADS, ROPE))
    key_rows = jnp.concatenate([kv_full[..., :NOPE], shared_key], -1).astype(BF)
    value_rows = kv_full[..., NOPE:].astype(BF)
    allowed = jax.vmap(attention_mask)(segments)[:, None]
    scores = jnp.einsum("mqhe,mkhe->mhqk", queries, key_rows, preferred_element_type=F32)
    scores = jnp.where(allowed, scores * (NOPE + ROPE) ** (-0.5), MASKED)
    powers = jnp.exp(scores - jnp.max(scores, -1, keepdims=True))
    softmax_rows = powers / jnp.sum(powers, -1, keepdims=True)
    probability = softmax_rows.astype(BF)
    attended = (
        jnp.einsum("mhqk,mkhe->mqhe", probability, value_rows, preferred_element_type=F32)
        .reshape(count, HEADS * VDIM)
        .astype(BF)
    )
    residual = inputs + dot(attended, out_weight)
    hidden_f, scale_two = normalize(residual, ffn_gain)
    hidden = hidden_f.astype(BF)
    saved = (
        inputs, scale_one, normed, queries, kv_raw, scale_latent, latent, key_rows, value_rows,
        softmax_rows, probability, attended, residual, scale_two,
    )
    return hidden, saved


def attention_backward(grad_out, hidden_grad, saved, weights, tables):
    attn_gain, q_weight, kv_down, kv_gain, kv_up, out_weight, ffn_gain, router = weights
    cosine, sine_table = tables
    (
        inputs, scale_one, normed, queries, kv_raw, scale_latent, latent, key_rows, value_rows,
        softmax_rows, probability, attended, residual, scale_two,
    ) = saved
    count = inputs.shape[0]
    turn = (cosine[:, None, :], sine_table[:, None, :])
    residual_part, ffn_gain_grad = normalize_back(residual, scale_two, ffn_gain, hidden_grad)
    residual_grad = grad_out + residual_part
    mixed_grad = residual_grad.astype(BF)
    out_weight_grad = t_dot(attended, mixed_grad)
    attended_grad = dot_t(mixed_grad, out_weight).astype(BF).reshape(MICRO, SEQ, HEADS, VDIM)
    value_grad = jnp.einsum(
        "mhqk,mqhe->mkhe", probability, attended_grad, preferred_element_type=F32
    )
    probs_grad = jnp.einsum(
        "mqhe,mkhe->mhqk", attended_grad, value_rows, preferred_element_type=F32
    )
    inner = jnp.sum(softmax_rows * probs_grad, -1, keepdims=True)
    score_grad = (softmax_rows * (probs_grad - inner)).astype(BF)
    score_scale = (NOPE + ROPE) ** (-0.5)
    query_grad = score_scale * jnp.einsum(
        "mhqk,mkhe->mqhe", score_grad, key_rows, preferred_element_type=F32
    )
    keys_grad = score_scale * jnp.einsum(
        "mhqk,mqhe->mkhe", score_grad, queries, preferred_element_type=F32
    )
    q_raw_grad = (
        jnp.concatenate([query_grad[..., :NOPE], unrotate(query_grad[..., NOPE:], *turn)], -1)
        .reshape(count, HEADS * (NOPE + ROPE))
        .astype(BF)
    )
    q_weight_grad = t_dot(normed, q_raw_grad)
    kv_full_grad = (
        jnp.concatenate([keys_grad[..., :NOPE], value_grad], -1)
        .reshape(count, HEADS * (NOPE + VDIM))
        .astype(BF)
    )
    kv_up_grad = t_dot(latent, kv_full_grad)
    latent_grad = dot_t(kv_full_grad, kv_up)
    latent_part, kv_gain_grad = normalize_back(
        kv_raw[:, :RANK], scale_latent, kv_gain, latent_grad
    )
    rope_grad = unrotate(jnp.sum(keys_grad[..., NOPE:], 2), cosine, sine_table)
    kv_raw_grad = jnp.concatenate([latent_part, rope_grad.reshape(count, ROPE)], -1).astype(BF)
    kv_down_grad = t_dot(normed, kv_raw_grad)
    normed_grad = dot_t(q_raw_grad, q_weight) + dot_t(kv_raw_grad, kv_down)
    input_part, attn_gain_grad = normalize_back(inputs, scale_one, attn_gain, normed_grad)
    tokens_grad = residual_grad + input_part
    return tokens_grad, (
        attn_gain_grad, q_weight_grad, kv_down_grad, kv_gain_grad, kv_up_grad, out_weight_grad,
        ffn_gain_grad,
    )


def body(
    grid,
    tokens,
    cotangent,
    routes,
    segments,
    attn_gain,
    q_weight,
    kv_down,
    kv_gain,
    kv_up,
    out_weight,
    ffn_gain,
    router,
    shared_gate,
    shared_up,
    shared_down,
    expert_gate,
    expert_up,
    expert_down,
):
    devices = grid.devices
    dp_size = grid.size["p"]
    experts = router.shape[1]
    tables = rope_tables(SEQ, ROPE)
    me_dp = lax.axis_index("dp")
    count = MICRO * SEQ
    eff = expert_gate.shape[2]

    window = -(-eff // (128 * dp_size)) * 128
    starts = [min(k * window, eff - window) for k in range(dp_size)]

    def start_of(peer):
        return jnp.minimum(peer * window, eff - window)

    def columns_for(array):
        return lambda peer: lax.dynamic_slice_in_dim(array[0], start_of(peer), window, 1)

    def rows_for(array):
        return lambda peer: lax.dynamic_slice_in_dim(array[0], start_of(peer), window, 0)

    gate_part = jnp.concatenate(in_order(swap_windows(columns_for(expert_gate), dp_size)), 0)
    up_part = jnp.concatenate(in_order(swap_windows(columns_for(expert_up), dp_size)), 0)
    down_part = jnp.concatenate(in_order(swap_windows(rows_for(expert_down), dp_size)), 1)
    fresh = jnp.arange(window, dtype=jnp.int32) + start_of(me_dp) >= me_dp * window
    gate_part = jnp.where(fresh[None, :], gate_part, 0)
    up_part = jnp.where(fresh[None, :], up_part, 0)
    down_part = jnp.where(fresh[:, None], down_part, 0)

    share = shared_gate.shape[1] // devices
    both = jnp.concatenate(
        [shared_gate.reshape(-1, devices, share), shared_up.reshape(-1, devices, share)], 2
    )
    shared_in = lax.all_to_all(
        both.transpose(1, 0, 2), ("dp", "expert"), split_axis=0, concat_axis=0, tiled=True
    ).reshape(D, 2 * share)
    room = -(-share // 128) * 128
    shared_in = jnp.concatenate(
        [
            jnp.pad(shared_in[:, :share], ((0, 0), (0, room - share))),
            jnp.pad(shared_in[:, share:], ((0, 0), (0, room - share))),
        ],
        1,
    )
    shared_part = jnp.pad(shared_down, ((0, room - share), (0, 0)))

    small_shapes = (attn_gain.shape, ffn_gain.shape, kv_gain.shape, router.shape)
    small = pack([attn_gain[None], ffn_gain[None], kv_gain[None], router[None]], 1)[0]
    up_shape = kv_up.shape
    kv_up_sent = kv_up if up_shape[0] % 16 == 0 else kv_up.reshape(16, -1)
    first, second = ("q", "r", "p"), ("q", "p", "r")
    got = gather_all(
        grid,
        [q_weight, kv_down, kv_up_sent, out_weight, small],
        [
            (0, 0, q_weight.shape[1], first),
            (3, 0, out_weight.shape[1], second),
            (2, 0, kv_up_sent.shape[1], second),
            (1, 0, kv_down.shape[1], second),
            (4, 0, 128, first),
        ],
        0,
    )
    gains = unpack(got[4], small_shapes)
    weights = (
        gains[0].reshape(-1).astype(F32),
        got[0].reshape(D, -1),
        got[1].reshape(D, -1),
        gains[2].reshape(-1).astype(F32),
        got[2].reshape(RANK, -1),
        got[3].reshape(-1, D),
        gains[1].reshape(-1).astype(F32),
        gains[3].reshape(D, experts),
    )
    router_full = weights[7]

    token_rows = tokens.reshape(count, D)
    grad_out = cotangent.reshape(count, D)
    route_rows = routes.reshape(count, TOP)
    hidden, saved = attention_forward(token_rows, segments.reshape(MICRO, SEQ), weights, tables)
    logits = dot(hidden, router_full)
    choose = route_rows[:, :, None] == jnp.arange(experts, dtype=jnp.int32)[None, None, :]
    choose = choose.astype(F32)
    gate_share = jax.nn.softmax(jnp.sum(choose * logits[:, None, :], -1), -1)
    dense_share = jnp.sum(choose * gate_share[..., None], 1)
    dense_gates = jnp.where(jnp.sum(choose, 1) > 0, dense_share, -1.0)

    half = D // 2
    capacity = capacity_for(experts)
    expert = lax.axis_index("expert")
    own_weights = (gate_part, up_part, down_part, shared_in, shared_part)

    def gather_of(chunk):
        piece = slice(chunk * SEQ, (chunk + 1) * SEQ)
        sent = [hidden[piece], grad_out[piece], dense_gates[piece].T]
        orders = [(0, 0, half, first), (0, half, half, second)]
        orders += [(1, 0, half, first), (1, half, half, second), (2, 0, SEQ, first)]
        return Gather(grid, sent, orders)

    kept_hidden, kept_grad = [], []

    def experts_of(gathered):
        hidden_all, grad_all, gates_all = gathered
        kept_hidden.append(hidden_all)
        kept_grad.append(grad_all)
        share = lax.dynamic_index_in_dim(gates_all, expert, 1, keepdims=False)
        return Experts(
            hidden_all.reshape(-1, D),
            grad_all.reshape(-1, D),
            share.reshape(-1, GROUP),
            own_weights,
            capacity,
        )

    def sums_of(done):
        hidden_part, out_part, gate_grad = done[:3]
        mine = (jnp.arange(experts, dtype=jnp.int32) == expert)[None, :, None]
        gate_grad = jnp.where(mine, gate_grad.reshape(devices, 1, SEQ), 0.0)
        shape = (devices, SEQ, D)
        return [hidden_part.reshape(shape), gate_grad, out_part.reshape(shape)]

    over = [(0, 0, half, ("p", "r")), (0, half, half, ("r", "p"))]
    over_gates = [(1, 0, SEQ, ("p", "r"))]
    over_out = [(2, 0, half, ("p", "r")), (2, half, half, ("r", "p"))]
    if devices <= 32:
        (gathered,) = together(grid, [gather_of(0)], 1, "gather_first")
        gathered, done_0 = together(
            grid, [gather_of(1), experts_of(gathered)], 2, "gather_second_experts_first"
        )
        everything = over + over_gates + over_out
        sums_0, done_1 = together(
            grid,
            [Scatter(grid, sums_of(done_0), everything, [[0, 1], [2]]), experts_of(gathered)],
            3,
            "scatter_first_experts_second",
        )
        (sums_1,) = together(
            grid, [Scatter(grid, sums_of(done_1), everything, [[0, 1], [2]])], 4, "scatter_second"
        )
        sums, done = (sums_0, sums_1), (done_0, done_1)
    else:
        sums, done = [], []
        for chunk in range(MICRO):
            part = gather_of(chunk)
            if chunk:
                before = tuple(sums[-1])
                *part.inputs, sums[-1] = lax.optimization_barrier((*part.inputs, before))
            (gathered,) = together(grid, [part], 1, "gather")
            part = experts_of(gathered)
            (now,) = together(grid, [part], None, "experts")
            parts = sums_of(now)
            (hidden_gates,) = together(
                grid, [Scatter(grid, parts[:2], over + over_gates, [[0, 1]])], 2, "scatter_hidden"
            )
            (out_sum,) = together(grid, [Scatter(grid, parts[2:], over, [[0]])], 3, "scatter_out")
            sums.append((*hidden_gates, *out_sum))
            done.append(now)
    hidden_sum = jnp.concatenate([entry[0] for entry in sums], 0)
    gate_grad = jnp.concatenate([entry[1].T for entry in sums], 0)
    result = saved[12] + jnp.concatenate([entry[2] for entry in sums], 0)

    dense_share = jnp.maximum(dense_share, 0.0)
    inner = jnp.sum(dense_share * gate_grad, -1, keepdims=True)
    logit_grad = (dense_share * (gate_grad - inner)).astype(BF)
    router_grad = t_dot(hidden, logit_grad)
    hidden_grad = hidden_sum + dot_t(logit_grad, router_full)
    tokens_grad, (
        attn_gain_grad, q_weight_grad, kv_down_grad, kv_gain_grad, kv_up_grad, out_weight_grad,
        ffn_gain_grad,
    ) = attention_backward(grad_out.astype(F32), hidden_grad, saved, weights, tables)

    small_grads = pack(
        [
            attn_gain_grad.reshape(devices, -1),
            ffn_gain_grad.reshape(devices, -1),
            kv_gain_grad.reshape(devices, -1),
            router_grad.reshape(devices, -1),
        ],
        devices,
    )
    def halves(a, columns):
        part = columns // 256 * 128
        return [(a, 0, part, ("p", "r")), (a, part, columns - part, ("r", "p"))]

    q_sum, down_sum, up_sum, out_weight_sum, small_sum = sum_scattered(
        grid,
        [
            q_weight_grad.astype(BF).reshape((devices,) + q_weight.shape),
            kv_down_grad.astype(BF).reshape((devices,) + kv_down.shape),
            kv_up_grad.astype(BF).reshape((devices,) + kv_up_sent.shape),
            out_weight_grad.astype(BF).reshape((devices,) + out_weight.shape),
            small_grads,
        ],
        halves(0, q_weight.shape[1])
        + halves(1, kv_down.shape[1])
        + halves(2, kv_up_sent.shape[1])
        + halves(3, out_weight.shape[1])
        + [(4, 0, 128, ("p", "r"))],
        [[3], [2, 1], [0, 4]],
        5,
    )
    small_sums = unpack(small_sum[None], small_shapes)

    def total(pairs):
        return functools.reduce(jnp.add, [t_dot(left, right) for left, right in pairs])

    kept = [entry[3:] for entry in done]
    chunks = range(MICRO)
    both_grad = total([(kept[c][0], kept[c][2]) for c in chunks])
    gate_grad_part, up_grad_part = both_grad[:, :window], both_grad[:, window:]
    down_grad_part = total([(kept[c][3], kept[c][1]) for c in chunks])
    hidden_rows = [kept_hidden[c].reshape(-1, D) for c in chunks]
    grad_rows = [kept_grad[c].reshape(-1, D) for c in chunks]
    shared_in_grad = total([(hidden_rows[c], kept[c][4]) for c in chunks])
    shared_down_grad = total([(kept[c][5], grad_rows[c]) for c in chunks])[:share]
    shared_in_grad = jnp.concatenate(
        [shared_in_grad[:, :share], shared_in_grad[:, room : room + share]], 1
    )
    shared_back = lax.all_to_all(
        shared_in_grad.astype(BF).reshape(devices, -1, 2 * share),
        ("dp", "expert"), split_axis=0, concat_axis=0, tiled=True,
    ).astype(F32)
    shared_back = shared_back.transpose(1, 0, 2)
    shared_gate_grad = shared_back[:, :, :share].reshape(shared_gate.shape)
    shared_up_grad = shared_back[:, :, share:].reshape(shared_up.shape)

    def whole(part, axis, other, extent):
        def for_peer(peer):
            return lax.dynamic_slice_in_dim(part, peer * extent, extent, other)

        got_back = swap_windows(lambda peer: for_peer(peer).astype(BF), dp_size)
        got_back = [for_peer(me_dp)] + [piece.astype(F32) for piece in got_back[1:]]
        pieces = []
        for k, piece in enumerate(in_order(got_back)):
            skip = k * window - starts[k]
            pieces.append(lax.slice_in_dim(piece, skip, window, axis=axis))
        return jnp.concatenate(pieces, axis)[None]

    extent = expert_gate.shape[1]
    return (
        result.astype(BF).reshape(tokens.shape),
        tokens_grad.astype(BF).reshape(tokens.shape),
        small_sums[0].reshape(-1),
        q_sum,
        down_sum,
        small_sums[2].reshape(-1),
        up_sum.reshape(up_shape),
        out_weight_sum,
        small_sums[1].reshape(-1),
        small_sums[3].reshape(router.shape),
        shared_gate_grad,
        shared_up_grad,
        shared_down_grad,
        whole(gate_grad_part, 1, 0, extent),
        whole(up_grad_part, 1, 0, extent),
        whole(down_grad_part, 0, 1, extent),
    )


def solution(mesh):
    return jax.shard_map(
        functools.partial(body, Grid(mesh)),
        mesh=mesh,
        in_specs=(
            P(None, ("dp", "expert"), None, None),
            P(None, ("dp", "expert"), None, None),
            P(None, ("dp", "expert"), None, None),
            P(None, ("dp", "expert"), None),
            P(("dp", "expert")),
            P(("dp", "expert"), None),
            P(("dp", "expert"), None),
            P(("dp", "expert")),
            P(("dp", "expert"), None),
            P(("dp", "expert"), None),
            P(("dp", "expert")),
            P(("dp", "expert"), None),
            P(("dp", "expert"), None),
            P(("dp", "expert"), None),
            P(("dp", "expert"), None),
            P("expert", "dp", None),
            P("expert", "dp", None),
            P("expert", None, "dp"),
        ),
        out_specs=(
            P(None, ("dp", "expert"), None, None),
            P(None, ("dp", "expert"), None, None),
            P(("dp", "expert")),
            P(("dp", "expert"), None),
            P(("dp", "expert"), None),
            P(("dp", "expert")),
            P(("dp", "expert"), None),
            P(("dp", "expert"), None),
            P(("dp", "expert")),
            P(("dp", "expert"), None),
            P(("dp", "expert"), None),
            P(("dp", "expert"), None),
            P(("dp", "expert"), None),
            P("expert", "dp", None),
            P("expert", "dp", None),
            P("expert", None, "dp"),
        ),
        check_vma=False,
    )
```

time: 1290 us -> 1140 us (0.88)
  matrix products: 301 us -> 113 us
  Pallas kernels: 793 us -> 834 us
    dot_general x10 -> x5, matrix products: 89.7 us -> 22.2 us  [dot_t(): lax.dot_general(left, right, (((1,), (1,)), ((), ())), preferred_element_...]
    dot_general x5 -> x0, matrix products: 57.8 us -> none  [the longest x1 21.2 us: experts_step(): jnp.einsum('bst,bsd->btd', picks, expert_out.reshape(blocks, capacity, D)...]
    dot_general x10 -> x5, matrix products: 74.9 us -> 20.8 us  [dot(): return jnp.dot(left, right, preferred_element_type=F32)]
    pallas_call x5 -> x6, Pallas kernels: 793 us -> 834 us  [together(): pl.pallas_call(kernel, out_shape=[shape for part in parts for shape in pa...]
    dynamic_slice x5 -> x2, local copies, waits for them, and re-layouts: 19.9 us -> 3.8 us  [columns_for(): lax.dynamic_slice_in_dim(array[0], start_of(peer), window, 1)]
    slice x0 -> x7, local copies, waits for them, and re-layouts: none -> 13.4 us  [the longest x1 8.13 us: body(): both_grad[:, window:]]
    dot_general x10 -> x13, matrix products: 69.2 us -> 61.1 us  [t_dot(): lax.dot_general(left, right, (((0,), (0,)), ((), ())), preferred_element_...]
  transfers between devices with their start and end apart: 8 -> 8, of which waited for: 0 -> 0; matrix products, arithmetic and copies ran while one was open for 34% -> 14% of each run, Pallas kernels for 62% -> 44%
where the time goes in v1:
time: 1140 us; the launch traced here: 1130 us
  Pallas kernels  834 us (73%)
  matrix products  113 us (10%)
  local copies, waits for them, and re-layouts  101 us (9%)
  other arithmetic  65.6 us (6%)
  starting transfers between devices  18 us (2%)
    pallas_call x6, Pallas kernels, together(): pl.pallas_call(kernel, out_shape=[shape for part in parts for shape in pa...  834 us
    dot_general x13, matrix products, t_dot(): lax.dot_general(left, right, (((0,), (0,)), ((), ())), preferred_element_...  61.1 us
    dot_general x2, local copies, waits for them, and re-layouts, dot(): return jnp.dot(left, right, preferred_element_type=F32)  23.3 us
  transfers between devices with their start and end apart: 8, of which 0 were waited for; matrix products, arithmetic and copies ran while one was open for 14% of the time, Pallas kernels for 44%

profile of v1, /device:TPU:16, one launch (start us, length us, event | category | flops | bytes accessed | tf_op | source)
XLA Modules:
  0.0 1133.8 jit_solution(16437445331555501145)
XLA Ops:
  9.0 6.3 all-to-all-start
  25.3 222.4 %gather_all.1 = (bf16[32,64,3072]{2,1,0:T(8,128)(2,1)}, bf16[32,64,576]{2,1,0:T(8,128)(2,1)}, bf16[32,16,4096]{2,1,0:T(8,128)(2,1)}, bf16[32,64,2048]{2,1,0:T(8,128)(2,1)}, bf16[32,16,128]{2,1,0:T(8,128)(2,1)}) custom-call(bf16[64,3072]{1,0:T(8,128)(2,1)} %refs_0_.1, bf16[64,576]{1,0:T(8,128)(2,1)} %refs_1_.1, bf16[16,4096]{1,0:T(8,128)(2,1)} %refs_2_.1, ...), custom_call_target="tpu_custom_call" | custom-call | tf_op jit(solution)/shard_map/gather_all/pallas_call | solution.py:511
  249.7 2.8 fusion.53
  254.8 16.9 %copy.153 = bf16[3072,2048]{1,0:T(8,128)(2,1)} copy(bf16[3072,2048]{0,1:T(8,128)(2,1)} %bitcast.217) | data formatting | bytes 25165824 | tf_op jit(solution)/shard_map/dot_general | solution.py:870
  271.7 9.0 fusion.26
  283.2 6.4 copy.152
  289.6 3.7 convolution_convert_fusion.5
  298.3 5.0 multiply_reduce_fusion.3
  307.6 80.4 %gather_first.1 = (bf16[32,64,2048]{2,1,0:T(8,128)(2,1)}, bf16[32,64,2048]{2,1,0:T(8,128)(2,1)}, f32[32,16,64]{2,1,0:T(8,128)}) custom-call(bf16[64,2048]{1,0:T(8,128)(2,1)} %get-tuple-element.205.refs_0_, bf16[64,2048]{1,0:T(8,128)(2,1)} %get-tuple-element.203.refs_1_, f32[16,64]{1,0:T(8,128)} %get-tuple-element.215.refs_2_), custom_call_target="tpu_custom_call" | custom-call | tf_op jit(solution)/shard_map/gather_first/pallas_call | solution.py:511
  398.3 2.8 bitcast_select_fusion.3
  406.8 3.3 maximum_select_fusion.1
  410.1 123.9 %gather_second_experts_first.1 = (bf16[32,64,2048]{2,1,0:T(8,128)(2,1)}, bf16[32,64,2048]{2,1,0:T(8,128)(2,1)}, f32[32,16,64]{2,1,0:T(8,128)}, bf16[2048,2048]{1...) custom-call(bf16[64,2048]{1,0:T(8,128)(2,1)} %get-tuple-element.206., ...), custom_call_target="tpu_custom_call" | custom-call | tf_op jit(solution)/shard_map/gather_second_experts_first/pallas_call | solution.py:511
  537.8 122.6 %scatter_first_experts_second.1 = (f32[64,2048]{1,0:T(8,128)}, f32[16,64]{1,0:T(8,128)}, f32[64,2048]{1,0:T(8,128)}, bf16[2048,2048]{1,0:T(8,128)(2,1)}, bf16[20...) custom-call(bf16[32,64,2048]{2,1,0:T(8,128)(2,1)} %bitcast.250, ...), custom_call_target="tpu_custom_call" | custom-call | tf_op jit(solution)/shard_map/scatter_first_experts_second/pallas_call | solution.py:511
  662.6 90.4 %scatter_second.1 = (f32[64,2048]{1,0:T(8,128)}, f32[16,64]{1,0:T(8,128)}, f32[64,2048]{1,0:T(8,128)}) custom-call(bf16[32,64,2048]{2,1,0:T(8,128)(2,1)} %bitcast.244, f32[32,16,64]{2,1,0:T(8,128)} %broadcast_select_fusion.refs_1_, bf16[32,64,2048]{2,1,0:T(8,128)(2,1)} %bitcast.245), custom_call_target="tpu_custom_call" | custom-call | tf_op jit(solution)/shard_map/scatter_second/pallas_call | solution.py:511
  761.0 6.7 fusion.6
  768.6 3.1 convolution_bitcast_fusion
  777.9 5.7 convolution_convert_fusion.1
  800.9 3.3 convolution_convert_fusion.2
  808.5 6.5 convolution_convert_fusion
  815.0 9.0 fusion.55
  828.2 4.6 all-to-all-start.1
  835.0 5.5 fusion.61
  840.5 3.5 convolution_add_fusion.1
  849.5 9.6 fusion.60
  859.1 12.9 %convolution_add_fusion = f32[2048,1536]{1,0:T(8,128)} fusion(f32[2048,1536]{1,0:T(8,128)} %fusion.60, bf16[1024,2048]{1,0:T(8,128)(2,1)S(1)} %copy-done.89, bf16[1024,1536]{1,0:T(8,128)(2,1)S(1)} %copy-done.91), kind=kOutput, calls=%fused_computation.2 | convolution fusion | flops 6445596672 | bytes 32505856 | tf_op jit(solution)/shard_map/dot_general | solution.py:878
  872.0 8.1 fusion.48
  880.2 5.6 dynamic-slice_convert_fusion.1
  891.0 4.3 copy.168
  895.3 194.4 %sum_scattered.1 = (f32[64,3072]{1,0:T(8,128)}, f32[64,576]{1,0:T(8,128)}, f32[16,4096]{1,0:T(8,128)}, f32[64,2048]{1,0:T(8,128)}, f32[16,128]{1,0:T(8,128)}) custom-call(bf16[32,64,3072]{2,1,0:T(8,128)(2,1)} %bitcast.205, bf16[32,64,576]{2,1,0:T(8,128)(2,1)} %bitcast.233, bf16[32,16,4096]{2,1,0:T(8,128)(2,1)} %bitcast.226, bf16[32,64,2048]{2,1,0:T(8,128)(2,1)} %bitcast.216, ...), custom_call_target="tpu_custom_call" | custom-call | tf_op jit(solution)/shard_map/sum_scattered/pallas_call | solution.py:511
  1115.4 5.3 maximum_bitcast_fusion.2
  1122.9 2.9 maximum_bitcast_fusion.1
  1127.6 2.9 maximum_bitcast_fusion
  (385 shorter events, 141.8 us)
Async XLA Ops:
  3.9 11.5 %copy-start.19 = (bf16[1,1408,1024]{2,1,0:T(8,128)(2,1)S(1)}, bf16[1,1408,1024]{2,1,0:T(8,128)(2,1)}, u32[]{:S(2)}) copy-start(bf16[1,1408,1024]{2,1,0:T(8,128)(2,1)} %param.35) | copy-start | bytes 8650756
  9.0 383.0 %all-to-all-start = ((bf16[32,64,176]{2,1,0:T(8,128)(2,1)}), bf16[32,64,176]{2,1,0:T(8,128)(2,1)}, u32[]{:S(2)}, u32[]{:S(2)}) async-start(bf16[32,64,176]{2,1,0:T(8,128)(2,1)} %maximum_bitcast_fusion.3), calls=%async_computation | async-start | bytes 2097152 | tf_op jit(solution)/shard_map/all_to_all | solution.py:1072
  17.0 7.6 copy-start.87
  17.0 231.9 %copy-start.5 = (bf16[2,1,64,2048]{3,2,1,0:T(8,128)(2,1)S(1)}, bf16[2,1,64,2048]{3,2,1,0:T(8,128)(2,1)}, u32[]{:S(2)}) copy-start(bf16[2,1,64,2048]{3,2,1,0:T(8,128)(2,1)} %param.18) | copy-start | bytes 1572868
  17.0 378.8 %collective-permute-start.2 = (bf16[768,1024]{1,0:T(8,128)(2,1)}, bf16[768,1024]{1,0:T(8,128)(2,1)}, u32[]{:S(2)}, u32[]{:S(2)}) collective-permute-start(bf16[768,1024]{1,0:T(8,128)(2,1)} %dynamic-slice_bitcast_fusion), channel_id=1, source_target_pairs={{0,16},{16,0},{1,17},{17,1},{2,18},{18,2},{3,19},{19,3},{4,20},{20... | collective-permute-start | bytes 4718600 | tf_op jit(solution)/shard_map/ppermute | solution.py:907
  20.4 377.9 %collective-permute-start.1 = (bf16[1024,768]{1,0:T(8,128)(2,1)}, bf16[1024,768]{1,0:T(8,128)(2,1)}, u32[]{:S(2)}, u32[]{:S(2)}) collective-permute-start(bf16[1024,768]{1,0:T(8,128)(2,1)} %dynamic-slice_bitcast_fusion.1), channel_id=1, source_target_pairs={{0,16},{16,0},{1,17},{17,1},{2,18},{18,2},{3,19},{19,3},{4,20},{20... | collective-permute-start | bytes 4718600 | tf_op jit(solution)/shard_map/ppermute | solution.py:907
  23.0 380.3 %collective-permute-start = (bf16[1024,768]{1,0:T(8,128)(2,1)}, bf16[1024,768]{1,0:T(8,128)(2,1)}, u32[]{:S(2)}, u32[]{:S(2)}) collective-permute-start(bf16[1024,768]{1,0:T(8,128)(2,1)} %dynamic-slice_bitcast_fusion.2), channel_id=1, source_target_pairs={{0,16},{16,0},{1,17},{17,1},{2,18},{18,2},{3,19},{19,3},{4,20},{20... | collective-permute-start | bytes 4718600 | tf_op jit(solution)/shard_map/ppermute | solution.py:907
  249.3 22.4 %copy-start.9 = (bf16[2,1,64,2048]{3,2,1,0:T(8,128)(2,1)}, bf16[2,1,64,2048]{3,2,1,0:T(8,128)(2,1)S(1)}, u32[]{:S(2)}) copy-start(bf16[2,1,64,2048]{3,2,1,0:T(8,128)(2,1)S(1)} %fusion.20) | copy-start | bytes 1572868
  253.5 29.3 %copy-start.53 = (f32[64,32]{1,0:T(8,128)}, f32[64,32]{1,0:T(8,128)S(1)}, u32[]{:S(2)}) copy-start(f32[64,32]{1,0:T(8,128)S(1)} %get-tuple-element.220) | copy-start | bytes 24580
  253.6 29.3 %copy-start.71 = (f32[512]{0:T(512)}, f32[512]{0:T(512)S(1)}, u32[]{:S(2)}) copy-start(f32[512]{0:T(512)S(1)} %reshape.517) | copy-start | bytes 6148
  254.7 49.7 %copy-start.14 = (bf16[2048,16]{1,0:T(8,128)(2,1)}, bf16[2048,16]{1,0:T(8,128)(2,1)S(1)}, u32[]{:S(2)}) copy-start(bf16[2048,16]{1,0:T(8,128)(2,1)S(1)} %reshape_reshape.6) | copy-start | bytes 196612
  254.7 28.2 %copy-start.75 = (f32[128]{0:T(128)}, f32[128]{0:T(128)S(1)}, u32[]{:S(2)}) copy-start(f32[128]{0:T(128)S(1)} %add_rsqrt_fusion.2) | copy-start | bytes 1540
  282.8 11.0 copy-start.38
  761.0 16.9 %copy-start.2 = (f32[128,2048]{1,0:T(8,128)}, f32[128,2048]{1,0:T(8,128)S(1)}, u32[]{:S(2)}) copy-start(f32[128,2048]{1,0:T(8,128)S(1)} %get-tuple-element.200) | copy-start | bytes 3145732
  777.9 8.0 slice-start.2
  815.0 9.0 copy-start.51
  815.0 9.2 copy-start.7
  815.0 9.2 copy-start.63
  815.0 9.2 copy-start.84
  826.7 8.3 copy-start.45
  828.2 266.5 %all-to-all-start.1 = ((bf16[32,64,176]{2,1,0:T(8,128)(2,1)}), bf16[32,64,176]{2,1,0:T(8,128)(2,1)}, u32[]{:S(2)}, u32[]{:S(2)}) async-start(bf16[32,64,176]{2,1,0:T(8,128)(2,1)} %pad_maximum_fusion.3), calls=%async_computation.1 | async-start | bytes 2097152 | tf_op jit(solution)/shard_map/all_to_all | solution.py:1257
  840.5 9.0 copy-start.88
  848.0 255.0 %collective-permute-start.5 = (bf16[768,1024]{1,0:T(8,128)(2,1)}, bf16[768,1024]{1,0:T(8,128)(2,1)}, u32[]{:S(2)}, u32[]{:S(2)}) collective-permute-start(bf16[768,1024]{1,0:T(8,128)(2,1)} %dynamic-slice_convert_fusion), channel_id=1, source_target_pairs={{0,16},{16,0},{1,17},{17,1},{2,18},{18,2},{3,19},{19,3},{4,20},{20... | collective-permute-start | bytes 4718600 | tf_op jit(solution)/shard_map/ppermute | solution.py:907
  849.5 9.6 copy-start.89
  849.5 9.6 copy-start.91
  880.2 8.9 copy-start.25
  880.2 8.9 copy-start.26
  887.1 224.4 %collective-permute-start.3 = (bf16[1024,768]{1,0:T(8,128)(2,1)}, bf16[1024,768]{1,0:T(8,128)(2,1)}, u32[]{:S(2)}, u32[]{:S(2)}) collective-permute-start(bf16[1024,768]{1,0:T(8,128)(2,1)} %dynamic-slice_convert_fusion.2), channel_id=1, source_target_pairs={{0,16},{16,0},{1,17},{17,1},{2,18},{18,2},{3,19},{19,3},{4,20},{20... | collective-permute-start | bytes 4718600 | tf_op jit(solution)/shard_map/ppermute | solution.py:907
  888.1 216.9 %collective-permute-start.4 = (bf16[1024,768]{1,0:T(8,128)(2,1)}, bf16[1024,768]{1,0:T(8,128)(2,1)}, u32[]{:S(2)}, u32[]{:S(2)}) collective-permute-start(bf16[1024,768]{1,0:T(8,128)(2,1)} %dynamic-slice_convert_fusion.1), channel_id=1, source_target_pairs={{0,16},{16,0},{1,17},{17,1},{2,18},{18,2},{3,19},{19,3},{4,20},{20... | collective-permute-start | bytes 4718600 | tf_op jit(solution)/shard_map/ppermute | solution.py:907
  895.3 195.6 %copy-start.3 = (f32[128,2048]{1,0:T(8,128)S(1)}, f32[128,2048]{1,0:T(8,128)}, u32[]{:S(2)}) copy-start(f32[128,2048]{1,0:T(8,128)} %copy-done.2) | copy-start | bytes 3145732
  895.3 195.6 %copy-start.6 = (bf16[2,1,64,2048]{3,2,1,0:T(8,128)(2,1)S(1)}, bf16[2,1,64,2048]{3,2,1,0:T(8,128)(2,1)}, u32[]{:S(2)}) copy-start(bf16[2,1,64,2048]{3,2,1,0:T(8,128)(2,1)} %param.18) | copy-start | bytes 1572868
  1099.6 7.8 slice-start.4
  (84 other events, 320.4 us)

commit v2 on v1

--- a/solution.py
+++ b/solution.py
@@ -2,6 +2,7 @@
 
 import jax
 import jax.numpy as jnp
+import numpy as np
 from jax import lax
 from jax.experimental import pallas as pl
 from jax.experimental.pallas import tpu as pltpu
@@ -542,11 +543,19 @@
     return wrap
 
 
+def window_start(peer, peers, window, eff):
+    return pl.multiple_of(peer * window - lax.div(peer, peers - 1) * (peers * window - eff), 128)
+
+
 class Experts:
-    def __init__(self, hidden, grad, share, weights, capacity):
-        gate, up, down, shared_in, shared_down = weights
+    def __init__(self, grid, hidden, grad, share, weights, capacity):
+        own, got, shared_in, shared_down = weights
+        self.grid = grid
+        self.peers = grid.size["p"]
+        self.eff = own[0].shape[1]
+        self.extent = own[0].shape[0]
         count = hidden.shape[0]
-        window = gate.shape[1]
+        window = got[0].shape[2]
         self.supers = count // (2 * GROUP)
         self.slots = GROUP // SEQ * capacity
         self.capacity = capacity
@@ -554,10 +563,10 @@
         rows = 2 * self.slots
         total = self.supers * rows
         groups = count // GROUP
-        self.inputs = [hidden, grad, share, gate, up, down, shared_in, shared_down]
+        self.inputs = [hidden, grad, share, *own, *got, shared_in, shared_down]
         hbm = pl.BlockSpec(memory_space=pl.ANY)
         vmem = pl.BlockSpec(memory_space=pltpu.VMEM)
-        self.in_specs = [hbm, hbm] + [vmem] * 6
+        self.in_specs = [hbm, hbm, vmem] + [hbm] * 6 + [vmem] * 2
         shared_width = shared_in.shape[1]
         kept = [(rows, D), (rows, D), (rows, 2 * window), (rows, window)]
         kept += [(2 * GROUP, shared_width), (2 * GROUP, shared_width // 2)]
@@ -583,11 +592,17 @@
                 pltpu.SemaphoreType.DMA((2,)),
                 pltpu.SemaphoreType.DMA((len(kept), 2)),
                 pltpu.SemaphoreType.DMA((2, 2)),
+                pltpu.VMEM((D, window), BF),
+                pltpu.VMEM((D, window), BF),
+                pltpu.VMEM((window, D), BF),
+                pltpu.SemaphoreType.DMA((3, self.peers)),
             ]
         )
 
     def steps(self, at, ins, outs, scratch):
-        hidden, grad, share, gate, up, down, shared_in, shared_down = ins
+        hidden, grad, share = ins[:3]
+        own, got = ins[3:6], ins[6:9]
+        shared_in, shared_down = ins[9:]
         hidden_out, out_out, gate_grad = outs[:3]
         kept_out = outs[3:]
         hidden_in, grad_in = scratch[:2]
@@ -596,7 +611,7 @@
         a_pre, b_pre, flow = scratch[10:13]
         row_grad, expert_out = scratch[13:15]
         keys, picks, picks_t, share_rows, gate_rows, shared_pre = scratch[15:21]
-        load_sem, keep_sem, part_sem = scratch[21:]
+        load_sem, keep_sem, part_sem, gate, up, down, weight_sem = scratch[21:]
         slots, window, supers = self.slots, self.window, self.supers
         rows = 2 * slots
         half = shared_in.shape[1] // 2
@@ -622,7 +637,25 @@
             piece = pl.ds((2 * k + j) * GROUP, GROUP)
             return pltpu.make_async_copy(parts[n].at[j], target.at[piece, :], part_sem.at[n, j])
 
+        me, peers, extent = at["p"], self.peers, self.extent
+        first = window_start(me, peers, window, self.eff)
+        weight_copies = []
+        for n, weight in enumerate((gate, up, down)):
+            for step in range(peers):
+                peer = lax.rem(me + peers - step, peers)
+                share_of_d = pl.ds(pl.multiple_of(peer * extent, extent), extent)
+                target = weight.at[:, share_of_d] if n == 2 else weight.at[share_of_d, :]
+                if step:
+                    source = got[n].at[step - 1]
+                else:
+                    units = pl.ds(first, window)
+                    source = own[n].at[units, :] if n == 2 else own[n].at[:, units]
+                weight_copies.append(
+                    pltpu.make_async_copy(source, target, weight_sem.at[n, step])
+                )
         for copy in load(0):
+            copy.start()
+        for copy in weight_copies:
             copy.start()
         row_of = lax.broadcasted_iota(jnp.int32, (GROUP, GROUP), 0)
         column_of = lax.broadcasted_iota(jnp.int32, (GROUP, GROUP), 1)
@@ -632,6 +665,16 @@
         place = jnp.dot(chosen.astype(BF), earlier, preferred_element_type=F32)
         sequence = lax.div(lax.broadcasted_iota(jnp.int32, place.shape, 1), SEQ).astype(F32)
         keys[...] = jnp.where(chosen > 0, place + sequence * self.capacity, -1.0)
+        for copy in weight_copies:
+            copy.wait()
+        twice = peers * window - self.eff
+        if twice:
+
+            @pl.when(me == peers - 1)
+            def _():
+                gate[:, pl.ds(0, twice)] = jnp.zeros((D, twice), BF)
+                up[:, pl.ds(0, twice)] = jnp.zeros((D, twice), BF)
+                down[pl.ds(0, twice), :] = jnp.zeros((twice, D), BF)
 
         for k in range(supers):
             slot = k % 2
@@ -795,75 +838,606 @@
                 put(n, supers - 1, j).wait()
 
 
+class Exchange:
+    def __init__(self, grid, arrays, views, shapes):
+        self.grid, self.views = grid, views
+        self.peers = grid.size["p"]
+        self.inputs = list(arrays)
+        hbm = pl.BlockSpec(memory_space=pl.ANY)
+        self.in_specs = [hbm] * len(arrays)
+        self.out_shapes = [
+            jax.ShapeDtypeStruct((self.peers - 1,) + shape, a.dtype)
+            for a, shape in zip(arrays, shapes)
+        ]
+        self.out_specs = [hbm] * len(arrays)
+        self.scratch = [pltpu.SemaphoreType.DMA((len(arrays), self.peers - 1))] * 2
+
+    def steps(self, at, ins, outs, scratch):
+        send_sem, recv_sem = scratch
+        yield 1
+        copies = []
+        for n, view in enumerate(self.views):
+            for step in range(1, self.peers):
+                there = self.grid.shift(at, {"p": step})
+                copy = pltpu.make_async_remote_copy(
+                    src_ref=view(ins[n], there["p"], step),
+                    dst_ref=outs[n].at[step - 1],
+                    send_sem=send_sem.at[n, step - 1],
+                    recv_sem=recv_sem.at[n, step - 1],
+                    device_id=self.grid.mesh_id(there),
+                    device_id_type=MESH_ID,
+                )
+                copy.start()
+                copies.append(copy)
+        yield
+        for copy in copies:
+            copy.wait()
+
+
+SCALE = (NOPE + ROPE) ** (-0.5)
+HALF = ROPE // 2
+TURN = HEADS * HALF
+WIDE = HEADS * NOPE
+
+
+def spread():
+    row = lax.broadcasted_iota(jnp.int32, (128, TURN), 0)
+    lane = lax.broadcasted_iota(jnp.int32, (128, TURN), 1)
+    return (lax.rem(lane, HALF) == row).astype(BF)
+
+
+def of_head(h):
+    lane = lax.broadcasted_iota(jnp.int32, (MICRO * SEQ, 2 * TURN), 1)
+    return jnp.bitwise_and(jnp.right_shift(lane, 5), HEADS - 1) == h
+
+
+def rms_scale(values):
+    return lax.rsqrt(jnp.mean(values * values, -1, keepdims=True) + EPSILON)
+
+
+class AttentionForward:
+    def __init__(self, tokens, routes, allowed, tables, gains, weights, experts):
+        count = MICRO * SEQ
+        self.experts = experts
+        self.inputs = [tokens, routes, allowed, *tables, *gains, *weights]
+        vmem = pl.BlockSpec(memory_space=pltpu.VMEM)
+        hbm = pl.BlockSpec(memory_space=pl.ANY)
+        self.in_specs = [vmem] * 8 + [hbm] * 5
+        shapes = [
+            ((count, D), BF), ((experts, count), F32),
+            ((count, D), BF), ((count, WIDE), BF), ((count, 2 * TURN), BF), ((count, RANK), F32),
+            ((count, RANK), BF), ((count, 2 * TURN), BF), ((count, 2 * WIDE), BF),
+            ((HEADS, count, count), F32), ((count, WIDE), BF), ((count, D), F32),
+        ]
+        self.out_shapes = [jax.ShapeDtypeStruct(shape, kind) for shape, kind in shapes]
+        self.out_specs = [vmem] * len(shapes)
+        self.scratch = [pltpu.VMEM(w.shape, BF) for w in weights] + [
+            pltpu.VMEM((count, RANK + 256), F32),
+            pltpu.VMEM((count, 2 * TURN), F32),
+            pltpu.SemaphoreType.DMA((5,)),
+        ]
+
+    def steps(self, at, ins, outs, scratch):
+        tokens, routes, allowed, cosine, sine, attn_gain, kv_gain, ffn_gain = ins[:8]
+        (
+            hidden, gates, normed, q_plain, q_turned, kv_low, latent, k_turned, kv, chances,
+            attended, residual,
+        ) = outs
+        q_weight, kv_down, kv_up, out_weight, router = scratch[:5]
+        kv_raw, q_raw, sem = scratch[5:]
+        yield 9
+        loads = [
+            pltpu.make_async_copy(ins[8 + n], scratch[n], sem.at[n]) for n in range(5)
+        ]
+        for n in (1, 0, 2, 3, 4):
+            loads[n].start()
+        values = tokens[...].astype(F32)
+        normed[...] = (values * rms_scale(values) * attn_gain[...]).astype(BF)
+        yield
+        loads[1].wait()
+
+        @tiles(RANK + 256, 256)
+        def _(columns):
+            kv_raw[:, columns] = dot(normed[...], kv_down[:, columns])
+
+        low = kv_raw[:, pl.ds(0, RANK)]
+        kv_low[...] = low
+        latent[...] = (low * rms_scale(low) * kv_gain[...]).astype(BF)
+        first, second = kv_raw[:, pl.ds(RANK, 128)], kv_raw[:, pl.ds(RANK + 128, 128)]
+        c, s = cosine[:, pl.ds(0, 128)], sine[:, pl.ds(0, 128)]
+        lay = spread()
+        k_turned[:, pl.ds(0, TURN)] = dot((first * c - second * s).astype(BF), lay).astype(BF)
+        k_turned[:, pl.ds(TURN, TURN)] = dot((second * c + first * s).astype(BF), lay).astype(BF)
+        yield
+        loads[0].wait()
+
+        @tiles(WIDE, 256)
+        def _(columns):
+            q_plain[:, columns] = dot(normed[...], q_weight[:, columns]).astype(BF)
+
+        yield
+        for n in range(4):
+            columns = pl.ds(n * 256, 256)
+            q_raw[:, columns] = dot(normed[...], q_weight[:, pl.ds(WIDE + n * 256, 256)])
+        first, second = q_raw[:, pl.ds(0, TURN)], q_raw[:, pl.ds(TURN, TURN)]
+        q_turned[:, pl.ds(0, TURN)] = (first * cosine[...] - second * sine[...]).astype(BF)
+        q_turned[:, pl.ds(TURN, TURN)] = (second * cosine[...] + first * sine[...]).astype(BF)
+        yield
+        loads[2].wait()
+
+        @tiles(2 * WIDE, 256)
+        def _(columns):
+            kv[:, columns] = dot(latent[...], kv_up[:, columns]).astype(BF)
+
+        yield
+
+        @pl.loop(0, HEADS)
+        def _(h):
+            plain = pl.ds(pl.multiple_of(h * NOPE, NOPE), NOPE)
+            keys = pl.ds(pl.multiple_of(h * 2 * NOPE, NOPE), NOPE)
+            both = pl.ds(pl.multiple_of(h * 2 * NOPE + NOPE, NOPE), VDIM)
+            turned = jnp.where(of_head(h), q_turned[...].astype(F32), 0.0).astype(BF)
+            scores = dot_t(q_plain[:, plain], kv[:, keys]) + dot_t(turned, k_turned[...])
+            scores = jnp.where(allowed[...] > 0, scores * SCALE, MASKED)
+            powers = jnp.exp(scores - jnp.max(scores, -1, keepdims=True))
+            chance = powers / jnp.sum(powers, -1, keepdims=True)
+            chances[h] = chance
+            attended[:, plain] = dot(chance.astype(BF), kv[:, both]).astype(BF)
+
+        yield
+        loads[3].wait()
+
+        @tiles(D, 256)
+        def _(columns):
+            residual[:, columns] = tokens[:, columns].astype(F32) + dot(
+                attended[...], out_weight[:, columns]
+            )
+
+        yield
+        values = residual[...]
+        hidden[...] = (values * rms_scale(values) * ffn_gain[...]).astype(BF)
+        loads[4].wait()
+        logits = dot(hidden[...], router[...])
+        lane = lax.broadcasted_iota(jnp.int32, logits.shape, 1)
+        chosen = lane < 0
+        for k in range(TOP):
+            chosen = jnp.logical_or(chosen, routes[:, pl.ds(k, 1)] == lane)
+        logits = jnp.where(chosen, logits, MASKED)
+        powers = jnp.where(chosen, jnp.exp(logits - jnp.max(logits, -1, keepdims=True)), 0.0)
+        share = powers / jnp.sum(powers, -1, keepdims=True)
+        gates[...] = jnp.where(chosen, share, -1.0).T[: self.experts]
+        yield
+
+
+class AttentionBackward:
+    def __init__(self, cotangent, hidden_sum, gate_grad, saved, tokens, tables, gains, weights):
+        count = MICRO * SEQ
+        self.experts = gate_grad.shape[0]
+        self.inputs = [cotangent, hidden_sum, gate_grad, *tables, *gains, *saved, tokens, *weights]
+        vmem = pl.BlockSpec(memory_space=pltpu.VMEM)
+        hbm = pl.BlockSpec(memory_space=pl.ANY)
+        self.in_specs = [vmem] * (8 + 12 + 1) + [hbm] * 5
+        self.grads = [(WIDE, D), (RANK, 2 * WIDE), (D, WIDE + 2 * TURN), (D, RANK + 256)]
+        self.out_shapes = [jax.ShapeDtypeStruct(shape, BF) for shape in self.grads] + [
+            jax.ShapeDtypeStruct((count, D), BF),
+            jax.ShapeDtypeStruct((1, D), F32),
+            jax.ShapeDtypeStruct((1, RANK), F32),
+            jax.ShapeDtypeStruct((1, D), F32),
+            jax.ShapeDtypeStruct((D, 128), F32),
+        ]
+        self.out_specs = [hbm] * 4 + [vmem] * 5
+        self.scratch = [pltpu.VMEM(w.shape, BF) for w in weights] + [
+            pltpu.VMEM((2, 256, 2 * WIDE), BF),
+            pltpu.VMEM((count, 128), F32),
+            pltpu.VMEM((count, D), F32),
+            pltpu.VMEM((count, D), F32),
+            pltpu.VMEM((count, D), BF),
+            pltpu.VMEM((count, WIDE), BF),
+            pltpu.VMEM((count, WIDE + 2 * TURN), BF),
+            pltpu.VMEM((count, 2 * WIDE), BF),
+            pltpu.VMEM((count, RANK + 256), BF),
+            pltpu.VMEM((count, 2 * TURN), F32),
+            pltpu.VMEM((count, 2 * TURN), F32),
+            pltpu.SemaphoreType.DMA((5,)),
+            pltpu.SemaphoreType.DMA((2,)),
+        ]
+
+    def steps(self, at, ins, outs, scratch):
+        cotangent, hidden_sum, gate_grad, cosine, sine, attn_gain, kv_gain, ffn_gain = ins[:8]
+        (
+            hidden, gates, normed, q_plain, q_turned, kv_low, latent, k_turned, kv, chances,
+            attended, residual,
+        ) = ins[8:20]
+        tokens_grad, attn_gain_grad, kv_gain_grad, ffn_gain_grad, router_grad = outs[4:]
+        q_weight, kv_down, kv_up, out_weight, router = scratch[:5]
+        (
+            buffers, turned_gates, hidden_grad, residual_grad, mixed, attended_grad, q_grad, kv_grad,
+            kv_raw_grad, q_turn_grad, k_turn_grad, sem, out_sem,
+        ) = scratch[5:]
+        experts = self.experts
+        yield 4 + sum(shape[0] // 256 for shape in self.grads)
+        loads = [
+            pltpu.make_async_copy(ins[21 + n], scratch[n], sem.at[n]) for n in range(5)
+        ]
+        for n in (4, 3, 2, 0, 1):
+            loads[n].start()
+        share = jnp.maximum(gates[...], 0.0)
+        inner = jnp.sum(share * gate_grad[...], 0, keepdims=True)
+        turned_gates[...] = jnp.zeros_like(turned_gates)
+        turned_gates[pl.ds(0, experts), :] = share * (gate_grad[...] - inner)
+        logit_grad = turned_gates[...].T.astype(BF)
+        loads[4].wait()
+
+        @tiles(D, 256)
+        def _(columns):
+            router_grad[columns, :] = t_dot(hidden[:, columns], logit_grad)
+            hidden_grad[:, columns] = hidden_sum[:, columns] + dot_t(
+                logit_grad, router[columns, :]
+            )
+
+        def norm_back(values, gain, gradient):
+            scale = rms_scale(values)
+            weighted = gradient * gain
+            mean = jnp.mean(weighted * values, -1, keepdims=True)
+            gain_grad = jnp.sum(gradient * values * scale, 0, keepdims=True)
+            return scale * weighted - values * (scale * scale * scale * mean), gain_grad
+
+        part, ffn_gain_grad[...] = norm_back(residual[...], ffn_gain[...], hidden_grad[...])
+        total = cotangent[...].astype(F32) + part
+        residual_grad[...] = total
+        mixed[...] = total.astype(BF)
+        yield
+        loads[3].wait()
+
+        @tiles(WIDE, 256)
+        def _(columns):
+            attended_grad[:, columns] = dot_t(mixed[...], out_weight[columns, :]).astype(BF)
+
+        yield
+        turn = [0]
+        stores = {}
+
+        def weight_grad(n, left, right):
+            rows, width = self.grads[n]
+            for k in range(rows // 256):
+                slot = turn[0] % 2
+                turn[0] += 1
+                if slot in stores:
+                    stores[slot].wait()
+                piece = pl.ds(k * 256, 256)
+
+                @tiles(width, 256)
+                def _(columns):
+                    buffers[slot, :, columns] = t_dot(left[:, piece], right[:, columns]).astype(BF)
+
+                stores[slot] = pltpu.make_async_copy(
+                    buffers.at[slot, :, pl.ds(0, width)], outs[n].at[piece, :], out_sem.at[slot]
+                )
+                stores[slot].start()
+                yield
+
+        yield from weight_grad(0, attended, mixed)
+        q_turn_grad[...] = jnp.zeros_like(q_turn_grad)
+        k_turn_grad[...] = jnp.zeros_like(k_turn_grad)
+
+        @pl.loop(0, HEADS)
+        def _(h):
+            plain = pl.ds(pl.multiple_of(h * NOPE, NOPE), NOPE)
+            keys = pl.ds(pl.multiple_of(h * 2 * NOPE, NOPE), NOPE)
+            both = pl.ds(pl.multiple_of(h * 2 * NOPE + NOPE, NOPE), VDIM)
+            chance = chances[h]
+            grads = attended_grad[:, plain]
+            kv_grad[:, both] = t_dot(chance.astype(BF), grads).astype(BF)
+            chance_grad = dot_t(grads, kv[:, both])
+            mean = jnp.sum(chance * chance_grad, -1, keepdims=True)
+            score_grad = (chance * (chance_grad - mean)).astype(BF)
+            q_grad[:, plain] = (dot(score_grad, kv[:, keys]) * SCALE).astype(BF)
+            kv_grad[:, keys] = (t_dot(score_grad, q_plain[:, plain]) * SCALE).astype(BF)
+            mine = of_head(h)
+            turned = jnp.where(mine, q_turned[...].astype(F32), 0.0).astype(BF)
+            q_turn_grad[...] += jnp.where(mine, dot(score_grad, k_turned[...]), 0.0) * SCALE
+            k_turn_grad[...] += t_dot(score_grad, turned) * SCALE
+
+        yield
+        first, second = q_turn_grad[:, pl.ds(0, TURN)], q_turn_grad[:, pl.ds(TURN, TURN)]
+        c, s = cosine[...], sine[...]
+        q_grad[:, pl.ds(WIDE, TURN)] = (first * c + second * s).astype(BF)
+        q_grad[:, pl.ds(WIDE + TURN, TURN)] = (second * c - first * s).astype(BF)
+        lay = spread()
+
+        def gathered(columns):
+            values = k_turn_grad[:, columns]
+            high = values.astype(BF)
+            low = (values - high.astype(F32)).astype(BF)
+            return dot_t(high, lay) + dot_t(low, lay)
+
+        first, second = gathered(pl.ds(0, TURN)), gathered(pl.ds(TURN, TURN))
+        c, s = cosine[:, pl.ds(0, 128)], sine[:, pl.ds(0, 128)]
+        kv_raw_grad[:, pl.ds(RANK, 128)] = (first * c + second * s).astype(BF)
+        kv_raw_grad[:, pl.ds(RANK + 128, 128)] = (second * c - first * s).astype(BF)
+        loads[2].wait()
+        latent_grad = dot_t(kv_grad[...], kv_up[...])
+        part, kv_gain_grad[...] = norm_back(kv_low[...], kv_gain[...], latent_grad)
+        kv_raw_grad[:, pl.ds(0, RANK)] = part.astype(BF)
+        yield from weight_grad(1, latent, kv_grad)
+        yield from weight_grad(2, normed, q_grad)
+        yield from weight_grad(3, normed, kv_raw_grad)
+        loads[0].wait()
+        loads[1].wait()
+
+        @tiles(D, 256)
+        def _(columns):
+            hidden_grad[:, columns] = dot_t(q_grad[...], q_weight[columns, :]) + dot_t(
+                kv_raw_grad[...], kv_down[columns, :]
+            )
+
+        part, attn_gain_grad[...] = norm_back(
+            ins[20][...].astype(F32), attn_gain[...], hidden_grad[...]
+        )
+        tokens_grad[...] = (residual_grad[...] + part).astype(BF)
+        yield
+        for store in stores.values():
+            store.wait()
+
+
+class WeightGrads:
+    TILE = 256
+
+    def __init__(self, grid, kept, extent):
+        self.grid, self.extent, self.chunks = grid, extent, len(kept)
+        self.inputs = [array for entry in kept for array in entry]
+        rows, grad_rows, ab_grad, scaled, shared_grad, shared_inner, hidden, grad = kept[0]
+        self.window = scaled.shape[1]
+        hbm = pl.BlockSpec(memory_space=pl.ANY)
+        self.in_specs = [hbm] * len(self.inputs)
+        peers = grid.size["p"]
+        window, tile = self.window, self.TILE
+        self.out_shapes = [
+            jax.ShapeDtypeStruct((extent, 2 * window), F32),
+            jax.ShapeDtypeStruct((window, extent), F32),
+            jax.ShapeDtypeStruct((peers - 1, extent, 2 * window), BF),
+            jax.ShapeDtypeStruct((peers - 1, window, extent), BF),
+            jax.ShapeDtypeStruct((D, shared_grad.shape[1]), BF),
+            jax.ShapeDtypeStruct((shared_inner.shape[1], D), F32),
+        ]
+        self.out_specs = [hbm] * 6
+        self.jobs = [(0, 2, True), (1, 3, False), (6, 4, True), (7, 5, False)]
+        self.scratch = []
+        for streamed, resident, left in self.jobs:
+            a, b = kept[0][streamed], kept[0][resident]
+            self.scratch.append(pltpu.VMEM((self.chunks,) + b.shape, BF))
+            self.scratch.append(pltpu.VMEM((2, self.chunks, a.shape[0], tile), BF))
+            shape = (tile, b.shape[1]) if left else (b.shape[1], tile)
+            self.scratch.append(pltpu.VMEM((2,) + shape, F32))
+            self.scratch.append(pltpu.VMEM((2,) + shape, BF))
+        self.scratch += [
+            pltpu.SemaphoreType.DMA((4, self.chunks)),
+            pltpu.SemaphoreType.DMA((4, 2, self.chunks)),
+            pltpu.SemaphoreType.DMA((4, 2)),
+        ]
+
+    def steps(self, at, ins, outs, scratch):
+        tile, extent, chunks = self.TILE, self.extent, self.chunks
+        peers = self.grid.size["p"]
+        kept = [ins[c * 8 : (c + 1) * 8] for c in range(chunks)]
+        whole_sem, tile_sem, out_sem = scratch[16:]
+        own_ab, own_down, sent_ab, sent_down, shared_in, shared_down = outs
+
+        def whole(job, c):
+            return pltpu.make_async_copy(
+                kept[c][self.jobs[job][1]], scratch[4 * job].at[c], whole_sem.at[job, c]
+            )
+
+        work = []
+        per_peer = extent // tile
+        for step in range(peers):
+            for job in range(2):
+                for k in range(per_peer):
+                    piece = pl.ds(k * tile, tile)
+                    if step == 0:
+                        target = own_ab.at[piece, :] if job == 0 else own_down.at[:, piece]
+                    elif job == 0:
+                        target = sent_ab.at[step - 1, piece, :]
+                    else:
+                        target = sent_down.at[step - 1, :, piece]
+                    peer = self.grid.shift(at, {"p": step})["p"]
+                    first = pl.multiple_of(peer * extent + k * tile, tile)
+                    work.append((job, first, target, step == 0))
+        for k in range(D // tile):
+            piece = pl.ds(k * tile, tile)
+            work.append((2, k * tile, shared_in.at[piece, :], False))
+            work.append((3, k * tile, shared_down.at[:, piece], True))
+        work.sort(key=lambda entry: entry[0] >= 2)
+        turns = [0] * 4
+        numbered = []
+        for job, first, target, wide in work:
+            numbered.append((job, first, target, wide, turns[job]))
+            turns[job] += 1
+        yield len(work)
+
+        def fetch(number, c):
+            job, first, _, _, turn = numbered[number]
+            return pltpu.make_async_copy(
+                kept[c][self.jobs[job][0]].at[:, pl.ds(first, tile)],
+                scratch[4 * job + 1].at[turn % 2, c],
+                tile_sem.at[job, turn % 2, c],
+            )
+
+        def store(number):
+            job, _, target, wide, turn = numbered[number]
+            source = scratch[4 * job + (2 if wide else 3)].at[turn % 2]
+            return pltpu.make_async_copy(source, target, out_sem.at[job, turn % 2])
+
+        for c in range(chunks):
+            for job in range(2):
+                whole(job, c).start()
+            fetch(0, c).start()
+            for job in range(2, 4):
+                whole(job, c).start()
+        begun = set()
+        last = {}
+        for number, (job, _, _, wide, turn) in enumerate(numbered):
+            if number + 1 < len(numbered):
+                for c in range(chunks):
+                    fetch(number + 1, c).start()
+            if job not in begun:
+                begun.add(job)
+                for c in range(chunks):
+                    whole(job, c).wait()
+            for c in range(chunks):
+                fetch(number, c).wait()
+            if (job, turn % 2) in last:
+                store(last[job, turn % 2]).wait()
+            last[job, turn % 2] = number
+            resident, streamed = scratch[4 * job], scratch[4 * job + 1].at[turn % 2]
+            result = scratch[4 * job + (2 if wide else 3)].at[turn % 2]
+            left = self.jobs[job][2]
+
+            @tiles(resident.shape[2], 256)
+            def _(columns):
+                total = None
+                for c in range(chunks):
+                    if left:
+                        term = t_dot(streamed[c], resident[c, :, columns])
+                    else:
+                        term = t_dot(resident[c, :, columns], streamed[c])
+                    total = term if total is None else total + term
+                if left:
+                    result[:, columns] = total.astype(result.dtype)
+                else:
+                    result[columns, :] = total.astype(result.dtype)
+
+            store(number).start()
+            yield
+        for number in last.values():
+            store(number).wait()
+
+
+class Assemble:
+    TILE = 128
+
+    def __init__(self, grid, own_ab, own_down, got_ab, got_down, eff):
+        self.grid, self.eff = grid, eff
+        self.extent = own_ab.shape[0]
+        self.window = own_down.shape[0]
+        self.peers = 1 + len(got_ab)
+        self.inputs = [own_ab, own_down, *got_ab, *got_down]
+        hbm = pl.BlockSpec(memory_space=pl.ANY)
+        self.in_specs = [hbm] * len(self.inputs)
+        self.out_shapes = [
+            jax.ShapeDtypeStruct((self.extent, eff), F32),
+            jax.ShapeDtypeStruct((self.extent, eff), F32),
+            jax.ShapeDtypeStruct((eff, self.extent), F32),
+        ]
+        self.out_specs = [hbm] * 3
+        tile, window = self.TILE, self.window
+        self.scratch = [
+            pltpu.VMEM((2, tile, 2 * window), F32),
+            pltpu.VMEM((2, window, tile), F32),
+            pltpu.VMEM((2, self.peers - 1, tile, 2 * window), BF),
+            pltpu.VMEM((2, self.peers - 1, window, tile), BF),
+            pltpu.VMEM((2, 2, tile, eff), F32),
+            pltpu.VMEM((2, eff, tile), F32),
+            pltpu.SemaphoreType.DMA((2, 2, self.peers)),
+            pltpu.SemaphoreType.DMA((2, 3)),
+        ]
+
+    def steps(self, at, ins, outs, scratch):
+        tile, window, peers, eff = self.TILE, self.window, self.peers, self.eff
+        own = ins[:2]
+        got = (ins[2 : 1 + peers], ins[1 + peers :])
+        own_tiles, got_tiles = scratch[:2], scratch[2:4]
+        both, down, in_sem, out_sem = scratch[4:]
+        count = self.extent // tile
+        yield 2 * count
+        work = [(job, k) for job in range(2) for k in range(count)]
+
+        def piece_of(array, job, k):
+            piece = pl.ds(k * tile, tile)
+            return array.at[piece, :] if job == 0 else array.at[:, piece]
+
+        def fetch(job, k):
+            copies = []
+            for source in range(peers):
+                array = own[job] if source == 0 else got[job][source - 1]
+                target = own_tiles[job].at[k % 2]
+                if source:
+                    target = got_tiles[job].at[k % 2, source - 1]
+                copies.append(
+                    pltpu.make_async_copy(
+                        piece_of(array, job, k), target, in_sem.at[job, k % 2, source]
+                    )
+                )
+            return copies
+
+        def store(job, k):
+            if job:
+                return [
+                    pltpu.make_async_copy(
+                        down.at[k % 2], piece_of(outs[2], 1, k), out_sem.at[k % 2, 2]
+                    )
+                ]
+            return [
+                pltpu.make_async_copy(
+                    both.at[k % 2, n], piece_of(outs[n], 0, k), out_sem.at[k % 2, n]
+                )
+                for n in range(2)
+            ]
+
+        for copy in fetch(*work[0]):
+            copy.start()
+        for number, (job, k) in enumerate(work):
+            if number + 1 < len(work):
+                for copy in fetch(*work[number + 1]):
+                    copy.start()
+            for copy in fetch(job, k):
+                copy.wait()
+            if k >= 2:
+                for copy in store(job, k - 2):
+                    copy.wait()
+            for peer in range(peers):
+                first = peer * window
+                width = min(window, eff - first)
+                skip = window - width
+                for source in range(peers):
+
+                    @pl.when(lax.rem(at["p"] - peer + peers, peers) == source)
+                    def _():
+                        if source:
+                            view = got_tiles[job].at[k % 2, source - 1]
+                        else:
+                            view = own_tiles[job].at[k % 2]
+                        if job:
+                            down[k % 2, pl.ds(first, width), :] = view[
+                                pl.ds(skip, width), :
+                            ].astype(F32)
+                        else:
+                            for n in range(2):
+                                both[k % 2, n, :, pl.ds(first, width)] = view[
+                                    :, pl.ds(n * window + skip, width)
+                                ].astype(F32)
+
+            for copy in store(job, k):
+                copy.start()
+            yield
+        for job in range(2):
+            for k in range(max(0, count - 2), count):
+                for copy in store(job, k):
+                    copy.wait()
+
+
 def gather_all(grid, arrays, items, collective_id):
     return together(grid, [Gather(grid, arrays, items)], collective_id, "gather_all")[0]
 
 
-def sum_scattered(grid, arrays, items, rounds, collective_id):
-    part = Scatter(grid, arrays, items, rounds)
-    return together(grid, [part], collective_id, "sum_scattered")[0]
-
-
-def normalize(values, gain_row):
-    scale_rows = lax.rsqrt(jnp.mean(values * values, -1, keepdims=True) + EPSILON)
-    return (values * scale_rows * gain_row, scale_rows)
-
-
-def normalize_back(values, scale_rows, gain_row, gradient):
-    weighted = gradient * gain_row
-    gain_grad = jnp.sum(gradient * values * scale_rows, 0)
-    inner_mean = jnp.mean(weighted * values, -1, keepdims=True)
-    return (
-        scale_rows * weighted - values * scale_rows * scale_rows * scale_rows * inner_mean,
-        gain_grad,
-    )
-
-
-def rope_tables(length, width):
-    half_width = width // 2
-    frequency = ROPE_BASE ** (-2.0 * jnp.arange(half_width, dtype=jnp.float32) / width)
-    angles = jnp.arange(length, dtype=jnp.float32)[:, None] * frequency[None, :]
-    return (jnp.cos(angles), jnp.sin(angles))
-
-
-def rotate(values, cosine, sine_table):
-    half_width = values.shape[-1] // 2
-    front_half = values[..., :half_width]
-    back_half = values[..., half_width:]
-    return jnp.concatenate(
-        [
-            front_half * cosine - back_half * sine_table,
-            back_half * cosine + front_half * sine_table,
-        ],
-        -1,
-    )
-
-
-def unrotate(gradient, cosine, sine_table):
-    half_width = gradient.shape[-1] // 2
-    front_half = gradient[..., :half_width]
-    back_half = gradient[..., half_width:]
-    return jnp.concatenate(
-        [
-            front_half * cosine + back_half * sine_table,
-            back_half * cosine - front_half * sine_table,
-        ],
-        -1,
-    )
+def position_tables():
+    frequency = ROPE_BASE ** (-2.0 * np.arange(HALF) / ROPE)
+    angles = np.tile(np.arange(SEQ)[:, None] * frequency[None, :], (MICRO, HEADS))
+    return [jnp.asarray(np.cos(angles), F32), jnp.asarray(np.sin(angles), F32)]
 
 
 def capacity_for(expert_count):
     return min(SEQ, ((4 * SEQ * TOP + 3 * expert_count - 1) // (3 * expert_count) + 7) // 8 * 8)
-
-
-def silu_parts(pre_act):
-    sigma_rows = jax.nn.sigmoid(pre_act)
-    return (pre_act * sigma_rows, sigma_rows * (1.0 + pre_act * (1.0 - sigma_rows)))
-
-
-def attention_mask(segment_row):
-    places = jnp.arange(segment_row.shape[0], dtype=jnp.int32)
-    return (places[:, None] >= places[None, :]) & (segment_row[:, None] == segment_row[None, :])
 
 
 def dot(left, right):
@@ -898,121 +1472,26 @@
     return parts
 
 
-def swap_windows(pieces, axis_size):
+def plain_weight_grads(grid, kept, extent):
     me = lax.axis_index("dp")
-    got = [pieces(me)]
-    for step in range(1, axis_size):
-        peer = lax.rem(me + step, axis_size)
-        perm = [(k, (k + step) % axis_size) for k in range(axis_size)]
-        got.append(lax.ppermute(pieces(peer), "dp", perm))
-    return got
-
-
-def in_order(got):
-    me = lax.axis_index("dp")
-    count = len(got)
-    ordered = []
-    for k in range(count):
-        value = got[0]
-        for step in range(1, count):
-            value = jnp.where(lax.rem(me - k + count, count) == step, got[step], value)
-        ordered.append(value)
-    return ordered
-
-
-def attention_forward(rows, segments, weights, tables):
-    attn_gain, q_weight, kv_down, kv_gain, kv_up, out_weight, ffn_gain, router = weights
-    cosine, sine_table = tables
-    count = rows.shape[0]
-    inputs = rows.astype(F32)
-    normed_f, scale_one = normalize(inputs, attn_gain)
-    normed = normed_f.astype(BF)
-    q_raw = dot(normed, q_weight).reshape(MICRO, SEQ, HEADS, NOPE + ROPE)
-    turn = (cosine[:, None, :], sine_table[:, None, :])
-    queries = jnp.concatenate([q_raw[..., :NOPE], rotate(q_raw[..., NOPE:], *turn)], -1).astype(BF)
-    kv_raw = dot(normed, kv_down)
-    latent_f, scale_latent = normalize(kv_raw[:, :RANK], kv_gain)
-    latent = latent_f.astype(BF)
-    key_rope = rotate(kv_raw[:, RANK:].reshape(MICRO, SEQ, ROPE), cosine, sine_table)
-    kv_full = dot(latent, kv_up).reshape(MICRO, SEQ, HEADS, NOPE + VDIM)
-    shared_key = jnp.broadcast_to(key_rope[:, :, None, :], (MICRO, SEQ, HEADS, ROPE))
-    key_rows = jnp.concatenate([kv_full[..., :NOPE], shared_key], -1).astype(BF)
-    value_rows = kv_full[..., NOPE:].astype(BF)
-    allowed = jax.vmap(attention_mask)(segments)[:, None]
-    scores = jnp.einsum("mqhe,mkhe->mhqk", queries, key_rows, preferred_element_type=F32)
-    scores = jnp.where(allowed, scores * (NOPE + ROPE) ** (-0.5), MASKED)
-    powers = jnp.exp(scores - jnp.max(scores, -1, keepdims=True))
-    softmax_rows = powers / jnp.sum(powers, -1, keepdims=True)
-    probability = softmax_rows.astype(BF)
-    attended = (
-        jnp.einsum("mhqk,mkhe->mqhe", probability, value_rows, preferred_element_type=F32)
-        .reshape(count, HEADS * VDIM)
-        .astype(BF)
-    )
-    residual = inputs + dot(attended, out_weight)
-    hidden_f, scale_two = normalize(residual, ffn_gain)
-    hidden = hidden_f.astype(BF)
-    saved = (
-        inputs, scale_one, normed, queries, kv_raw, scale_latent, latent, key_rows, value_rows,
-        softmax_rows, probability, attended, residual, scale_two,
-    )
-    return hidden, saved
-
-
-def attention_backward(grad_out, hidden_grad, saved, weights, tables):
-    attn_gain, q_weight, kv_down, kv_gain, kv_up, out_weight, ffn_gain, router = weights
-    cosine, sine_table = tables
-    (
-        inputs, scale_one, normed, queries, kv_raw, scale_latent, latent, key_rows, value_rows,
-        softmax_rows, probability, attended, residual, scale_two,
-    ) = saved
-    count = inputs.shape[0]
-    turn = (cosine[:, None, :], sine_table[:, None, :])
-    residual_part, ffn_gain_grad = normalize_back(residual, scale_two, ffn_gain, hidden_grad)
-    residual_grad = grad_out + residual_part
-    mixed_grad = residual_grad.astype(BF)
-    out_weight_grad = t_dot(attended, mixed_grad)
-    attended_grad = dot_t(mixed_grad, out_weight).astype(BF).reshape(MICRO, SEQ, HEADS, VDIM)
-    value_grad = jnp.einsum(
-        "mhqk,mqhe->mkhe", probability, attended_grad, preferred_element_type=F32
-    )
-    probs_grad = jnp.einsum(
-        "mqhe,mkhe->mhqk", attended_grad, value_rows, preferred_element_type=F32
-    )
-    inner = jnp.sum(softmax_rows * probs_grad, -1, keepdims=True)
-    score_grad = (softmax_rows * (probs_grad - inner)).astype(BF)
-    score_scale = (NOPE + ROPE) ** (-0.5)
-    query_grad = score_scale * jnp.einsum(
-        "mhqk,mkhe->mqhe", score_grad, key_rows, preferred_element_type=F32
-    )
-    keys_grad = score_scale * jnp.einsum(
-        "mhqk,mqhe->mkhe", score_grad, queries, preferred_element_type=F32
-    )
-    q_raw_grad = (
-        jnp.concatenate([query_grad[..., :NOPE], unrotate(query_grad[..., NOPE:], *turn)], -1)
-        .reshape(count, HEADS * (NOPE + ROPE))
-        .astype(BF)
-    )
-    q_weight_grad = t_dot(normed, q_raw_grad)
-    kv_full_grad = (
-        jnp.concatenate([keys_grad[..., :NOPE], value_grad], -1)
-        .reshape(count, HEADS * (NOPE + VDIM))
-        .astype(BF)
-    )
-    kv_up_grad = t_dot(latent, kv_full_grad)
-    latent_grad = dot_t(kv_full_grad, kv_up)
-    latent_part, kv_gain_grad = normalize_back(
-        kv_raw[:, :RANK], scale_latent, kv_gain, latent_grad
-    )
-    rope_grad = unrotate(jnp.sum(keys_grad[..., NOPE:], 2), cosine, sine_table)
-    kv_raw_grad = jnp.concatenate([latent_part, rope_grad.reshape(count, ROPE)], -1).astype(BF)
-    kv_down_grad = t_dot(normed, kv_raw_grad)
-    normed_grad = dot_t(q_raw_grad, q_weight) + dot_t(kv_raw_grad, kv_down)
-    input_part, attn_gain_grad = normalize_back(inputs, scale_one, attn_gain, normed_grad)
-    tokens_grad = residual_grad + input_part
-    return tokens_grad, (
-        attn_gain_grad, q_weight_grad, kv_down_grad, kv_gain_grad, kv_up_grad, out_weight_grad,
-        ffn_gain_grad,
+    peers = grid.size["p"]
+
+    def total(left, right):
+        return functools.reduce(jnp.add, [t_dot(entry[left], entry[right]) for entry in kept])
+
+    def share_of(array, step, axis):
+        peer = lax.rem(me + step, peers)
+        return lax.dynamic_slice_in_dim(array, peer * extent, extent, axis)
+
+    both, down = total(0, 2), total(3, 1)
+    steps = range(1, peers)
+    return (
+        share_of(both, 0, 0),
+        share_of(down, 0, 1),
+        jnp.stack([share_of(both, step, 0) for step in steps]).astype(BF),
+        jnp.stack([share_of(down, step, 1) for step in steps]).astype(BF),
+        total(6, 4).astype(BF),
+        total(5, 7),
     )
 
 
@@ -1040,30 +1519,96 @@
     devices = grid.devices
     dp_size = grid.size["p"]
     experts = router.shape[1]
-    tables = rope_tables(SEQ, ROPE)
-    me_dp = lax.axis_index("dp")
     count = MICRO * SEQ
     eff = expert_gate.shape[2]
-
+    extent = expert_gate.shape[1]
     window = -(-eff // (128 * dp_size)) * 128
-    starts = [min(k * window, eff - window) for k in range(dp_size)]
-
-    def start_of(peer):
-        return jnp.minimum(peer * window, eff - window)
-
-    def columns_for(array):
-        return lambda peer: lax.dynamic_slice_in_dim(array[0], start_of(peer), window, 1)
-
-    def rows_for(array):
-        return lambda peer: lax.dynamic_slice_in_dim(array[0], start_of(peer), window, 0)
-
-    gate_part = jnp.concatenate(in_order(swap_windows(columns_for(expert_gate), dp_size)), 0)
-    up_part = jnp.concatenate(in_order(swap_windows(columns_for(expert_up), dp_size)), 0)
-    down_part = jnp.concatenate(in_order(swap_windows(rows_for(expert_down), dp_size)), 1)
-    fresh = jnp.arange(window, dtype=jnp.int32) + start_of(me_dp) >= me_dp * window
-    gate_part = jnp.where(fresh[None, :], gate_part, 0)
-    up_part = jnp.where(fresh[None, :], up_part, 0)
-    down_part = jnp.where(fresh[:, None], down_part, 0)
+    own = (expert_gate[0], expert_up[0], expert_down[0])
+
+    rows = q_weight.shape[0]
+    q_heads = q_weight.reshape(rows, HEADS, NOPE + ROPE)
+    q_sent = jnp.concatenate(
+        [
+            q_heads[:, :, :NOPE].reshape(rows, WIDE),
+            q_heads[:, :, NOPE : NOPE + HALF].reshape(rows, TURN),
+            q_heads[:, :, NOPE + HALF :].reshape(rows, TURN),
+        ],
+        1,
+    )
+    gap = jnp.zeros((rows, 128 - HALF), BF)
+    down_sent = jnp.concatenate(
+        [kv_down[:, : RANK + HALF], gap, kv_down[:, RANK + HALF :], gap], 1
+    )
+    small_shapes = (attn_gain.shape, ffn_gain.shape, kv_gain.shape, router.shape)
+    small = pack([attn_gain[None], ffn_gain[None], kv_gain[None], router[None]], 1)[0]
+    up_shape = kv_up.shape
+    up_sent = kv_up if up_shape[0] % 16 == 0 else kv_up.reshape(16, -1)
+    first, second, third = ("q", "r", "p"), ("q", "p", "r"), ("p", "q", "r")
+
+    def columns_of(ref, peer, step):
+        return ref.at[:, pl.ds(window_start(peer, dp_size, window, eff), window)]
+
+    def rows_of(ref, peer, step):
+        return ref.at[pl.ds(window_start(peer, dp_size, window, eff), window), :]
+
+    gathered, windows = together(
+        grid,
+        [
+            Gather(
+                grid,
+                [q_sent, down_sent, up_sent, out_weight, small],
+                [
+                    (0, 0, q_sent.shape[1], third),
+                    (1, 0, down_sent.shape[1], third),
+                    (2, 0, up_sent.shape[1], ("r", "p", "q")),
+                    (3, 0, out_weight.shape[1], first),
+                    (4, 0, 128, first),
+                ],
+            ),
+            Exchange(grid, own[:2], [columns_of] * 2, [(extent, window)] * 2),
+        ],
+        0,
+        "gather_attention",
+    )
+    parts = unpack(gathered[4], small_shapes)
+    gains = [parts[n].reshape(1, -1).astype(F32) for n in (0, 2, 1)]
+    weights = [
+        gathered[0].reshape(D, -1),
+        gathered[1].reshape(D, -1),
+        gathered[2].reshape(RANK, -1),
+        gathered[3].reshape(-1, D),
+        jnp.pad(parts[3].reshape(D, experts), ((0, 0), (0, 128 - experts))),
+    ]
+
+    token_rows = tokens.reshape(count, D)
+    grad_out = cotangent.reshape(count, D)
+    tables = position_tables()
+    numbers = segments.reshape(1, -1) + 4 * (jnp.arange(count, dtype=jnp.int32) // SEQ)[None, :]
+    places = jnp.arange(count, dtype=jnp.int32)
+    allowed = (numbers == numbers.T) & (places[:, None] >= places[None, :])
+
+    def half_orders(a):
+        return [(a, 0, D // 2, first), (a, D // 2, D // 2, second)]
+
+    (grad_first,), saved, windows_down = together(
+        grid,
+        [
+            Gather(grid, [grad_out[:SEQ]], [(0, 0, D // 2, third), (0, D // 2, D // 2, second)]),
+            AttentionForward(
+                token_rows,
+                routes.reshape(count, TOP),
+                allowed.astype(F32),
+                tables,
+                gains,
+                weights,
+                experts,
+            ),
+            Exchange(grid, own[2:], [rows_of], [(window, extent)]),
+        ],
+        6,
+        "attention_forward",
+    )
+    hidden, dense_gates, residual = saved[0], saved[1], saved[11]
 
     share = shared_gate.shape[1] // devices
     both = jnp.concatenate(
@@ -1082,67 +1627,28 @@
     )
     shared_part = jnp.pad(shared_down, ((0, room - share), (0, 0)))
 
-    small_shapes = (attn_gain.shape, ffn_gain.shape, kv_gain.shape, router.shape)
-    small = pack([attn_gain[None], ffn_gain[None], kv_gain[None], router[None]], 1)[0]
-    up_shape = kv_up.shape
-    kv_up_sent = kv_up if up_shape[0] % 16 == 0 else kv_up.reshape(16, -1)
-    first, second = ("q", "r", "p"), ("q", "p", "r")
-    got = gather_all(
-        grid,
-        [q_weight, kv_down, kv_up_sent, out_weight, small],
-        [
-            (0, 0, q_weight.shape[1], first),
-            (3, 0, out_weight.shape[1], second),
-            (2, 0, kv_up_sent.shape[1], second),
-            (1, 0, kv_down.shape[1], second),
-            (4, 0, 128, first),
-        ],
-        0,
-    )
-    gains = unpack(got[4], small_shapes)
-    weights = (
-        gains[0].reshape(-1).astype(F32),
-        got[0].reshape(D, -1),
-        got[1].reshape(D, -1),
-        gains[2].reshape(-1).astype(F32),
-        got[2].reshape(RANK, -1),
-        got[3].reshape(-1, D),
-        gains[1].reshape(-1).astype(F32),
-        gains[3].reshape(D, experts),
-    )
-    router_full = weights[7]
-
-    token_rows = tokens.reshape(count, D)
-    grad_out = cotangent.reshape(count, D)
-    route_rows = routes.reshape(count, TOP)
-    hidden, saved = attention_forward(token_rows, segments.reshape(MICRO, SEQ), weights, tables)
-    logits = dot(hidden, router_full)
-    choose = route_rows[:, :, None] == jnp.arange(experts, dtype=jnp.int32)[None, None, :]
-    choose = choose.astype(F32)
-    gate_share = jax.nn.softmax(jnp.sum(choose * logits[:, None, :], -1), -1)
-    dense_share = jnp.sum(choose * gate_share[..., None], 1)
-    dense_gates = jnp.where(jnp.sum(choose, 1) > 0, dense_share, -1.0)
-
     half = D // 2
     capacity = capacity_for(experts)
     expert = lax.axis_index("expert")
-    own_weights = (gate_part, up_part, down_part, shared_in, shared_part)
+    own_weights = (own, (*windows, *windows_down), shared_in, shared_part)
 
     def gather_of(chunk):
         piece = slice(chunk * SEQ, (chunk + 1) * SEQ)
-        sent = [hidden[piece], grad_out[piece], dense_gates[piece].T]
-        orders = [(0, 0, half, first), (0, half, half, second)]
-        orders += [(1, 0, half, first), (1, half, half, second), (2, 0, SEQ, first)]
+        sent = [hidden[piece], dense_gates[:, piece]]
+        orders = half_orders(0) + [(1, 0, SEQ, first)]
+        if chunk:
+            sent.append(grad_out[piece])
+            orders += half_orders(2)
         return Gather(grid, sent, orders)
 
     kept_hidden, kept_grad = [], []
 
-    def experts_of(gathered):
-        hidden_all, grad_all, gates_all = gathered
+    def experts_of(hidden_all, gates_all, grad_all):
         kept_hidden.append(hidden_all)
         kept_grad.append(grad_all)
         share = lax.dynamic_index_in_dim(gates_all, expert, 1, keepdims=False)
         return Experts(
+            grid,
             hidden_all.reshape(-1, D),
             grad_all.reshape(-1, D),
             share.reshape(-1, GROUP),
@@ -1157,25 +1663,39 @@
         shape = (devices, SEQ, D)
         return [hidden_part.reshape(shape), gate_grad, out_part.reshape(shape)]
 
+    def kept_of(done):
+        flat = [(h.reshape(-1, D), g.reshape(-1, D)) for h, g in zip(kept_hidden, kept_grad)]
+        return [tuple(entry[3:]) + pair for entry, pair in zip(done, flat)]
+
     over = [(0, 0, half, ("p", "r")), (0, half, half, ("r", "p"))]
     over_gates = [(1, 0, SEQ, ("p", "r"))]
     over_out = [(2, 0, half, ("p", "r")), (2, half, half, ("r", "p"))]
     if devices <= 32:
         (gathered,) = together(grid, [gather_of(0)], 1, "gather_first")
         gathered, done_0 = together(
-            grid, [gather_of(1), experts_of(gathered)], 2, "gather_second_experts_first"
+            grid,
+            [gather_of(1), experts_of(*gathered, grad_first)],
+            2,
+            "gather_second_experts_first",
         )
         everything = over + over_gates + over_out
         sums_0, done_1 = together(
             grid,
-            [Scatter(grid, sums_of(done_0), everything, [[0, 1], [2]]), experts_of(gathered)],
+            [Scatter(grid, sums_of(done_0), everything, [[0, 1], [2]]), experts_of(*gathered)],
             3,
             "scatter_first_experts_second",
         )
-        (sums_1,) = together(
-            grid, [Scatter(grid, sums_of(done_1), everything, [[0, 1], [2]])], 4, "scatter_second"
+        kept = kept_of((done_0, done_1))
+        sums_1, weight_grads = together(
+            grid,
+            [
+                Scatter(grid, sums_of(done_1), everything, [[0, 1], [2]]),
+                WeightGrads(grid, kept, extent),
+            ],
+            4,
+            "scatter_second_weight_grads",
         )
-        sums, done = (sums_0, sums_1), (done_0, done_1)
+        sums = (sums_0, sums_1)
     else:
         sums, done = [], []
         for chunk in range(MICRO):
@@ -1183,8 +1703,8 @@
             if chunk:
                 before = tuple(sums[-1])
                 *part.inputs, sums[-1] = lax.optimization_barrier((*part.inputs, before))
-            (gathered,) = together(grid, [part], 1, "gather")
-            part = experts_of(gathered)
+            (gathered,) = together(grid, [part], 1 + 7 * chunk, "gather")
+            part = experts_of(*gathered, *([] if chunk else [grad_first]))
             (now,) = together(grid, [part], None, "experts")
             parts = sums_of(now)
             (hidden_gates,) = together(
@@ -1193,91 +1713,104 @@
             (out_sum,) = together(grid, [Scatter(grid, parts[2:], over, [[0]])], 3, "scatter_out")
             sums.append((*hidden_gates, *out_sum))
             done.append(now)
+        weight_grads = plain_weight_grads(grid, kept_of(done), extent)
     hidden_sum = jnp.concatenate([entry[0] for entry in sums], 0)
-    gate_grad = jnp.concatenate([entry[1].T for entry in sums], 0)
-    result = saved[12] + jnp.concatenate([entry[2] for entry in sums], 0)
-
-    dense_share = jnp.maximum(dense_share, 0.0)
-    inner = jnp.sum(dense_share * gate_grad, -1, keepdims=True)
-    logit_grad = (dense_share * (gate_grad - inner)).astype(BF)
-    router_grad = t_dot(hidden, logit_grad)
-    hidden_grad = hidden_sum + dot_t(logit_grad, router_full)
-    tokens_grad, (
-        attn_gain_grad, q_weight_grad, kv_down_grad, kv_gain_grad, kv_up_grad, out_weight_grad,
-        ffn_gain_grad,
-    ) = attention_backward(grad_out.astype(F32), hidden_grad, saved, weights, tables)
-
+    gate_grad = jnp.concatenate([entry[1] for entry in sums], 1)
+    result = residual + jnp.concatenate([entry[2] for entry in sums], 0)
+    own_ab, own_down, sent_ab, sent_down, shared_in_grad, shared_down_grad = weight_grads
+
+    def sent_to(ref, peer, step):
+        return ref.at[step - 1]
+
+    attention_grads, (got_ab, got_down) = together(
+        grid,
+        [
+            AttentionBackward(
+                grad_out, hidden_sum, gate_grad, saved, token_rows, tables, gains, weights
+            ),
+            Exchange(
+                grid,
+                [sent_ab, sent_down],
+                [sent_to] * 2,
+                [(extent, 2 * window), (window, extent)],
+            ),
+        ],
+        7,
+        "attention_backward",
+    )
+    (
+        out_weight_grad, kv_up_grad, q_weight_grad, kv_down_grad, tokens_grad, attn_gain_grad,
+        kv_gain_grad, ffn_gain_grad, router_grad,
+    ) = attention_grads
+    shared_down_grad = shared_down_grad[:share]
+    shared_in_grad = jnp.concatenate(
+        [shared_in_grad[:, :share], shared_in_grad[:, room : room + share]], 1
+    )
     small_grads = pack(
         [
             attn_gain_grad.reshape(devices, -1),
             ffn_gain_grad.reshape(devices, -1),
             kv_gain_grad.reshape(devices, -1),
-            router_grad.reshape(devices, -1),
+            router_grad[:, :experts].reshape(devices, -1),
         ],
         devices,
     )
+
     def halves(a, columns):
         part = columns // 256 * 128
         return [(a, 0, part, ("p", "r")), (a, part, columns - part, ("r", "p"))]
 
-    q_sum, down_sum, up_sum, out_weight_sum, small_sum = sum_scattered(
+    attention_sums = Scatter(
         grid,
         [
-            q_weight_grad.astype(BF).reshape((devices,) + q_weight.shape),
-            kv_down_grad.astype(BF).reshape((devices,) + kv_down.shape),
-            kv_up_grad.astype(BF).reshape((devices,) + kv_up_sent.shape),
-            out_weight_grad.astype(BF).reshape((devices,) + out_weight.shape),
+            q_weight_grad.reshape((devices,) + q_sent.shape),
+            kv_down_grad.reshape((devices,) + down_sent.shape),
+            kv_up_grad.reshape((devices,) + up_sent.shape),
+            out_weight_grad.reshape((devices,) + out_weight.shape),
             small_grads,
         ],
-        halves(0, q_weight.shape[1])
-        + halves(1, kv_down.shape[1])
-        + halves(2, kv_up_sent.shape[1])
+        halves(0, q_sent.shape[1])
+        + halves(1, down_sent.shape[1])
+        + halves(2, up_sent.shape[1])
         + halves(3, out_weight.shape[1])
         + [(4, 0, 128, ("p", "r"))],
         [[3], [2, 1], [0, 4]],
-        5,
+    )
+    experts_grads = Assemble(
+        grid,
+        own_ab,
+        own_down,
+        [got_ab[step] for step in range(dp_size - 1)],
+        [got_down[step] for step in range(dp_size - 1)],
+        eff,
+    )
+    (q_sum, down_sum, up_sum, out_weight_sum, small_sum), experts_grads = together(
+        grid, [attention_sums, experts_grads], 5, "scatter_attention_assemble"
     )
     small_sums = unpack(small_sum[None], small_shapes)
-
-    def total(pairs):
-        return functools.reduce(jnp.add, [t_dot(left, right) for left, right in pairs])
-
-    kept = [entry[3:] for entry in done]
-    chunks = range(MICRO)
-    both_grad = total([(kept[c][0], kept[c][2]) for c in chunks])
-    gate_grad_part, up_grad_part = both_grad[:, :window], both_grad[:, window:]
-    down_grad_part = total([(kept[c][3], kept[c][1]) for c in chunks])
-    hidden_rows = [kept_hidden[c].reshape(-1, D) for c in chunks]
-    grad_rows = [kept_grad[c].reshape(-1, D) for c in chunks]
-    shared_in_grad = total([(hidden_rows[c], kept[c][4]) for c in chunks])
-    shared_down_grad = total([(kept[c][5], grad_rows[c]) for c in chunks])[:share]
-    shared_in_grad = jnp.concatenate(
-        [shared_in_grad[:, :share], shared_in_grad[:, room : room + share]], 1
+    q_sum = jnp.concatenate(
+        [
+            q_sum[:, :WIDE].reshape(rows, HEADS, NOPE),
+            q_sum[:, WIDE : WIDE + TURN].reshape(rows, HEADS, HALF),
+            q_sum[:, WIDE + TURN :].reshape(rows, HEADS, HALF),
+        ],
+        2,
+    ).reshape(q_weight.shape)
+    down_sum = jnp.concatenate(
+        [down_sum[:, : RANK + HALF], down_sum[:, RANK + 128 : RANK + 128 + HALF]], 1
     )
+
     shared_back = lax.all_to_all(
-        shared_in_grad.astype(BF).reshape(devices, -1, 2 * share),
+        shared_in_grad.reshape(devices, -1, 2 * share),
         ("dp", "expert"), split_axis=0, concat_axis=0, tiled=True,
     ).astype(F32)
     shared_back = shared_back.transpose(1, 0, 2)
     shared_gate_grad = shared_back[:, :, :share].reshape(shared_gate.shape)
     shared_up_grad = shared_back[:, :, share:].reshape(shared_up.shape)
 
-    def whole(part, axis, other, extent):
-        def for_peer(peer):
-            return lax.dynamic_slice_in_dim(part, peer * extent, extent, other)
-
-        got_back = swap_windows(lambda peer: for_peer(peer).astype(BF), dp_size)
-        got_back = [for_peer(me_dp)] + [piece.astype(F32) for piece in got_back[1:]]
-        pieces = []
-        for k, piece in enumerate(in_order(got_back)):
-            skip = k * window - starts[k]
-            pieces.append(lax.slice_in_dim(piece, skip, window, axis=axis))
-        return jnp.concatenate(pieces, axis)[None]
-
-    extent = expert_gate.shape[1]
     return (
         result.astype(BF).reshape(tokens.shape),
-        tokens_grad.astype(BF).reshape(tokens.shape),
+        tokens_grad.reshape(tokens.shape),
         small_sums[0].reshape(-1),
         q_sum,
         down_sum,
@@ -1289,9 +1822,9 @@
         shared_gate_grad,
         shared_up_grad,
         shared_down_grad,
-        whole(gate_grad_part, 1, 0, extent),
-        whole(up_grad_part, 1, 0, extent),
-        whole(down_grad_part, 0, 1, extent),
+        experts_grads[0][None],
+        experts_grads[1][None],
+        experts_grads[2][None],
     )
 
 

time: 1140 us -> 976 us (0.86)
  matrix products: 113 us -> 0 us
  other arithmetic: 65.6 us -> 18.4 us
  Pallas kernels: 834 us -> 878 us
  local copies, waits for them, and re-layouts: 101 us -> 59.1 us
    dot_general x29 -> x0, matrix products: 113 us -> none  [the longest x13 61.1 us: t_dot(): lax.dot_general(left, right, (((0,), (0,)), ((), ())), preferred_element_...]
    pallas_call x6 -> x8, Pallas kernels: 834 us -> 878 us  [together(): pl.pallas_call(kernel, out_shape=[shape for part in parts for shape in pa...]
    select_n x12 -> x0, other arithmetic: 23.4 us -> none  [the longest x9 18 us: in_order(): value = jnp.where(lax.rem(me - k + count, count) == step, got[step], value)]
    dot_general x2 -> x0, local copies, waits for them, and re-layouts: 23.3 us -> none  [dot(): return jnp.dot(left, right, preferred_element_type=F32)]
    convert_element_type x11 -> x3, local copies, waits for them, and re-layouts: 15.6 us -> 2.01 us  [body(): gains = [parts[n].reshape(1, -1).astype(F32) for n in (0, 2, 1)]]
  transfers between devices with their start and end apart: 8 -> 2, of which waited for: 0 -> 0; matrix products, arithmetic and copies ran while one was open for 14% -> 4% of each run, Pallas kernels for 44% -> 55%
where the time goes in v2:
time: 976 us; the launch traced here: 967 us
  Pallas kernels  878 us (90%)
  local copies, waits for them, and re-layouts  59.1 us (6%)
  other arithmetic  18.4 us (2%)
  starting transfers between devices  10.2 us (1%)
    pallas_call x8, Pallas kernels, together(): pl.pallas_call(kernel, out_shape=[shape for part in parts for shape in pa...  878 us
  transfers between devices with their start and end apart: 2, of which 0 were waited for; matrix products, arithmetic and copies ran while one was open for 4% of the time, Pallas kernels for 55%

profile of v2, /device:TPU:16, one launch (start us, length us, event | category | flops | bytes accessed | tf_op | source)
XLA Modules:
  0.0 966.9 jit_solution(2182445363562096660)
XLA Ops:
  0.6 2.2 reshape.290
  3.1 2.3 reshape.291
  5.6 1.5 maximum_bitcast_fusion
  7.1 5.9 all-to-all-start
  17.2 147.4 %gather_attention.1 = (bf16[32,64,3072]{2,1,0:T(8,128)(2,1)}, bf16[32,64,768]{2,1,0:T(8,128)(2,1)}, bf16[32,16,4096]{2,1,0:T(8,128)(2,1)}, bf16[32,64,2048]{2,1,...) custom-call(bf16[64,3072]{1,0:T(8,128)(2,1)} %pad_maximum_fusion.3.refs_, ...), custom_call_target="tpu_custom_call" | custom-call | tf_op jit(solution)/shard_map/gather_attention/pallas_call | solution.py:512
  172.6 77.7 %attention_forward.1 = (bf16[32,64,2048]{2,1,0:T(8,128)(2,1)}, bf16[128,2048]{1,0:T(8,128)(2,1)}, f32[16,128]{1,0:T(8,128)}, bf16[128,2048]{1,0:T(8,128)(2,1)}, ...) custom-call(bf16[64,2048]{1,0:T(8,128)(2,1)} %get-tuple-element.207., ...), custom_call_target="tpu_custom_call" | custom-call | tf_op jit(solution)/shard_map/attention_forward/pallas_call | solution.py:512
  250.3 1.4 fusion.12
  251.7 1.9 fusion.10
  253.6 47.4 %gather_first.1 = (bf16[32,64,2048]{2,1,0:T(8,128)(2,1)}, f32[32,16,64]{2,1,0:T(8,128)}) custom-call(bf16[64,2048]{1,0:T(8,128)(2,1)} %get-tuple-element.204.refs_0_, f32[16,64]{1,0:T(8,128)} %get-tuple-element.214.refs_1_), custom_call_target="tpu_custom_call" | custom-call | tf_op jit(solution)/shard_map/gather_first/pallas_call | solution.py:512
  305.0 118.5 %gather_second_experts_first.1 = (bf16[32,64,2048]{2,1,0:T(8,128)(2,1)}, f32[32,16,64]{2,1,0:T(8,128)}, bf16[32,64,2048]{2,1,0:T(8,128)(2,1)}, bf16[2048,2048]{1...) custom-call(bf16[64,2048]{1,0:T(8,128)(2,1)} %get-tuple-element.205., ...), custom_call_target="tpu_custom_call" | custom-call | tf_op jit(solution)/shard_map/gather_second_experts_first/pallas_call | solution.py:512
  426.6 122.5 %scatter_first_experts_second.1 = (f32[64,2048]{1,0:T(8,128)}, f32[16,64]{1,0:T(8,128)}, f32[64,2048]{1,0:T(8,128)}, bf16[2048,2048]{1,0:T(8,128)(2,1)}, bf16[20...) custom-call(bf16[32,64,2048]{2,1,0:T(8,128)(2,1)} %bitcast.102, ...), custom_call_target="tpu_custom_call" | custom-call | tf_op jit(solution)/shard_map/scatter_first_experts_second/pallas_call | solution.py:512
  550.7 100.4 %scatter_second_weight_grads.1 = (f32[64,2048]{1,0:T(8,128)}, f32[16,64]{1,0:T(8,128)}, f32[64,2048]{1,0:T(8,128)}, f32[1024,1536]{1,0:T(8,128)}, f32[768,1024]{...) custom-call(bf16[32,64,2048]{2,1,0:T(8,128)(2,1)} %bitcast.100, ...), custom_call_target="tpu_custom_call" | custom-call | tf_op jit(solution)/shard_map/scatter_second_weight_grads/pallas_call | solution.py:512
  651.2 1.4 fusion.8
  652.5 1.5 pad_maximum_fusion.2
  654.0 4.2 all-to-all-start.1
  658.9 2.7 fusion.2
  661.6 117.2 %attention_backward.1 = (bf16[2048,2048]{1,0:T(8,128)(2,1)}, bf16[512,4096]{1,0:T(8,128)(2,1)}, bf16[2048,3072]{1,0:T(8,128)(2,1)}, bf16[2048,768]{1,0:T(8,128)(...) custom-call(bf16[128,2048]{1,0:T(8,128)(2,1)} %bitcast.120, ...), custom_call_target="tpu_custom_call" | custom-call | tf_op jit(solution)/shard_map/attention_backward/pallas_call | solution.py:512
  778.8 1.9 reshape.310
  781.2 1.4 reduce.27
  782.6 1.4 reduce.28
  784.1 1.4 reduce.29
  786.4 146.9 %scatter_attention_assemble.1 = (f32[64,3072]{1,0:T(8,128)}, f32[64,768]{1,0:T(8,128)}, f32[16,4096]{1,0:T(8,128)}, f32[64,2048]{1,0:T(8,128)}, f32[16,128]{1,0:...) custom-call(bf16[32,64,3072]{2,1,0:T(8,128)(2,1)} %bitcast.97, ...), custom_call_target="tpu_custom_call" | custom-call | tf_op jit(solution)/shard_map/scatter_attention_assemble/pallas_call | solution.py:512
  939.1 1.3 reshape.316
  941.2 2.0 slice.136
  945.4 1.4 fusion.7
  947.4 1.4 reshape.320
  948.8 1.8 copy.56
  950.7 1.4 reshape.321
  953.6 2.3 copy.78
  955.9 5.7 copy.79
  961.6 2.5 copy.80
  964.1 2.5 copy.81
  (125 shorter events, 34.3 us)
Async XLA Ops:
  3.1 9.9 %copy-start.5 = (bf16[64,3072]{1,0:T(8,128)(2,1)S(1)}, bf16[64,3072]{1,0:T(8,128)(2,1)}, u32[]{:S(2)}) copy-start(bf16[64,3072]{1,0:T(8,128)(2,1)} %param.25) | copy-start | bytes 1179652
  7.0 7.6 copy-start.8
  7.0 7.7 copy-start.12
  7.0 7.9 copy-start.16
  7.0 7.9 copy-start.17
  7.0 7.9 copy-start.18
  7.1 296.4 %all-to-all-start = ((bf16[32,64,176]{2,1,0:T(8,128)(2,1)}), bf16[32,64,176]{2,1,0:T(8,128)(2,1)S(1)}, u32[]{:S(2)}, u32[]{:S(2)}) async-start(bf16[32,64,176]{2,1,0:T(8,128)(2,1)} %maximum_bitcast_fusion), calls=%async_computation | async-start | bytes 2097152 | tf_op jit(solution)/shard_map/all_to_all | solution.py:1617
  17.2 152.3 %copy-start.14 = (s32[2,1,64]{2,1,0:T(1,128)S(1)}, s32[2,1,64]{2,1,0:T(1,128)}, u32[]{:S(2)}) copy-start(s32[2,1,64]{2,1,0:T(1,128)} %param.23) | copy-start | bytes 1540
  17.2 153.1 %copy-start.11 = (s32[2,1,64,6]{2,1,3,0:T(1,128)S(1)}, s32[2,1,64,6]{2,1,3,0:T(1,128)}, u32[]{:S(2)}) copy-start(s32[2,1,64,6]{2,1,3,0:T(1,128)} %param.22) | copy-start | bytes 9220
  17.2 154.6 %copy-start.1 = (bf16[2,1,64,2048]{3,2,1,0:T(8,128)(2,1)S(1)}, bf16[2,1,64,2048]{3,2,1,0:T(8,128)(2,1)}, u32[]{:S(2)}) copy-start(bf16[2,1,64,2048]{3,2,1,0:T(8,128)(2,1)} %param.21) | copy-start | bytes 1572868
  172.6 130.0 %copy-start.6 = (bf16[88,2048]{1,0:T(8,128)(2,1)S(1)}, bf16[88,2048]{1,0:T(8,128)(2,1)}, u32[]{:S(2)}) copy-start(bf16[88,2048]{1,0:T(8,128)(2,1)} %param.34) | copy-start | bytes 1081348
  250.3 53.4 %copy-start.15 = (pred[128]{0:T(512)(128)(4,1)S(1)}, pred[128]{0:T(512)(128)(4,1)}, u32[]{:S(2)}) copy-start(pred[128]{0:T(512)(128)(4,1)} %constant.44.clone.1) | copy-start | bytes 388
  651.1 7.1 copy-start.9
  651.1 7.1 copy-start.10
  651.1 7.8 copy-start
  651.1 7.8 copy-start.3
  654.0 291.1 %all-to-all-start.1 = ((bf16[32,64,176]{2,1,0:T(8,128)(2,1)}), bf16[32,64,176]{2,1,0:T(8,128)(2,1)S(1)}, u32[]{:S(2)}, u32[]{:S(2)}) async-start(bf16[32,64,176]{2,1,0:T(8,128)(2,1)} %bitcast.112), calls=%async_computation.1 | async-start | bytes 2097152 | tf_op jit(solution)/shard_map/all_to_all | solution.py:1803
  933.3 4.4 copy-start.2
  937.7 2.7 copy-start.13
  945.4 16.2 %slice-start.2 = ((s8[5767168]{0:T(1024)(128)(4,1)}), s8[1572864]{0:T(1024)(128)(4,1)S(1)}, s32[]{:S(2)}) async-start(s8[5767168]{0:T(1024)(128)(4,1)} %bitcast.108), calls=%async_computation.4 | async-start | bytes 3145728
  947.4 4.7 copy-start.4
  947.4 5.5 copy-start.7
  952.9 8.7 slice-start.3
  955.9 8.2 slice-start
  961.6 2.5 slice-start.1

commit v3 on v2

--- a/solution.py
+++ b/solution.py
@@ -59,6 +59,9 @@
     def mesh_id(self, at):
         return (at["p"], self.expert_of(at))
 
+    def device_id(self, number):
+        return (lax.div(number, self.experts), lax.rem(number, self.experts))
+
     def partners(self, at):
         found = [{**at, "c": 1 - at["c"]}]
         for axis, size in self.size.items():
@@ -66,11 +69,16 @@
         return found
 
 
-def greet(grid, at):
+def greet(grid, at, everyone):
     barrier = pltpu.get_barrier_semaphore()
-    partners = grid.partners(at)
+    partners = [grid.mesh_id(partner) for partner in grid.partners(at)]
+    if everyone:
+        me = grid.number(at)
+        partners = [
+            grid.device_id(lax.rem(me + step, grid.devices)) for step in range(1, grid.devices)
+        ]
     for partner in partners:
-        pl.semaphore_signal(barrier, inc=1, device_id=grid.mesh_id(partner), device_id_type=MESH_ID)
+        pl.semaphore_signal(barrier, inc=1, device_id=partner, device_id_type=MESH_ID)
     pl.semaphore_wait(barrier, len(partners))
 
 
@@ -492,7 +500,7 @@
     def kernel(*refs):
         at = grid.here()
         if collective_id is not None:
-            greet(grid, at)
+            greet(grid, at, any(isinstance(part, AllToAll) for part in parts))
         ins, outs, scratch = [], [], []
         for list_of, key in ((ins, "inputs"), (outs, "out_shapes"), (scratch, "scratch")):
             for part in parts:
@@ -699,7 +707,7 @@
             for source, target in ((hidden_in, rows_in), (grad_in, grad_rows)):
                 for j in range(2):
 
-                    @tiles(D, 512)
+                    @tiles(D, 2048)
                     def _(columns):
                         target[pl.ds(j * slots, slots), columns] = jnp.dot(
                             picks[j],
@@ -710,7 +718,7 @@
                 yield
             for weight, target in ((gate, a_pre), (up, b_pre)):
 
-                @tiles(window, 256)
+                @tiles(window, window)
                 def _(columns):
                     target[:, columns] = jnp.dot(
                         rows_in[...], weight[:, columns], preferred_element_type=F32
@@ -718,7 +726,7 @@
 
                 yield
 
-            @tiles(window, 256)
+            @tiles(window, window)
             def _(columns):
                 flow[:, columns] = dot_t(grad_rows[...], down[columns, :])
 
@@ -748,7 +756,7 @@
                 )
             yield
 
-            @tiles(D, 256)
+            @tiles(D, 1024)
             def _(columns):
                 row_grad[:, columns] = (
                     dot_t(ab_grad[:, pl.ds(0, window)], gate[columns, :])
@@ -757,7 +765,7 @@
 
             yield
 
-            @tiles(D, 512)
+            @tiles(D, 2048)
             def _(columns):
                 expert_out[:, columns] = jnp.dot(
                     scaled[...], down[:, columns], preferred_element_type=F32
@@ -765,7 +773,7 @@
 
             yield
 
-            @tiles(2 * GROUP, GROUP)
+            @tiles(2 * GROUP, 2 * GROUP)
             def _(block):
                 shared_pre[block, :] = jnp.dot(
                     hidden_in[block, :], shared_in[...], preferred_element_type=F32
@@ -796,7 +804,7 @@
                 if k:
                     put(0, k - 1, j).wait()
 
-                @tiles(D, 256)
+                @tiles(D, 1024)
                 def _(columns):
                     parts[0][j, :, columns] = (
                         jnp.dot(
@@ -813,7 +821,7 @@
                 if k:
                     put(1, k - 1, j).wait()
 
-                @tiles(D, 256)
+                @tiles(D, 1024)
                 def _(columns):
                     parts[1][j, :, columns] = (
                         jnp.dot(
@@ -838,9 +846,47 @@
                 put(n, supers - 1, j).wait()
 
 
+class AllToAll:
+    def __init__(self, grid, array):
+        self.grid = grid
+        self.inputs = [array]
+        hbm = pl.BlockSpec(memory_space=pl.ANY)
+        self.in_specs, self.out_specs = [hbm], [hbm]
+        self.out_shapes = [jax.ShapeDtypeStruct(array.shape, array.dtype)]
+        self.scratch = [pltpu.SemaphoreType.DMA((grid.devices,))] * 2
+
+    def steps(self, at, ins, outs, scratch):
+        grid, (send_sem, recv_sem) = self.grid, scratch
+        me = grid.number(at)
+        yield 8
+
+        def copy(step):
+            there = lax.rem(me + step, grid.devices)
+            return pltpu.make_async_remote_copy(
+                src_ref=ins[0].at[there],
+                dst_ref=outs[0].at[me],
+                send_sem=send_sem.at[step],
+                recv_sem=recv_sem.at[step],
+                device_id=grid.device_id(there),
+                device_id_type=MESH_ID,
+            )
+
+        own = pltpu.make_async_copy(ins[0].at[me], outs[0].at[me], recv_sem.at[0])
+        own.start()
+        for k in range(8):
+            for step in range(1 + k, grid.devices, 8):
+                copy(step).start()
+            yield
+        own.wait()
+        for step in range(1, grid.devices):
+            copy(step).wait_send()
+            back = outs[0].at[lax.rem(me - step + grid.devices, grid.devices)]
+            pltpu.make_async_copy(back, back, recv_sem.at[step]).wait()
+
+
 class Exchange:
-    def __init__(self, grid, arrays, views, shapes):
-        self.grid, self.views = grid, views
+    def __init__(self, grid, arrays, views, shapes, begins=(0, 0)):
+        self.grid, self.views, self.begins = grid, views, begins
         self.peers = grid.size["p"]
         self.inputs = list(arrays)
         hbm = pl.BlockSpec(memory_space=pl.ANY)
@@ -854,22 +900,25 @@
 
     def steps(self, at, ins, outs, scratch):
         send_sem, recv_sem = scratch
-        yield 1
+        yield 20
         copies = []
-        for n, view in enumerate(self.views):
-            for step in range(1, self.peers):
-                there = self.grid.shift(at, {"p": step})
-                copy = pltpu.make_async_remote_copy(
-                    src_ref=view(ins[n], there["p"], step),
-                    dst_ref=outs[n].at[step - 1],
-                    send_sem=send_sem.at[n, step - 1],
-                    recv_sem=recv_sem.at[n, step - 1],
-                    device_id=self.grid.mesh_id(there),
-                    device_id_type=MESH_ID,
-                )
-                copy.start()
-                copies.append(copy)
-        yield
+        for k in range(20):
+            for n, view in enumerate(self.views):
+                if self.begins[n] != k:
+                    continue
+                for step in range(1, self.peers):
+                    there = self.grid.shift(at, {"p": step})
+                    copy = pltpu.make_async_remote_copy(
+                        src_ref=view(ins[n], there["p"], step),
+                        dst_ref=outs[n].at[step - 1],
+                        send_sem=send_sem.at[n, step - 1],
+                        recv_sem=recv_sem.at[n, step - 1],
+                        device_id=self.grid.mesh_id(there),
+                        device_id_type=MESH_ID,
+                    )
+                    copy.start()
+                    copies.append(copy)
+            yield
         for copy in copies:
             copy.wait()
 
@@ -895,14 +944,42 @@
     return lax.rsqrt(jnp.mean(values * values, -1, keepdims=True) + EPSILON)
 
 
+QUERY = WIDE + 2 * TURN
+ATTN_LANE, FFN_LANE = 126, 127
+
+
+def weight_buffers(weights):
+    q_weight, kv_down, kv_up, out_weight = weights
+    shapes = [(D, QUERY), kv_down.shape, kv_up.shape, out_weight.shape, (D, 128)]
+    return [pltpu.VMEM(shape, BF) for shape in shapes] + [pltpu.SemaphoreType.DMA((5,))]
+
+
+def weight_loads(sources, scratch):
+    q_weight, kv_down, kv_up, out_weight = sources
+    views = [q_weight.at[:, pl.ds(0, QUERY)], kv_down, kv_up, out_weight]
+    views.append(q_weight.at[:, pl.ds(QUERY, 128)])
+    return [
+        pltpu.make_async_copy(view, scratch[n], scratch[5].at[n]) for n, view in enumerate(views)
+    ]
+
+
+def gain_rows(router):
+    turned = router[...].astype(F32).T
+    return turned[ATTN_LANE : ATTN_LANE + 1], turned[FFN_LANE : FFN_LANE + 1]
+
+
+def kv_gain_row(kv_up):
+    return kv_up[:, pl.ds(2 * WIDE, 128)].astype(F32).T[:1]
+
+
 class AttentionForward:
-    def __init__(self, tokens, routes, allowed, tables, gains, weights, experts):
+    def __init__(self, tokens, routes, allowed, tables, weights, experts):
         count = MICRO * SEQ
         self.experts = experts
-        self.inputs = [tokens, routes, allowed, *tables, *gains, *weights]
+        self.inputs = [tokens, routes, allowed, *tables, *weights]
         vmem = pl.BlockSpec(memory_space=pltpu.VMEM)
         hbm = pl.BlockSpec(memory_space=pl.ANY)
-        self.in_specs = [vmem] * 8 + [hbm] * 5
+        self.in_specs = [vmem] * 5 + [hbm] * 4
         shapes = [
             ((count, D), BF), ((experts, count), F32),
             ((count, D), BF), ((count, WIDE), BF), ((count, 2 * TURN), BF), ((count, RANK), F32),
@@ -911,38 +988,39 @@
         ]
         self.out_shapes = [jax.ShapeDtypeStruct(shape, kind) for shape, kind in shapes]
         self.out_specs = [vmem] * len(shapes)
-        self.scratch = [pltpu.VMEM(w.shape, BF) for w in weights] + [
+        self.scratch = weight_buffers(weights) + [
             pltpu.VMEM((count, RANK + 256), F32),
             pltpu.VMEM((count, 2 * TURN), F32),
-            pltpu.SemaphoreType.DMA((5,)),
         ]
 
     def steps(self, at, ins, outs, scratch):
-        tokens, routes, allowed, cosine, sine, attn_gain, kv_gain, ffn_gain = ins[:8]
+        tokens, routes, allowed, cosine, sine = ins[:5]
         (
             hidden, gates, normed, q_plain, q_turned, kv_low, latent, k_turned, kv, chances,
             attended, residual,
         ) = outs
         q_weight, kv_down, kv_up, out_weight, router = scratch[:5]
-        kv_raw, q_raw, sem = scratch[5:]
-        yield 9
-        loads = [
-            pltpu.make_async_copy(ins[8 + n], scratch[n], sem.at[n]) for n in range(5)
-        ]
-        for n in (1, 0, 2, 3, 4):
+        kv_raw, q_raw = scratch[6:]
+        yield 16
+        loads = weight_loads(ins[5:], scratch)
+        for n in (4, 1, 0, 2, 3):
             loads[n].start()
+        loads[4].wait()
+        attn_gain, ffn_gain = gain_rows(router)
         values = tokens[...].astype(F32)
-        normed[...] = (values * rms_scale(values) * attn_gain[...]).astype(BF)
+        normed[...] = (values * rms_scale(values) * attn_gain).astype(BF)
         yield
         loads[1].wait()
 
-        @tiles(RANK + 256, 256)
+        @tiles(RANK + 256, RANK + 256)
         def _(columns):
             kv_raw[:, columns] = dot(normed[...], kv_down[:, columns])
 
         low = kv_raw[:, pl.ds(0, RANK)]
         kv_low[...] = low
-        latent[...] = (low * rms_scale(low) * kv_gain[...]).astype(BF)
+        loads[2].wait()
+        kv_gain = kv_gain_row(kv_up)
+        latent[...] = (low * rms_scale(low) * kv_gain).astype(BF)
         first, second = kv_raw[:, pl.ds(RANK, 128)], kv_raw[:, pl.ds(RANK + 128, 128)]
         c, s = cosine[:, pl.ds(0, 128)], sine[:, pl.ds(0, 128)]
         lay = spread()
@@ -951,28 +1029,23 @@
         yield
         loads[0].wait()
 
-        @tiles(WIDE, 256)
-        def _(columns):
+        for k in range(2):
+            columns = pl.ds(k * WIDE // 2, WIDE // 2)
             q_plain[:, columns] = dot(normed[...], q_weight[:, columns]).astype(BF)
-
-        yield
-        for n in range(4):
-            columns = pl.ds(n * 256, 256)
-            q_raw[:, columns] = dot(normed[...], q_weight[:, pl.ds(WIDE + n * 256, 256)])
+            yield
+        q_raw[...] = dot(normed[...], q_weight[:, pl.ds(WIDE, 2 * TURN)])
         first, second = q_raw[:, pl.ds(0, TURN)], q_raw[:, pl.ds(TURN, TURN)]
         q_turned[:, pl.ds(0, TURN)] = (first * cosine[...] - second * sine[...]).astype(BF)
         q_turned[:, pl.ds(TURN, TURN)] = (second * cosine[...] + first * sine[...]).astype(BF)
         yield
-        loads[2].wait()
-
-        @tiles(2 * WIDE, 256)
+
+        @tiles(2 * WIDE, 2048)
         def _(columns):
             kv[:, columns] = dot(latent[...], kv_up[:, columns]).astype(BF)
 
         yield
 
-        @pl.loop(0, HEADS)
-        def _(h):
+        def head(h):
             plain = pl.ds(pl.multiple_of(h * NOPE, NOPE), NOPE)
             keys = pl.ds(pl.multiple_of(h * 2 * NOPE, NOPE), NOPE)
             both = pl.ds(pl.multiple_of(h * 2 * NOPE + NOPE, NOPE), VDIM)
@@ -984,19 +1057,18 @@
             chances[h] = chance
             attended[:, plain] = dot(chance.astype(BF), kv[:, both]).astype(BF)
 
-        yield
+        for k in range(0, HEADS, 4):
+            pl.loop(k, k + 4)(head)
+            yield
         loads[3].wait()
-
-        @tiles(D, 256)
-        def _(columns):
+        for k in range(2):
+            columns = pl.ds(k * D // 2, D // 2)
             residual[:, columns] = tokens[:, columns].astype(F32) + dot(
                 attended[...], out_weight[:, columns]
             )
-
-        yield
+            yield
         values = residual[...]
-        hidden[...] = (values * rms_scale(values) * ffn_gain[...]).astype(BF)
-        loads[4].wait()
+        hidden[...] = (values * rms_scale(values) * ffn_gain).astype(BF)
         logits = dot(hidden[...], router[...])
         lane = lax.broadcasted_iota(jnp.int32, logits.shape, 1)
         chosen = lane < 0
@@ -1010,65 +1082,65 @@
 
 
 class AttentionBackward:
-    def __init__(self, cotangent, hidden_sum, gate_grad, saved, tokens, tables, gains, weights):
+    def __init__(self, cotangent, hidden_sum, gate_grad, saved, tokens, tables, weights):
         count = MICRO * SEQ
         self.experts = gate_grad.shape[0]
-        self.inputs = [cotangent, hidden_sum, gate_grad, *tables, *gains, *saved, tokens, *weights]
+        self.inputs = [cotangent, hidden_sum, gate_grad, *tables, *saved, tokens, *weights]
         vmem = pl.BlockSpec(memory_space=pltpu.VMEM)
         hbm = pl.BlockSpec(memory_space=pl.ANY)
-        self.in_specs = [vmem] * (8 + 12 + 1) + [hbm] * 5
-        self.grads = [(WIDE, D), (RANK, 2 * WIDE), (D, WIDE + 2 * TURN), (D, RANK + 256)]
+        self.in_specs = [vmem] * (5 + 12 + 1) + [hbm] * 4
+        self.grads = [weights[n].shape for n in (3, 2, 0, 1)]
         self.out_shapes = [jax.ShapeDtypeStruct(shape, BF) for shape in self.grads] + [
-            jax.ShapeDtypeStruct((count, D), BF),
-            jax.ShapeDtypeStruct((1, D), F32),
-            jax.ShapeDtypeStruct((1, RANK), F32),
-            jax.ShapeDtypeStruct((1, D), F32),
-            jax.ShapeDtypeStruct((D, 128), F32),
+            jax.ShapeDtypeStruct((count, D), BF)
         ]
-        self.out_specs = [hbm] * 4 + [vmem] * 5
-        self.scratch = [pltpu.VMEM(w.shape, BF) for w in weights] + [
-            pltpu.VMEM((2, 256, 2 * WIDE), BF),
+        self.out_specs = [hbm] * 4 + [vmem]
+        widest = max(width for _, width in self.grads)
+        self.scratch = weight_buffers(weights) + [
+            pltpu.VMEM((2, 256, widest), BF),
             pltpu.VMEM((count, 128), F32),
             pltpu.VMEM((count, D), F32),
             pltpu.VMEM((count, D), F32),
             pltpu.VMEM((count, D), BF),
             pltpu.VMEM((count, WIDE), BF),
-            pltpu.VMEM((count, WIDE + 2 * TURN), BF),
+            pltpu.VMEM((count, QUERY), BF),
             pltpu.VMEM((count, 2 * WIDE), BF),
             pltpu.VMEM((count, RANK + 256), BF),
             pltpu.VMEM((count, 2 * TURN), F32),
             pltpu.VMEM((count, 2 * TURN), F32),
-            pltpu.SemaphoreType.DMA((5,)),
+            pltpu.VMEM((D, 128), F32),
+            pltpu.VMEM((128, D), F32),
+            pltpu.VMEM((128, RANK), F32),
             pltpu.SemaphoreType.DMA((2,)),
         ]
 
     def steps(self, at, ins, outs, scratch):
-        cotangent, hidden_sum, gate_grad, cosine, sine, attn_gain, kv_gain, ffn_gain = ins[:8]
+        cotangent, hidden_sum, gate_grad, cosine, sine = ins[:5]
         (
             hidden, gates, normed, q_plain, q_turned, kv_low, latent, k_turned, kv, chances,
             attended, residual,
-        ) = ins[8:20]
-        tokens_grad, attn_gain_grad, kv_gain_grad, ffn_gain_grad, router_grad = outs[4:]
+        ) = ins[5:17]
+        tokens, tokens_grad = ins[17], outs[4]
         q_weight, kv_down, kv_up, out_weight, router = scratch[:5]
         (
             buffers, turned_gates, hidden_grad, residual_grad, mixed, attended_grad, q_grad, kv_grad,
-            kv_raw_grad, q_turn_grad, k_turn_grad, sem, out_sem,
-        ) = scratch[5:]
+            kv_raw_grad, q_turn_grad, k_turn_grad, router_grad, gain_grads, kv_gain_grads, out_sem,
+        ) = scratch[6:]
         experts = self.experts
-        yield 4 + sum(shape[0] // 256 for shape in self.grads)
-        loads = [
-            pltpu.make_async_copy(ins[21 + n], scratch[n], sem.at[n]) for n in range(5)
-        ]
+        yield 7 + sum(shape[0] // 256 for shape in self.grads)
+        loads = weight_loads(ins[18:], scratch)
         for n in (4, 3, 2, 0, 1):
             loads[n].start()
+        gain_grads[...] = jnp.zeros_like(gain_grads)
+        kv_gain_grads[...] = jnp.zeros_like(kv_gain_grads)
         share = jnp.maximum(gates[...], 0.0)
         inner = jnp.sum(share * gate_grad[...], 0, keepdims=True)
         turned_gates[...] = jnp.zeros_like(turned_gates)
         turned_gates[pl.ds(0, experts), :] = share * (gate_grad[...] - inner)
         logit_grad = turned_gates[...].T.astype(BF)
         loads[4].wait()
-
-        @tiles(D, 256)
+        attn_gain, ffn_gain = gain_rows(router)
+
+        @tiles(D, 1024)
         def _(columns):
             router_grad[columns, :] = t_dot(hidden[:, columns], logit_grad)
             hidden_grad[:, columns] = hidden_sum[:, columns] + dot_t(
@@ -1082,14 +1154,16 @@
             gain_grad = jnp.sum(gradient * values * scale, 0, keepdims=True)
             return scale * weighted - values * (scale * scale * scale * mean), gain_grad
 
-        part, ffn_gain_grad[...] = norm_back(residual[...], ffn_gain[...], hidden_grad[...])
+        part, gain_grads[pl.ds(FFN_LANE, 1), :] = norm_back(
+            residual[...], ffn_gain, hidden_grad[...]
+        )
         total = cotangent[...].astype(F32) + part
         residual_grad[...] = total
         mixed[...] = total.astype(BF)
         yield
         loads[3].wait()
 
-        @tiles(WIDE, 256)
+        @tiles(WIDE, 1024)
         def _(columns):
             attended_grad[:, columns] = dot_t(mixed[...], out_weight[columns, :]).astype(BF)
 
@@ -1097,8 +1171,8 @@
         turn = [0]
         stores = {}
 
-        def weight_grad(n, left, right):
-            rows, width = self.grads[n]
+        def weight_grad(n, left, right, width, beside=None):
+            rows, whole = self.grads[n]
             for k in range(rows // 256):
                 slot = turn[0] % 2
                 turn[0] += 1
@@ -1106,22 +1180,27 @@
                     stores[slot].wait()
                 piece = pl.ds(k * 256, 256)
 
-                @tiles(width, 256)
+                @tiles(width, width if width < 1024 else 1024)
                 def _(columns):
                     buffers[slot, :, columns] = t_dot(left[:, piece], right[:, columns]).astype(BF)
 
+                if beside is not None:
+                    lanes = beside[k * 256 : (k + 1) * 256, :]
+                    buffers[slot, :, pl.ds(width, 128)] = lanes.astype(BF)
+                if whole > width + 128:
+                    rest = pl.ds(width + 128, whole - width - 128)
+                    buffers[slot, :, rest] = jnp.zeros((256, whole - width - 128), BF)
                 stores[slot] = pltpu.make_async_copy(
-                    buffers.at[slot, :, pl.ds(0, width)], outs[n].at[piece, :], out_sem.at[slot]
+                    buffers.at[slot, :, pl.ds(0, whole)], outs[n].at[piece, :], out_sem.at[slot]
                 )
                 stores[slot].start()
                 yield
 
-        yield from weight_grad(0, attended, mixed)
+        yield from weight_grad(0, attended, mixed, D)
         q_turn_grad[...] = jnp.zeros_like(q_turn_grad)
         k_turn_grad[...] = jnp.zeros_like(k_turn_grad)
 
-        @pl.loop(0, HEADS)
-        def _(h):
+        def head(h):
             plain = pl.ds(pl.multiple_of(h * NOPE, NOPE), NOPE)
             keys = pl.ds(pl.multiple_of(h * 2 * NOPE, NOPE), NOPE)
             both = pl.ds(pl.multiple_of(h * 2 * NOPE + NOPE, NOPE), VDIM)
@@ -1138,7 +1217,9 @@
             q_turn_grad[...] += jnp.where(mine, dot(score_grad, k_turned[...]), 0.0) * SCALE
             k_turn_grad[...] += t_dot(score_grad, turned) * SCALE
 
-        yield
+        for k in range(0, HEADS, 4):
+            pl.loop(k, k + 4)(head)
+            yield
         first, second = q_turn_grad[:, pl.ds(0, TURN)], q_turn_grad[:, pl.ds(TURN, TURN)]
         c, s = cosine[...], sine[...]
         q_grad[:, pl.ds(WIDE, TURN)] = (first * c + second * s).astype(BF)
@@ -1156,26 +1237,29 @@
         kv_raw_grad[:, pl.ds(RANK, 128)] = (first * c + second * s).astype(BF)
         kv_raw_grad[:, pl.ds(RANK + 128, 128)] = (second * c - first * s).astype(BF)
         loads[2].wait()
-        latent_grad = dot_t(kv_grad[...], kv_up[...])
-        part, kv_gain_grad[...] = norm_back(kv_low[...], kv_gain[...], latent_grad)
+        latent_grad = dot_t(kv_grad[...], kv_up[:, pl.ds(0, 2 * WIDE)])
+        part, kv_gain_grads[pl.ds(0, 1), :] = norm_back(
+            kv_low[...], kv_gain_row(kv_up), latent_grad
+        )
         kv_raw_grad[:, pl.ds(0, RANK)] = part.astype(BF)
-        yield from weight_grad(1, latent, kv_grad)
-        yield from weight_grad(2, normed, q_grad)
-        yield from weight_grad(3, normed, kv_raw_grad)
         loads[0].wait()
         loads[1].wait()
 
-        @tiles(D, 256)
+        @tiles(D, 512)
         def _(columns):
             hidden_grad[:, columns] = dot_t(q_grad[...], q_weight[columns, :]) + dot_t(
                 kv_raw_grad[...], kv_down[columns, :]
             )
 
-        part, attn_gain_grad[...] = norm_back(
-            ins[20][...].astype(F32), attn_gain[...], hidden_grad[...]
+        yield
+        part, gain_grads[pl.ds(ATTN_LANE, 1), :] = norm_back(
+            tokens[...].astype(F32), attn_gain, hidden_grad[...]
         )
         tokens_grad[...] = (residual_grad[...] + part).astype(BF)
-        yield
+        router_grad[...] += gain_grads[...].T
+        yield from weight_grad(1, latent, kv_grad, 2 * WIDE, kv_gain_grads[...].T)
+        yield from weight_grad(2, normed, q_grad, QUERY, router_grad)
+        yield from weight_grad(3, normed, kv_raw_grad, RANK + 256)
         for store in stores.values():
             store.wait()
 
@@ -1452,26 +1536,6 @@
     return lax.dot_general(left, right, (((0,), (0,)), ((), ())), preferred_element_type=F32)
 
 
-def pack(parts, rows):
-    flat = jnp.concatenate([part.reshape(rows, -1) for part in parts], 1)
-    width = -(-flat.shape[1] // 2048) * 2048
-    flat = jnp.pad(flat, ((0, 0), (0, width - flat.shape[1])))
-    return flat.reshape(rows, width // 128, 128)
-
-
-def unpack(block, shapes):
-    rows = block.shape[0]
-    flat = block.reshape(rows, -1)
-    parts, first = [], 0
-    for shape in shapes:
-        size = 1
-        for extent in shape:
-            size *= extent
-        parts.append(flat[:, first : first + size].reshape((rows,) + shape))
-        first += size
-    return parts
-
-
 def plain_weight_grads(grid, kept, extent):
     me = lax.axis_index("dp")
     peers = grid.size["p"]
@@ -1527,11 +1591,21 @@
 
     rows = q_weight.shape[0]
     q_heads = q_weight.reshape(rows, HEADS, NOPE + ROPE)
+    beside = jnp.concatenate(
+        [
+            router,
+            jnp.zeros((rows, ATTN_LANE - experts), BF),
+            attn_gain[:, None],
+            ffn_gain[:, None],
+        ],
+        1,
+    )
     q_sent = jnp.concatenate(
         [
             q_heads[:, :, :NOPE].reshape(rows, WIDE),
             q_heads[:, :, NOPE : NOPE + HALF].reshape(rows, TURN),
             q_heads[:, :, NOPE + HALF :].reshape(rows, TURN),
+            beside,
         ],
         1,
     )
@@ -1539,10 +1613,25 @@
     down_sent = jnp.concatenate(
         [kv_down[:, : RANK + HALF], gap, kv_down[:, RANK + HALF :], gap], 1
     )
-    small_shapes = (attn_gain.shape, ffn_gain.shape, kv_gain.shape, router.shape)
-    small = pack([attn_gain[None], ffn_gain[None], kv_gain[None], router[None]], 1)[0]
-    up_shape = kv_up.shape
-    up_sent = kv_up if up_shape[0] % 16 == 0 else kv_up.reshape(16, -1)
+    up_rows = kv_up.shape[0]
+    up_room = 128 * max(1, 16 // up_rows)
+    up_wide = jnp.concatenate(
+        [kv_up, kv_gain[:, None], jnp.zeros((up_rows, up_room - 1), BF)], 1
+    )
+    up_sent = up_wide if up_rows % 16 == 0 else up_wide.reshape(16, -1)
+
+    share = shared_gate.shape[1] // devices
+    room = -(-share // 128) * 128
+    shared_sent = jnp.concatenate(
+        [
+            jnp.pad(
+                half.reshape(rows, devices, share).transpose(1, 0, 2),
+                ((0, 0), (0, 0), (0, room - share)),
+            )
+            for half in (shared_gate, shared_up)
+        ],
+        2,
+    )
     first, second, third = ("q", "r", "p"), ("q", "p", "r"), ("p", "q", "r")
 
     def columns_of(ref, peer, step):
@@ -1556,28 +1645,25 @@
         [
             Gather(
                 grid,
-                [q_sent, down_sent, up_sent, out_weight, small],
+                [q_sent, down_sent, up_sent, out_weight],
                 [
                     (0, 0, q_sent.shape[1], third),
                     (1, 0, down_sent.shape[1], third),
                     (2, 0, up_sent.shape[1], ("r", "p", "q")),
-                    (3, 0, out_weight.shape[1], first),
-                    (4, 0, 128, first),
+                    (3, 0, D // 2, first),
+                    (3, D // 2, D // 2, second),
                 ],
             ),
-            Exchange(grid, own[:2], [columns_of] * 2, [(extent, window)] * 2),
+            Exchange(grid, own[:2], [columns_of] * 2, [(extent, window)] * 2, (2, 5)),
         ],
         0,
         "gather_attention",
     )
-    parts = unpack(gathered[4], small_shapes)
-    gains = [parts[n].reshape(1, -1).astype(F32) for n in (0, 2, 1)]
     weights = [
         gathered[0].reshape(D, -1),
         gathered[1].reshape(D, -1),
         gathered[2].reshape(RANK, -1),
         gathered[3].reshape(-1, D),
-        jnp.pad(parts[3].reshape(D, experts), ((0, 0), (0, 128 - experts))),
     ]
 
     token_rows = tokens.reshape(count, D)
@@ -1590,41 +1676,29 @@
     def half_orders(a):
         return [(a, 0, D // 2, first), (a, D // 2, D // 2, second)]
 
-    (grad_first,), saved, windows_down = together(
+    (grad_first,), saved, windows_down, (shared_in,) = together(
         grid,
         [
-            Gather(grid, [grad_out[:SEQ]], [(0, 0, D // 2, third), (0, D // 2, D // 2, second)]),
+            Gather(
+                grid, [grad_out[:SEQ]], [(0, 0, 1536, third), (0, 1536, 512, ("p", "r", "q"))]
+            ),
             AttentionForward(
                 token_rows,
                 routes.reshape(count, TOP),
                 allowed.astype(F32),
                 tables,
-                gains,
                 weights,
                 experts,
             ),
-            Exchange(grid, own[2:], [rows_of], [(window, extent)]),
+            Exchange(grid, own[2:], [rows_of], [(window, extent)], (2,)),
+            AllToAll(grid, shared_sent),
         ],
         6,
         "attention_forward",
     )
     hidden, dense_gates, residual = saved[0], saved[1], saved[11]
 
-    share = shared_gate.shape[1] // devices
-    both = jnp.concatenate(
-        [shared_gate.reshape(-1, devices, share), shared_up.reshape(-1, devices, share)], 2
-    )
-    shared_in = lax.all_to_all(
-        both.transpose(1, 0, 2), ("dp", "expert"), split_axis=0, concat_axis=0, tiled=True
-    ).reshape(D, 2 * share)
-    room = -(-share // 128) * 128
-    shared_in = jnp.concatenate(
-        [
-            jnp.pad(shared_in[:, :share], ((0, 0), (0, room - share))),
-            jnp.pad(shared_in[:, share:], ((0, 0), (0, room - share))),
-        ],
-        1,
-    )
+    shared_in = shared_in.reshape(D, 2 * room)
     shared_part = jnp.pad(shared_down, ((0, room - share), (0, 0)))
 
     half = D // 2
@@ -1722,11 +1796,11 @@
     def sent_to(ref, peer, step):
         return ref.at[step - 1]
 
-    attention_grads, (got_ab, got_down) = together(
+    attention_grads, (got_ab, got_down), (shared_back,) = together(
         grid,
         [
             AttentionBackward(
-                grad_out, hidden_sum, gate_grad, saved, token_rows, tables, gains, weights
+                grad_out, hidden_sum, gate_grad, saved, token_rows, tables, weights
             ),
             Exchange(
                 grid,
@@ -1734,27 +1808,13 @@
                 [sent_to] * 2,
                 [(extent, 2 * window), (window, extent)],
             ),
+            AllToAll(grid, shared_in_grad.reshape(devices, -1, 2 * room)),
         ],
         7,
         "attention_backward",
     )
-    (
-        out_weight_grad, kv_up_grad, q_weight_grad, kv_down_grad, tokens_grad, attn_gain_grad,
-        kv_gain_grad, ffn_gain_grad, router_grad,
-    ) = attention_grads
+    out_weight_grad, kv_up_grad, q_weight_grad, kv_down_grad, tokens_grad = attention_grads
     shared_down_grad = shared_down_grad[:share]
-    shared_in_grad = jnp.concatenate(
-        [shared_in_grad[:, :share], shared_in_grad[:, room : room + share]], 1
-    )
-    small_grads = pack(
-        [
-            attn_gain_grad.reshape(devices, -1),
-            ffn_gain_grad.reshape(devices, -1),
-            kv_gain_grad.reshape(devices, -1),
-            router_grad[:, :experts].reshape(devices, -1),
-        ],
-        devices,
-    )
 
     def halves(a, columns):
         part = columns // 256 * 128
@@ -1767,14 +1827,12 @@
             kv_down_grad.reshape((devices,) + down_sent.shape),
             kv_up_grad.reshape((devices,) + up_sent.shape),
             out_weight_grad.reshape((devices,) + out_weight.shape),
-            small_grads,
         ],
         halves(0, q_sent.shape[1])
         + halves(1, down_sent.shape[1])
         + halves(2, up_sent.shape[1])
-        + halves(3, out_weight.shape[1])
-        + [(4, 0, 128, ("p", "r"))],
-        [[3], [2, 1], [0, 4]],
+        + halves(3, out_weight.shape[1]),
+        [[3], [2, 1], [0]],
     )
     experts_grads = Assemble(
         grid,
@@ -1784,15 +1842,16 @@
         [got_down[step] for step in range(dp_size - 1)],
         eff,
     )
-    (q_sum, down_sum, up_sum, out_weight_sum, small_sum), experts_grads = together(
+    (q_sum, down_sum, up_sum, out_weight_sum), experts_grads = together(
         grid, [attention_sums, experts_grads], 5, "scatter_attention_assemble"
     )
-    small_sums = unpack(small_sum[None], small_shapes)
+    up_sum = up_sum.reshape(up_rows, -1)
+    beside_sum = q_sum[:, QUERY:]
     q_sum = jnp.concatenate(
         [
             q_sum[:, :WIDE].reshape(rows, HEADS, NOPE),
             q_sum[:, WIDE : WIDE + TURN].reshape(rows, HEADS, HALF),
-            q_sum[:, WIDE + TURN :].reshape(rows, HEADS, HALF),
+            q_sum[:, WIDE + TURN : QUERY].reshape(rows, HEADS, HALF),
         ],
         2,
     ).reshape(q_weight.shape)
@@ -1800,25 +1859,20 @@
         [down_sum[:, : RANK + HALF], down_sum[:, RANK + 128 : RANK + 128 + HALF]], 1
     )
 
-    shared_back = lax.all_to_all(
-        shared_in_grad.reshape(devices, -1, 2 * share),
-        ("dp", "expert"), split_axis=0, concat_axis=0, tiled=True,
-    ).astype(F32)
-    shared_back = shared_back.transpose(1, 0, 2)
+    shared_back = shared_back.astype(F32).transpose(1, 0, 2)
     shared_gate_grad = shared_back[:, :, :share].reshape(shared_gate.shape)
-    shared_up_grad = shared_back[:, :, share:].reshape(shared_up.shape)
-
+    shared_up_grad = shared_back[:, :, room : room + share].reshape(shared_up.shape)
     return (
         result.astype(BF).reshape(tokens.shape),
         tokens_grad.reshape(tokens.shape),
-        small_sums[0].reshape(-1),
+        beside_sum[:, ATTN_LANE],
         q_sum,
         down_sum,
-        small_sums[2].reshape(-1),
-        up_sum.reshape(up_shape),
+        up_sum[:, 2 * WIDE],
+        up_sum[:, : 2 * WIDE],
         out_weight_sum,
-        small_sums[1].reshape(-1),
-        small_sums[3].reshape(router.shape),
+        beside_sum[:, FFN_LANE],
+        beside_sum[:, :experts],
         shared_gate_grad,
         shared_up_grad,
         shared_down_grad,

time: 976 us -> 913 us (0.935)
  Pallas kernels: 878 us -> 829 us
  starting transfers between devices: 10.2 us -> 0 us
    pallas_call x8, Pallas kernels: 878 us -> 829 us  [together(): pl.pallas_call(kernel, out_shape=[shape for part in parts for shape in pa...]
    all_to_all x2 -> x0, starting transfers between devices: 10.2 us -> none  [the longest x1 5.94 us: body(): lax.all_to_all(both.transpose(1, 0, 2), ('dp', 'expert'), split_axis=0, c...]
  transfers between devices with their start and end apart: 2 -> 0, of which waited for: 0 -> 0; matrix products, arithmetic and copies ran while one was open for 4% -> 0% of each run, Pallas kernels for 55% -> 0%
where the time goes in v3:
time: 913 us; the launch traced here: 903 us
  Pallas kernels  829 us (91%)
  local copies, waits for them, and re-layouts  58.2 us (6%)
  other arithmetic  14.5 us (2%)
    pallas_call x8, Pallas kernels, together(): pl.pallas_call(kernel, out_shape=[shape for part in parts for shape in pa...  829 us
    unnamed x38, local copies, waits for them, and re-layouts  19.2 us

profile of v3, /device:TPU:16, one launch (start us, length us, event | category | flops | bytes accessed | tf_op | source)
XLA Modules:
  0.0 902.9 jit_solution(10008732646490388008)
XLA Ops:
  1.2 1.3 reduce.17
  7.2 1.6 pad_maximum_fusion.3.refs_1_
  8.8 1.4 copy.44
  10.2 1.7 concatenate.29.refs_2_
  11.9 1.6 reshape.206
  17.6 1.3 reshape.215
  21.4 135.4 %gather_attention.1 = (bf16[32,64,3200]{2,1,0:T(8,128)(2,1)}, bf16[32,64,768]{2,1,0:T(8,128)(2,1)}, bf16[32,16,4224]{2,1,0:T(8,128)(2,1)}, bf16[32,64,2048]{2,1,...) custom-call(bf16[64,3200]{1,0:T(8,128)(2,1)} %concatenate.27.refs_0_, ...), custom_call_target="tpu_custom_call" | custom-call | tf_op jit(solution)/shard_map/gather_attention/pallas_call | solution.py:520
  156.8 81.0 %attention_forward.1 = (bf16[32,64,2048]{2,1,0:T(8,128)(2,1)}, bf16[128,2048]{1,0:T(8,128)(2,1)}, f32[16,128]{1,0:T(8,128)}, bf16[128,2048]{1,0:T(8,128)(2,1)}, ...) custom-call(bf16[64,2048]{1,0:T(8,128)(2,1)} %get-tuple-element.199., ...), custom_call_target="tpu_custom_call" | custom-call | tf_op jit(solution)/shard_map/attention_forward/pallas_call | solution.py:520
  237.7 1.4 fusion.12
  239.2 1.9 fusion.10
  241.1 44.5 %gather_first.1 = (bf16[32,64,2048]{2,1,0:T(8,128)(2,1)}, f32[32,16,64]{2,1,0:T(8,128)}) custom-call(bf16[64,2048]{1,0:T(8,128)(2,1)} %get-tuple-element.196.refs_0_, f32[16,64]{1,0:T(8,128)} %get-tuple-element.202.refs_1_), custom_call_target="tpu_custom_call" | custom-call | tf_op jit(solution)/shard_map/gather_first/pallas_call | solution.py:520
  287.2 96.6 %gather_second_experts_first.1 = (bf16[32,64,2048]{2,1,0:T(8,128)(2,1)}, f32[32,16,64]{2,1,0:T(8,128)}, bf16[32,64,2048]{2,1,0:T(8,128)(2,1)}, bf16[2048,2048]{1...) custom-call(bf16[64,2048]{1,0:T(8,128)(2,1)} %get-tuple-element.197., ...), custom_call_target="tpu_custom_call" | custom-call | tf_op jit(solution)/shard_map/gather_second_experts_first/pallas_call | solution.py:520
  387.0 97.6 %scatter_first_experts_second.1 = (f32[64,2048]{1,0:T(8,128)}, f32[16,64]{1,0:T(8,128)}, f32[64,2048]{1,0:T(8,128)}, bf16[2048,2048]{1,0:T(8,128)(2,1)}, bf16[20...) custom-call(bf16[32,64,2048]{2,1,0:T(8,128)(2,1)} %bitcast.88, ...), custom_call_target="tpu_custom_call" | custom-call | tf_op jit(solution)/shard_map/scatter_first_experts_second/pallas_call | solution.py:520
  486.2 100.3 %scatter_second_weight_grads.1 = (f32[64,2048]{1,0:T(8,128)}, f32[16,64]{1,0:T(8,128)}, f32[64,2048]{1,0:T(8,128)}, f32[1024,1536]{1,0:T(8,128)}, f32[768,1024]{...) custom-call(bf16[32,64,2048]{2,1,0:T(8,128)(2,1)} %bitcast.86, ...), custom_call_target="tpu_custom_call" | custom-call | tf_op jit(solution)/shard_map/scatter_second_weight_grads/pallas_call | solution.py:520
  586.5 1.4 pad_maximum_fusion.4.refs_2_
  587.9 2.0 fusion.3
  589.8 2.3 pad_maximum_fusion.refs_1_
  592.1 124.5 %attention_backward.1 = (bf16[2048,2048]{1,0:T(8,128)(2,1)}, bf16[512,4224]{1,0:T(8,128)(2,1)}, bf16[2048,3200]{1,0:T(8,128)(2,1)}, bf16[2048,768]{1,0:T(8,128)(...) custom-call(bf16[128,2048]{1,0:T(8,128)(2,1)} %bitcast.105, ...), custom_call_target="tpu_custom_call" | custom-call | tf_op jit(solution)/shard_map/attention_backward/pallas_call | solution.py:520
  716.6 149.1 %scatter_attention_assemble.1 = (f32[64,3200]{1,0:T(8,128)}, f32[64,768]{1,0:T(8,128)}, f32[16,4224]{1,0:T(8,128)}, f32[64,2048]{1,0:T(8,128)}, f32[1024,1408]{1...) custom-call(bf16[32,64,3200]{2,1,0:T(8,128)(2,1)} %bitcast.83, bf16[32,64,768]{2,1,0:T(8,128)(2,1)} %bitcast.101, ...), custom_call_target="tpu_custom_call" | custom-call | tf_op jit(solution)/shard_map/scatter_attention_assemble/pallas_call | solution.py:520
  865.7 1.3 slice_reduce_fusion.2
  867.0 1.7 slice.102
  868.7 1.5 slice_reduce_fusion
  877.4 1.3 reshape.238
  878.7 2.0 slice.107
  880.7 1.5 convert_bitcast_fusion
  883.9 1.4 reshape.240
  885.4 1.8 copy.59
  887.2 1.4 reshape.239
  889.4 2.5 copy.78
  891.9 5.7 copy.79
  897.6 2.5 copy.80
  900.1 2.5 copy.81
  (76 shorter events, 27.7 us)
Async XLA Ops:
  0.6 14.8 %copy-start.6 = (bf16[88,2048]{1,0:T(8,128)(2,1)S(1)}, bf16[88,2048]{1,0:T(8,128)(2,1)}, u32[]{:S(2)}) copy-start(bf16[88,2048]{1,0:T(8,128)(2,1)} %param.34) | copy-start | bytes 1081348
  10.2 6.1 copy-start.4
  13.5 4.0 copy-start.5
  16.3 4.2 copy-start.1
  486.2 100.3 %copy-start.7 = (f32[16,64]{1,0:T(8,128)S(1)}, f32[16,64]{1,0:T(8,128)}, u32[]{:S(2)}) copy-start(f32[16,64]{1,0:T(8,128)} %get-tuple-element.126) | copy-start | bytes 12292
  486.2 101.7 %copy-start = (f32[128,2048]{1,0:T(8,128)S(1)}, f32[128,2048]{1,0:T(8,128)}, u32[]{:S(2)}) copy-start(f32[128,2048]{1,0:T(8,128)} %get-tuple-element.91.refs_16_) | copy-start | bytes 3145732
  486.2 101.7 %copy-start.2 = (f32[64,2048]{1,0:T(8,128)S(1)}, f32[64,2048]{1,0:T(8,128)}, u32[]{:S(2)}) copy-start(f32[64,2048]{1,0:T(8,128)} %get-tuple-element.107) | copy-start | bytes 1572868
  882.1 15.4 %slice-start.2 = ((s8[5767168]{0:T(1024)(128)(4,1)}), s8[1572864]{0:T(1024)(128)(4,1)S(1)}, s32[]{:S(2)}) async-start(s8[5767168]{0:T(1024)(128)(4,1)} %bitcast.94), calls=%async_computation.2 | async-start | bytes 3145728
  883.9 4.7 copy-start.3
  888.6 8.9 slice-start.3
  891.9 8.2 slice-start
  897.6 2.5 slice-start.1

commit v4 on v3

--- a/solution.py
+++ b/solution.py
@@ -884,6 +884,64 @@
             pltpu.make_async_copy(back, back, recv_sem.at[step]).wait()
 
 
+def chosen_lanes(height, shift, share):
+    row = lax.broadcasted_iota(jnp.int32, (height, 128), 0)
+    lane = lax.broadcasted_iota(jnp.int32, (height, 128), 1)
+    return jnp.logical_and(row - lane == shift, lane < share).astype(BF)
+
+
+class SharedColumns:
+    def __init__(self, arrays, devices):
+        rows, self.width = arrays[0].shape
+        self.devices, self.share = devices, self.width // devices
+        vmem = pl.BlockSpec(memory_space=pltpu.VMEM)
+        self.inputs = list(arrays)
+        self.in_specs = [vmem] * len(arrays)
+        self.out_shapes = [jax.ShapeDtypeStruct((devices, rows, 128 * len(arrays)), BF)]
+        self.out_specs = [vmem]
+        self.scratch = []
+
+    def steps(self, at, ins, outs, scratch):
+        share = self.share
+        yield self.devices
+        for k in range(self.devices):
+            first = share * k // 128 * 128
+            width = min(256, self.width - first)
+            lanes = chosen_lanes(width, share * k - first, share)
+            for n, array in enumerate(ins):
+                outs[0][k, :, pl.ds(128 * n, 128)] = dot(
+                    array[:, pl.ds(first, width)], lanes
+                ).astype(BF)
+            yield
+
+
+class SharedRows:
+    def __init__(self, array, width):
+        devices, rows, lanes = array.shape
+        self.devices, self.width, self.share = devices, width, width // devices
+        vmem = pl.BlockSpec(memory_space=pltpu.VMEM)
+        self.inputs, self.in_specs = [array], [vmem]
+        self.out_shapes = [jax.ShapeDtypeStruct((rows, width), F32)] * (lanes // 128)
+        self.out_specs = [vmem] * (lanes // 128)
+        self.scratch = []
+
+    def steps(self, at, ins, outs, scratch):
+        share = self.share
+        yield self.width // 128
+        for w in range(self.width // 128):
+            totals = [None] * len(outs)
+            for k in range(128 * w // share, (128 * w + 127) // share + 1):
+                row = lax.broadcasted_iota(jnp.int32, (128, 128), 0)
+                lane = lax.broadcasted_iota(jnp.int32, (128, 128), 1)
+                place = jnp.logical_and(row - lane == 128 * w - share * k, row < share).astype(BF)
+                for n in range(len(outs)):
+                    term = dot(ins[0][k, :, pl.ds(128 * n, 128)], place)
+                    totals[n] = term if totals[n] is None else totals[n] + term
+            for out, total in zip(outs, totals):
+                out[:, pl.ds(128 * w, 128)] = total
+            yield
+
+
 class Exchange:
     def __init__(self, grid, arrays, views, shapes, begins=(0, 0)):
         self.grid, self.views, self.begins = grid, views, begins
@@ -1082,18 +1140,19 @@
 
 
 class AttentionBackward:
-    def __init__(self, cotangent, hidden_sum, gate_grad, saved, tokens, tables, weights):
+    def __init__(self, cotangent, hidden_sum, gate_grad, out_sums, saved, tokens, tables, weights):
         count = MICRO * SEQ
         self.experts = gate_grad.shape[0]
-        self.inputs = [cotangent, hidden_sum, gate_grad, *tables, *saved, tokens, *weights]
+        self.inputs = [cotangent, hidden_sum, gate_grad, *tables, *saved, tokens, *out_sums]
+        self.inputs += weights
         vmem = pl.BlockSpec(memory_space=pltpu.VMEM)
         hbm = pl.BlockSpec(memory_space=pl.ANY)
-        self.in_specs = [vmem] * (5 + 12 + 1) + [hbm] * 4
+        self.in_specs = [vmem] * (5 + 12 + 1 + MICRO) + [hbm] * 4
         self.grads = [weights[n].shape for n in (3, 2, 0, 1)]
         self.out_shapes = [jax.ShapeDtypeStruct(shape, BF) for shape in self.grads] + [
             jax.ShapeDtypeStruct((count, D), BF)
-        ]
-        self.out_specs = [hbm] * 4 + [vmem]
+        ] * 2
+        self.out_specs = [hbm] * 4 + [vmem] * 2
         widest = max(width for _, width in self.grads)
         self.scratch = weight_buffers(weights) + [
             pltpu.VMEM((2, 256, widest), BF),
@@ -1119,7 +1178,7 @@
             hidden, gates, normed, q_plain, q_turned, kv_low, latent, k_turned, kv, chances,
             attended, residual,
         ) = ins[5:17]
-        tokens, tokens_grad = ins[17], outs[4]
+        tokens, (tokens_grad, result) = ins[17], outs[4:]
         q_weight, kv_down, kv_up, out_weight, router = scratch[:5]
         (
             buffers, turned_gates, hidden_grad, residual_grad, mixed, attended_grad, q_grad, kv_grad,
@@ -1127,9 +1186,12 @@
         ) = scratch[6:]
         experts = self.experts
         yield 7 + sum(shape[0] // 256 for shape in self.grads)
-        loads = weight_loads(ins[18:], scratch)
+        loads = weight_loads(ins[18 + MICRO :], scratch)
         for n in (4, 3, 2, 0, 1):
             loads[n].start()
+        for k in range(MICRO):
+            piece = pl.ds(k * SEQ, SEQ)
+            result[piece, :] = (residual[piece, :] + ins[18 + k][...]).astype(BF)
         gain_grads[...] = jnp.zeros_like(gain_grads)
         kv_gain_grads[...] = jnp.zeros_like(kv_gain_grads)
         share = jnp.maximum(gates[...], 0.0)
@@ -1536,6 +1598,129 @@
     return lax.dot_general(left, right, (((0,), (0,)), ((), ())), preferred_element_type=F32)
 
 
+PIECES = 4
+
+
+def finish_kernel(copied, experts, *refs):
+    q_sum, down_sum, up_sum = refs[:3]
+    sources = refs[3 : 3 + copied]
+    q_out, down_out, up_out, gains_out, kv_gain_out, router_out = refs[3 + copied : 9 + copied]
+    targets = refs[9 + copied : 9 + 2 * copied]
+    held = refs[9 + 2 * copied : 9 + 3 * copied]
+    in_sem, out_sem = refs[9 + 3 * copied :]
+    arriving, leaving = [], []
+    for n, source in enumerate(sources):
+        part = source.shape[0] // PIECES
+        for k in range(PIECES):
+            piece = pl.ds(k * part, part)
+            into = pltpu.make_async_copy(source.at[piece, :], held[n].at[piece, :], in_sem.at[n, k])
+            into.start()
+            arriving.append(into)
+            leaving.append(
+                pltpu.make_async_copy(
+                    held[n].at[piece, :], targets[n].at[piece, :], out_sem.at[n, k]
+                )
+            )
+    for h in range(0, HEADS, 2):
+        pieces = []
+        for head in (h, h + 1):
+            pieces.append(q_sum[:, head * NOPE : (head + 1) * NOPE])
+            for half in range(2):
+                first = WIDE + half * TURN + head * HALF
+                pieces.append(q_sum[:, first : first + HALF])
+        width = 2 * (NOPE + ROPE)
+        q_out[:, pl.ds(h * (NOPE + ROPE), width)] = jnp.concatenate(pieces, 1)
+    down_out[...] = jnp.concatenate(
+        [down_sum[:, : RANK + HALF], down_sum[:, RANK + 128 : RANK + 128 + HALF]], 1
+    )
+    up_out[...] = up_sum[:, : 2 * WIDE]
+    beside = q_sum[:, QUERY:].T
+    gains_out[...] = beside[ATTN_LANE:]
+    router_out[...] = beside[:experts]
+    kv_gain_out[...] = up_sum[:, 2 * WIDE : 2 * WIDE + 128].T[:1]
+    for into, out in zip(arriving, leaving):
+        into.wait()
+        out.start()
+    for out in leaving:
+        out.wait()
+
+
+def finished(q_sum, down_sum, up_sum, plain, experts):
+    rows, up_rows = q_sum.shape[0], up_sum.shape[0]
+    vmem = pl.BlockSpec(memory_space=pltpu.VMEM)
+    hbm = pl.BlockSpec(memory_space=pl.ANY)
+    shapes = [
+        (rows, HEADS * (NOPE + ROPE)), (rows, RANK + ROPE), (up_rows, 2 * WIDE), (2, rows),
+        (1, up_rows), (experts, rows),
+    ]
+    return pl.pallas_call(
+        functools.partial(finish_kernel, len(plain), experts),
+        out_shape=[jax.ShapeDtypeStruct(shape, F32) for shape in shapes]
+        + [jax.ShapeDtypeStruct(array.shape, array.dtype) for array in plain],
+        in_specs=[vmem] * 3 + [hbm] * len(plain),
+        out_specs=[vmem] * 6 + [hbm] * len(plain),
+        scratch_shapes=[pltpu.VMEM(array.shape, array.dtype) for array in plain]
+        + [pltpu.SemaphoreType.DMA((len(plain), PIECES))] * 2,
+        compiler_params=pltpu.CompilerParams(vmem_limit_bytes=62 * 2**20),
+        name="finish",
+    )(q_sum, down_sum, up_sum, *plain)
+
+
+def prepare_kernel(q_weight, kv_down, kv_up, router, gains, kv_gain, shared_down, q_out, down_out, up_out, shared_out):
+    rows = q_weight.shape[0]
+    values = q_weight[...].astype(F32)
+    head = NOPE + ROPE
+    for h in range(0, HEADS, 2):
+        pair = [values[:, k * head : k * head + NOPE] for k in (h, h + 1)]
+        q_out[:, pl.ds(h * NOPE, 2 * NOPE)] = jnp.concatenate(pair, 1).astype(BF)
+    for half in range(2):
+        for h in range(0, HEADS, 4):
+            starts = [k * head + NOPE + half * HALF for k in range(h, h + 4)]
+            pieces = [values[:, start : start + HALF] for start in starts]
+            first = WIDE + half * TURN + h * HALF
+            q_out[:, pl.ds(first, 4 * HALF)] = jnp.concatenate(pieces, 1).astype(BF)
+    experts = router.shape[1]
+    beside = [
+        router[...].astype(F32),
+        jnp.zeros((rows, ATTN_LANE - experts), F32),
+        gains[...].astype(F32).T,
+    ]
+    q_out[:, pl.ds(QUERY, 128)] = jnp.concatenate(beside, 1).astype(BF)
+    low = kv_down[...].astype(F32)
+    gap = jnp.zeros((rows, 128 - HALF), F32)
+    down_out[:, pl.ds(0, RANK)] = kv_down[:, pl.ds(0, RANK)]
+    for half in range(2):
+        first = RANK + half * HALF
+        down_out[:, pl.ds(RANK + half * 128, 128)] = jnp.concatenate(
+            [low[:, first : first + HALF], gap], 1
+        ).astype(BF)
+    up_out[:, pl.ds(0, 2 * WIDE)] = kv_up[...]
+    up_rows, room = kv_up.shape[0], up_out.shape[1] - 2 * WIDE
+    up_out[:, pl.ds(2 * WIDE, room)] = jnp.concatenate(
+        [kv_gain[...].astype(F32).T, jnp.zeros((up_rows, room - 1), F32)], 1
+    ).astype(BF)
+    share = shared_down.shape[0]
+    shared_out[pl.ds(0, share), :] = shared_down[...]
+    left = shared_out.shape[0] - share
+    shared_out[pl.ds(share, left), :] = jnp.zeros((left, D), BF)
+
+
+def prepared(q_weight, kv_down, kv_up, router, gains, kv_gain, shared_down, up_room, room):
+    rows, up_rows = q_weight.shape[0], kv_up.shape[0]
+    vmem = pl.BlockSpec(memory_space=pltpu.VMEM)
+    shapes = [
+        (rows, QUERY + 128), (rows, RANK + 256), (up_rows, 2 * WIDE + up_room), (room, D),
+    ]
+    return pl.pallas_call(
+        prepare_kernel,
+        out_shape=[jax.ShapeDtypeStruct(shape, BF) for shape in shapes],
+        in_specs=[vmem] * 7,
+        out_specs=[vmem] * 4,
+        compiler_params=pltpu.CompilerParams(vmem_limit_bytes=62 * 2**20),
+        name="prepare",
+    )(q_weight, kv_down, kv_up, router, gains, kv_gain, shared_down)
+
+
 def plain_weight_grads(grid, kept, extent):
     me = lax.axis_index("dp")
     peers = grid.size["p"]
@@ -1590,48 +1775,23 @@
     own = (expert_gate[0], expert_up[0], expert_down[0])
 
     rows = q_weight.shape[0]
-    q_heads = q_weight.reshape(rows, HEADS, NOPE + ROPE)
-    beside = jnp.concatenate(
-        [
-            router,
-            jnp.zeros((rows, ATTN_LANE - experts), BF),
-            attn_gain[:, None],
-            ffn_gain[:, None],
-        ],
-        1,
-    )
-    q_sent = jnp.concatenate(
-        [
-            q_heads[:, :, :NOPE].reshape(rows, WIDE),
-            q_heads[:, :, NOPE : NOPE + HALF].reshape(rows, TURN),
-            q_heads[:, :, NOPE + HALF :].reshape(rows, TURN),
-            beside,
-        ],
-        1,
-    )
-    gap = jnp.zeros((rows, 128 - HALF), BF)
-    down_sent = jnp.concatenate(
-        [kv_down[:, : RANK + HALF], gap, kv_down[:, RANK + HALF :], gap], 1
-    )
     up_rows = kv_up.shape[0]
     up_room = 128 * max(1, 16 // up_rows)
-    up_wide = jnp.concatenate(
-        [kv_up, kv_gain[:, None], jnp.zeros((up_rows, up_room - 1), BF)], 1
+    room = 128
+    q_sent, down_sent, up_wide, shared_part = prepared(
+        q_weight,
+        kv_down,
+        kv_up,
+        router,
+        jnp.stack([attn_gain, ffn_gain]),
+        kv_gain[None],
+        shared_down,
+        up_room,
+        room,
     )
     up_sent = up_wide if up_rows % 16 == 0 else up_wide.reshape(16, -1)
 
     share = shared_gate.shape[1] // devices
-    room = -(-share // 128) * 128
-    shared_sent = jnp.concatenate(
-        [
-            jnp.pad(
-                half.reshape(rows, devices, share).transpose(1, 0, 2),
-                ((0, 0), (0, 0), (0, room - share)),
-            )
-            for half in (shared_gate, shared_up)
-        ],
-        2,
-    )
     first, second, third = ("q", "r", "p"), ("q", "p", "r"), ("p", "q", "r")
 
     def columns_of(ref, peer, step):
@@ -1640,7 +1800,7 @@
     def rows_of(ref, peer, step):
         return ref.at[pl.ds(window_start(peer, dp_size, window, eff), window), :]
 
-    gathered, windows = together(
+    gathered, windows, (shared_sent,) = together(
         grid,
         [
             Gather(
@@ -1655,6 +1815,7 @@
                 ],
             ),
             Exchange(grid, own[:2], [columns_of] * 2, [(extent, window)] * 2, (2, 5)),
+            SharedColumns([shared_gate, shared_up], devices),
         ],
         0,
         "gather_attention",
@@ -1696,10 +1857,9 @@
         6,
         "attention_forward",
     )
-    hidden, dense_gates, residual = saved[0], saved[1], saved[11]
+    hidden, dense_gates = saved[0], saved[1]
 
     shared_in = shared_in.reshape(D, 2 * room)
-    shared_part = jnp.pad(shared_down, ((0, room - share), (0, 0)))
 
     half = D // 2
     capacity = capacity_for(experts)
@@ -1790,7 +1950,7 @@
         weight_grads = plain_weight_grads(grid, kept_of(done), extent)
     hidden_sum = jnp.concatenate([entry[0] for entry in sums], 0)
     gate_grad = jnp.concatenate([entry[1] for entry in sums], 1)
-    result = residual + jnp.concatenate([entry[2] for entry in sums], 0)
+    out_sums = [entry[2] for entry in sums]
     own_ab, own_down, sent_ab, sent_down, shared_in_grad, shared_down_grad = weight_grads
 
     def sent_to(ref, peer, step):
@@ -1800,7 +1960,7 @@
         grid,
         [
             AttentionBackward(
-                grad_out, hidden_sum, gate_grad, saved, token_rows, tables, weights
+                grad_out, hidden_sum, gate_grad, out_sums, saved, token_rows, tables, weights
             ),
             Exchange(
                 grid,
@@ -1813,7 +1973,9 @@
         7,
         "attention_backward",
     )
-    out_weight_grad, kv_up_grad, q_weight_grad, kv_down_grad, tokens_grad = attention_grads
+    (
+        out_weight_grad, kv_up_grad, q_weight_grad, kv_down_grad, tokens_grad, result,
+    ) = attention_grads
     shared_down_grad = shared_down_grad[:share]
 
     def halves(a, columns):
@@ -1832,7 +1994,7 @@
         + halves(1, down_sent.shape[1])
         + halves(2, up_sent.shape[1])
         + halves(3, out_weight.shape[1]),
-        [[3], [2, 1], [0]],
+        [[0], [3], [2], [1]],
     )
     experts_grads = Assemble(
         grid,
@@ -1842,43 +2004,45 @@
         [got_down[step] for step in range(dp_size - 1)],
         eff,
     )
-    (q_sum, down_sum, up_sum, out_weight_sum), experts_grads = together(
-        grid, [attention_sums, experts_grads], 5, "scatter_attention_assemble"
+    (
+        (q_sum, down_sum, up_sum, out_weight_sum), experts_grads,
+        (shared_gate_grad, shared_up_grad),
+    ) = together(
+        grid,
+        [attention_sums, experts_grads, SharedRows(shared_back, shared_gate.shape[1])],
+        5,
+        "scatter_attention_assemble",
     )
-    up_sum = up_sum.reshape(up_rows, -1)
-    beside_sum = q_sum[:, QUERY:]
-    q_sum = jnp.concatenate(
-        [
-            q_sum[:, :WIDE].reshape(rows, HEADS, NOPE),
-            q_sum[:, WIDE : WIDE + TURN].reshape(rows, HEADS, HALF),
-            q_sum[:, WIDE + TURN : QUERY].reshape(rows, HEADS, HALF),
-        ],
-        2,
-    ).reshape(q_weight.shape)
-    down_sum = jnp.concatenate(
-        [down_sum[:, : RANK + HALF], down_sum[:, RANK + 128 : RANK + 128 + HALF]], 1
-    )
-
-    shared_back = shared_back.astype(F32).transpose(1, 0, 2)
-    shared_gate_grad = shared_back[:, :, :share].reshape(shared_gate.shape)
-    shared_up_grad = shared_back[:, :, room : room + share].reshape(shared_up.shape)
-    return (
-        result.astype(BF).reshape(tokens.shape),
-        tokens_grad.reshape(tokens.shape),
-        beside_sum[:, ATTN_LANE],
+    (
+        q_grad, down_grad, up_grad, gain_grads, kv_gain_grad, router_grad, result, tokens_grad,
+        out_weight_grad, shared_gate_grad, shared_up_grad, gate_grad, expert_up_grad,
+        expert_down_grad,
+    ) = finished(
         q_sum,
         down_sum,
-        up_sum[:, 2 * WIDE],
-        up_sum[:, : 2 * WIDE],
-        out_weight_sum,
-        beside_sum[:, FFN_LANE],
-        beside_sum[:, :experts],
+        up_sum.reshape(up_rows, -1),
+        [
+            result, tokens_grad, out_weight_sum, shared_gate_grad, shared_up_grad, *experts_grads,
+        ],
+        experts,
+    )
+    return (
+        result.reshape(tokens.shape),
+        tokens_grad.reshape(tokens.shape),
+        gain_grads[0],
+        q_grad,
+        down_grad,
+        kv_gain_grad[0],
+        up_grad,
+        out_weight_grad,
+        gain_grads[1],
+        router_grad.T,
         shared_gate_grad,
         shared_up_grad,
         shared_down_grad,
-        experts_grads[0][None],
-        experts_grads[1][None],
-        experts_grads[2][None],
+        gate_grad[None],
+        expert_up_grad[None],
+        expert_down_grad[None],
     )
 
 

time: 913 us -> 874 us (0.957)
  local copies, waits for them, and re-layouts: 58.2 us -> 15.6 us
  Pallas kernels: 829 us -> 841 us
    pallas_call x0 -> x2, Pallas kernels: none -> 19.8 us  [the longest x1 17.3 us: finished(): pl.pallas_call(functools.partial(finish_kernel, len(plain), experts), out...]
    unnamed x38 -> x9, local copies, waits for them, and re-layouts: 19.2 us -> 3.33 us
    slice x15 -> x0, local copies, waits for them, and re-layouts: 12.8 us -> none  [the longest x1 1.84 us: body(): shared_gate_grad = shared_back[:, :, :share].reshape(shared_gate.shape)]
where the time goes in v4:
time: 874 us; the launch traced here: 866 us
  Pallas kernels  841 us (96%)
  local copies, waits for them, and re-layouts  15.6 us (2%)
    pallas_call x8, Pallas kernels, together(): pl.pallas_call(kernel, out_shape=[shape for part in parts for shape in pa...  821 us

profile of v4, /device:TPU:16, one launch (start us, length us, event | category | flops | bytes accessed | tf_op | source)
XLA Modules:
  0.0 866.1 jit_solution(6787823161920790646)
XLA Ops:
  0.7 0.5 broadcast.75
  1.2 1.3 reduce.11
  2.5 0.1 reshape.170
  2.6 1.2 pad_maximum_fusion.2.gains
  3.8 1.4 copy.37.router
  5.2 0.7 fusion.1.refs_3_
  5.9 1.4 copy.36
  7.3 1.9 slice_bitcast_fusion
  9.2 2.5 prepare.1
  11.7 137.5 %gather_attention.1 = (bf16[32,64,3200]{2,1,0:T(8,128)(2,1)}, bf16[32,64,768]{2,1,0:T(8,128)(2,1)}, bf16[32,16,4224]{2,1,0:T(8,128)(2,1)}, bf16[32,64,2048]{2,1,...) custom-call(bf16[64,3200]{1,0:T(8,128)(2,1)} %get-tuple-element.109.refs, ...), custom_call_target="tpu_custom_call" | custom-call | tf_op jit(solution)/shard_map/gather_attention/pallas_call | solution.py:520
  149.2 81.0 %attention_forward.1 = (bf16[32,64,2048]{2,1,0:T(8,128)(2,1)}, bf16[128,2048]{1,0:T(8,128)(2,1)}, f32[16,128]{1,0:T(8,128)}, bf16[128,2048]{1,0:T(8,128)(2,1)}, ...) custom-call(bf16[64,2048]{1,0:T(8,128)(2,1)} %get-tuple-element.221., ...), custom_call_target="tpu_custom_call" | custom-call | tf_op jit(solution)/shard_map/attention_forward/pallas_call | solution.py:520
  230.2 1.4 fusion.5
  231.6 1.9 fusion.4
  233.5 46.4 %gather_first.1 = (bf16[32,64,2048]{2,1,0:T(8,128)(2,1)}, f32[32,16,64]{2,1,0:T(8,128)}) custom-call(bf16[64,2048]{1,0:T(8,128)(2,1)} %get-tuple-element.218.refs_0_, f32[16,64]{1,0:T(8,128)} %get-tuple-element.222.refs_1_), custom_call_target="tpu_custom_call" | custom-call | tf_op jit(solution)/shard_map/gather_first/pallas_call | solution.py:520
  279.9 1.0 dynamic-slice_reduce_fusion.1
  280.8 0.7 reshape.177.refs_5_
  281.5 95.5 %gather_second_experts_first.1 = (bf16[32,64,2048]{2,1,0:T(8,128)(2,1)}, f32[32,16,64]{2,1,0:T(8,128)}, bf16[32,64,2048]{2,1,0:T(8,128)(2,1)}, bf16[2048,2048]{1...) custom-call(bf16[64,2048]{1,0:T(8,128)(2,1)} %get-tuple-element.219., ...), custom_call_target="tpu_custom_call" | custom-call | tf_op jit(solution)/shard_map/gather_second_experts_first/pallas_call | solution.py:520
  377.0 1.0 dynamic-slice_reduce_fusion
  378.0 0.7 reshape.183.refs_5_
  378.6 0.8 broadcast_in_dim.52
  379.4 0.8 broadcast_select_fusion.1.refs_1_
  380.2 97.6 %scatter_first_experts_second.1 = (f32[64,2048]{1,0:T(8,128)}, f32[16,64]{1,0:T(8,128)}, f32[64,2048]{1,0:T(8,128)}, bf16[2048,2048]{1,0:T(8,128)(2,1)}, bf16[20...) custom-call(bf16[32,64,2048]{2,1,0:T(8,128)(2,1)} %bitcast.76, ...), custom_call_target="tpu_custom_call" | custom-call | tf_op jit(solution)/shard_map/scatter_first_experts_second/pallas_call | solution.py:520
  477.8 0.8 broadcast_in_dim.55
  478.6 0.8 broadcast_select_fusion.refs_1_
  479.4 101.1 %scatter_second_weight_grads.1 = (f32[64,2048]{1,0:T(8,128)}, f32[16,64]{1,0:T(8,128)}, f32[64,2048]{1,0:T(8,128)}, f32[1024,1536]{1,0:T(8,128)}, f32[768,1024]{...) custom-call(bf16[32,64,2048]{2,1,0:T(8,128)(2,1)} %bitcast.74, ...), custom_call_target="tpu_custom_call" | custom-call | tf_op jit(solution)/shard_map/scatter_second_weight_grads/pallas_call | solution.py:520
  580.5 2.1 pad_maximum_fusion.refs_1_
  582.6 1.4 pad_maximum_fusion.1.refs_2_
  584.0 124.2 %attention_backward.1 = (bf16[2048,2048]{1,0:T(8,128)(2,1)}, bf16[512,4224]{1,0:T(8,128)(2,1)}, bf16[2048,3200]{1,0:T(8,128)(2,1)}, bf16[2048,768]{1,0:T(8,128)(...) custom-call(bf16[128,2048]{1,0:T(8,128)(2,1)} %bitcast.86, ...), custom_call_target="tpu_custom_call" | custom-call | tf_op jit(solution)/shard_map/attention_backward/pallas_call | solution.py:520
  708.2 138.1 %scatter_attention_assemble.1 = (f32[64,3200]{1,0:T(8,128)}, f32[64,768]{1,0:T(8,128)}, f32[16,4224]{1,0:T(8,128)}, f32[64,2048]{1,0:T(8,128)}, f32[1024,1408]{1...) custom-call(bf16[32,64,3200]{2,1,0:T(8,128)(2,1)} %bitcast.71, ...), custom_call_target="tpu_custom_call" | custom-call | tf_op jit(solution)/shard_map/scatter_attention_assemble/pallas_call | solution.py:520
  846.4 17.3 %finish.1 = (f32[64,3072]{1,0:T(8,128)}, f32[64,576]{1,0:T(8,128)}, f32[16,4096]{1,0:T(8,128)}, f32[2,64]{1,0:T(2,128)}, f32[1,16]{1,0:T(1,128)}, /*index=5*/f32...) custom-call(f32[64,3200]{1,0:T(8,128)} %get-tuple-element.176.refs_0, ...), custom_call_target="tpu_custom_call" | custom-call | tf_op jit(solution)/shard_map/finish/pallas_call | solution.py:1656
  863.7 1.3 slice_bitcast_fusion.2
  865.0 0.9 slice.43
  (8 shorter events, 0.0 us)
Async XLA Ops:
  479.4 101.2 %copy-start = (f32[64,2048]{1,0:T(8,128)S(1)}, f32[64,2048]{1,0:T(8,128)}, u32[]{:S(2)}) copy-start(f32[64,2048]{1,0:T(8,128)} %get-tuple-element.133) | copy-start | bytes 1572868
  479.4 103.3 %copy-start.2 = (f32[16,64]{1,0:T(8,128)S(1)}, f32[16,64]{1,0:T(8,128)}, u32[]{:S(2)}) copy-start(f32[16,64]{1,0:T(8,128)} %get-tuple-element.150) | copy-start | bytes 12292
  846.4 18.6 %copy-start.1 = (f32[128,2048]{1,0:T(8,128)S(1)}, f32[128,2048]{1,0:T(8,128)}, u32[]{:S(2)}) copy-start(f32[128,2048]{1,0:T(8,128)} %get-tuple-element.198) | copy-start | bytes 3145732

commit v5 on v4

--- a/solution.py
+++ b/solution.py
@@ -272,8 +272,9 @@
 
 
 class Scatter:
-    def __init__(self, grid, arrays, items, rounds):
+    def __init__(self, grid, arrays, items, rounds, windows=None):
         count = len(items)
+        self.windows = windows or [(n, 0, a.shape[2]) for n, a in enumerate(arrays)]
         chips = grid.devices // 2
         q_size = grid.size["q"]
         self.grid, self.items, self.rounds = grid, items, rounds
@@ -281,19 +282,20 @@
         self.in_specs = [pl.BlockSpec(memory_space=pl.ANY)] * len(arrays)
         self.out_shapes = [jax.ShapeDtypeStruct(a.shape[1:], F32) for a in arrays]
         self.out_specs = [pl.BlockSpec(memory_space=pltpu.VMEM)] * len(arrays)
-        scratch = [pltpu.VMEM((chips,) + a.shape[1:], a.dtype) for a in arrays]
-        scratch += [pltpu.VMEM((2 * AHEAD,) + a.shape[1:], a.dtype) for a in arrays]
+        blocks = [((arrays[n].shape[1], width), arrays[n].dtype) for n, _, width in self.windows]
+        scratch = [pltpu.VMEM((chips,) + shape, kind) for shape, kind in blocks]
+        scratch += [pltpu.VMEM((2 * AHEAD,) + shape, kind) for shape, kind in blocks]
         most = 0
         for a, _, width, order in items:
             n1, n2 = (grid.size[axis] for axis in order)
             shares = ((n1 - 1) * n2 * q_size, (n2 - 1) * q_size, q_size)
             most = max(most, shares[0] + shares[1])
             for share in shares:
-                scratch.append(pltpu.VMEM((share, arrays[a].shape[1], width), arrays[a].dtype))
+                scratch.append(pltpu.VMEM((share, blocks[a][0][0], width), blocks[a][1]))
         self.scratch = scratch + [
-            pltpu.SemaphoreType.DMA((len(arrays), chips)),
-            pltpu.SemaphoreType.DMA((len(arrays), chips)),
-            pltpu.SemaphoreType.DMA((len(arrays), chips)),
+            pltpu.SemaphoreType.DMA((len(blocks), chips)),
+            pltpu.SemaphoreType.DMA((len(blocks), chips)),
+            pltpu.SemaphoreType.DMA((len(blocks), chips)),
             pltpu.SemaphoreType.DMA((count, most)),
             pltpu.SemaphoreType.DMA((count, most)),
             pltpu.SemaphoreType.DMA((count, q_size)),
@@ -302,7 +304,7 @@
 
     def steps(self, at, ins, outs, scratch):
         grid, items = self.grid, self.items
-        count, arrays = len(items), len(ins)
+        count, arrays = len(items), len(self.windows)
         held, crossed = scratch[:arrays], scratch[arrays : 2 * arrays]
         landing = scratch[2 * arrays : 2 * arrays + 3 * count]
         load_sem, core_send, core_recv, send_sem, recv_sem, line_send, line_recv = scratch[
@@ -330,9 +332,13 @@
         blocks = [(n, block) for n in range(len(self.rounds)) for block in near_blocks]
         round_of = {a: n for n, members in enumerate(self.rounds) for a in members}
 
+        def source(a, number):
+            array, first, width = self.windows[a]
+            return ins[array].at[number, :, pl.ds(first, width)]
+
         def load(a, block):
             return pltpu.make_async_copy(
-                ins[a].at[owner(at, block)], held[a].at[flat(block)], load_sem.at[a, flat(block)]
+                source(a, owner(at, block)), held[a].at[flat(block)], load_sem.at[a, flat(block)]
             )
 
         def crossed_at(a, block):
@@ -340,7 +346,7 @@
 
         def across(a, block):
             return pltpu.make_async_remote_copy(
-                src_ref=ins[a].at[owner(sibling, block)],
+                src_ref=source(a, owner(sibling, block)),
                 dst_ref=crossed_at(a, block),
                 send_sem=core_send.at[a, flat(block)],
                 recv_sem=core_recv.at[a, flat(block)],
@@ -426,11 +432,12 @@
             a, first, width, _ = items[i]
             parts = [held[a].at[at["q"], :, pl.ds(first, width)]]
             for step in range(1, q_size):
-                source = lax.rem(at["q"] + step, q_size)
-                view = landing[3 * i + 2].at[source]
-                pltpu.make_async_copy(view, view, line_recv.at[i, source]).wait()
+                back = lax.rem(at["q"] + step, q_size)
+                view = landing[3 * i + 2].at[back]
+                pltpu.make_async_copy(view, view, line_recv.at[i, back]).wait()
                 parts.append(view)
-            add_rows(outs[a].at[:, pl.ds(first, width)], *parts)
+            array, window_first, _ = self.windows[a]
+            add_rows(outs[array].at[:, pl.ds(window_first + first, width)], *parts)
 
         ticks = []
         for n, members in enumerate(self.rounds):
@@ -1439,7 +1446,7 @@
             result = scratch[4 * job + (2 if wide else 3)].at[turn % 2]
             left = self.jobs[job][2]
 
-            @tiles(resident.shape[2], 256)
+            @tiles(resident.shape[2], resident.shape[2])
             def _(columns):
                 total = None
                 for c in range(chunks):
@@ -1800,7 +1807,7 @@
     def rows_of(ref, peer, step):
         return ref.at[pl.ds(window_start(peer, dp_size, window, eff), window), :]
 
-    gathered, windows, (shared_sent,) = together(
+    gathered, windows_in, (shared_sent,) = together(
         grid,
         [
             Gather(
@@ -1864,7 +1871,7 @@
     half = D // 2
     capacity = capacity_for(experts)
     expert = lax.axis_index("expert")
-    own_weights = (own, (*windows, *windows_down), shared_in, shared_part)
+    own_weights = (own, (*windows_in, *windows_down), shared_in, shared_part)
 
     def gather_of(chunk):
         piece = slice(chunk * SEQ, (chunk + 1) * SEQ)
@@ -1903,7 +1910,6 @@
 
     over = [(0, 0, half, ("p", "r")), (0, half, half, ("r", "p"))]
     over_gates = [(1, 0, SEQ, ("p", "r"))]
-    over_out = [(2, 0, half, ("p", "r")), (2, half, half, ("r", "p"))]
     if devices <= 32:
         (gathered,) = together(grid, [gather_of(0)], 1, "gather_first")
         gathered, done_0 = together(
@@ -1912,10 +1918,13 @@
             2,
             "gather_second_experts_first",
         )
-        everything = over + over_gates + over_out
+        windows = [(0, 0, D), (1, 0, SEQ), (2, 0, half), (2, half, half)]
+        everything = over + over_gates
+        for a in (2, 3):
+            everything += [(a, 0, half // 2, ("p", "r")), (a, half // 2, half // 2, ("r", "p"))]
         sums_0, done_1 = together(
             grid,
-            [Scatter(grid, sums_of(done_0), everything, [[0, 1], [2]]), experts_of(*gathered)],
+            [Scatter(grid, sums_of(done_0), everything, [[0, 1], [2], [3]], windows), experts_of(*gathered)],
             3,
             "scatter_first_experts_second",
         )
@@ -1923,7 +1932,7 @@
         sums_1, weight_grads = together(
             grid,
             [
-                Scatter(grid, sums_of(done_1), everything, [[0, 1], [2]]),
+                Scatter(grid, sums_of(done_1), everything, [[0, 1], [2], [3]], windows),
                 WeightGrads(grid, kept, extent),
             ],
             4,

time: 874 us -> 863 us (0.987)
  Pallas kernels: 841 us -> 829 us
    pallas_call x8, Pallas kernels: 821 us -> 809 us  [together(): pl.pallas_call(kernel, out_shape=[shape for part in parts for shape in pa...]
where the time goes in v5:
time: 863 us; the launch traced here: 854 us
  Pallas kernels  829 us (96%)
  local copies, waits for them, and re-layouts  15.6 us (2%)
    pallas_call x8, Pallas kernels, together(): pl.pallas_call(kernel, out_shape=[shape for part in parts for shape in pa...  809 us
    pallas_call x1, Pallas kernels, finished(): pl.pallas_call(functools.partial(finish_kernel, len(plain), experts), out...  17.3 us

profile of v5, /device:TPU:16, one launch (start us, length us, event | category | flops | bytes accessed | tf_op | source)
XLA Modules:
  0.0 854.1 jit_solution(6514402367307485088)
XLA Ops:
  0.7 0.5 broadcast.75
  1.2 1.3 reduce.11
  2.5 0.1 reshape.170
  2.6 1.2 pad_maximum_fusion.2.gains
  3.8 1.4 copy.37.router
  5.2 0.7 fusion.1.refs_3_
  5.9 1.4 copy.36
  7.3 1.9 slice_bitcast_fusion
  9.2 2.5 prepare.1
  11.7 137.5 %gather_attention.1 = (bf16[32,64,3200]{2,1,0:T(8,128)(2,1)}, bf16[32,64,768]{2,1,0:T(8,128)(2,1)}, bf16[32,16,4224]{2,1,0:T(8,128)(2,1)}, bf16[32,64,2048]{2,1,...) custom-call(bf16[64,3200]{1,0:T(8,128)(2,1)} %get-tuple-element.109.refs, ...), custom_call_target="tpu_custom_call" | custom-call | tf_op jit(solution)/shard_map/gather_attention/pallas_call | solution.py:527
  149.2 81.0 %attention_forward.1 = (bf16[32,64,2048]{2,1,0:T(8,128)(2,1)}, bf16[128,2048]{1,0:T(8,128)(2,1)}, f32[16,128]{1,0:T(8,128)}, bf16[128,2048]{1,0:T(8,128)(2,1)}, ...) custom-call(bf16[64,2048]{1,0:T(8,128)(2,1)} %get-tuple-element.221., ...), custom_call_target="tpu_custom_call" | custom-call | tf_op jit(solution)/shard_map/attention_forward/pallas_call | solution.py:527
  230.2 1.4 fusion.5
  231.6 1.9 fusion.4
  233.5 46.4 %gather_first.1 = (bf16[32,64,2048]{2,1,0:T(8,128)(2,1)}, f32[32,16,64]{2,1,0:T(8,128)}) custom-call(bf16[64,2048]{1,0:T(8,128)(2,1)} %get-tuple-element.218.refs_0_, f32[16,64]{1,0:T(8,128)} %get-tuple-element.222.refs_1_), custom_call_target="tpu_custom_call" | custom-call | tf_op jit(solution)/shard_map/gather_first/pallas_call | solution.py:527
  279.9 1.0 dynamic-slice_reduce_fusion.1
  280.8 0.7 reshape.177.refs_5_
  281.5 95.3 %gather_second_experts_first.1 = (bf16[32,64,2048]{2,1,0:T(8,128)(2,1)}, f32[32,16,64]{2,1,0:T(8,128)}, bf16[32,64,2048]{2,1,0:T(8,128)(2,1)}, bf16[2048,2048]{1...) custom-call(bf16[64,2048]{1,0:T(8,128)(2,1)} %get-tuple-element.219., ...), custom_call_target="tpu_custom_call" | custom-call | tf_op jit(solution)/shard_map/gather_second_experts_first/pallas_call | solution.py:527
  376.8 1.0 dynamic-slice_reduce_fusion
  377.8 0.7 reshape.183.refs_5_
  378.5 0.8 broadcast_in_dim.52
  379.2 0.8 broadcast_select_fusion.1.refs_1_
  380.0 95.7 %scatter_first_experts_second.1 = (f32[64,2048]{1,0:T(8,128)}, f32[16,64]{1,0:T(8,128)}, f32[64,2048]{1,0:T(8,128)}, bf16[2048,2048]{1,0:T(8,128)(2,1)}, bf16[20...) custom-call(bf16[32,64,2048]{2,1,0:T(8,128)(2,1)} %bitcast.76, ...), custom_call_target="tpu_custom_call" | custom-call | tf_op jit(solution)/shard_map/scatter_first_experts_second/pallas_call | solution.py:527
  475.8 0.8 broadcast_in_dim.55
  476.5 0.8 broadcast_select_fusion.refs_1_
  477.3 91.3 %scatter_second_weight_grads.1 = (f32[64,2048]{1,0:T(8,128)}, f32[16,64]{1,0:T(8,128)}, f32[64,2048]{1,0:T(8,128)}, f32[1024,1536]{1,0:T(8,128)}, f32[768,1024]{...) custom-call(bf16[32,64,2048]{2,1,0:T(8,128)(2,1)} %bitcast.74, ...), custom_call_target="tpu_custom_call" | custom-call | tf_op jit(solution)/shard_map/scatter_second_weight_grads/pallas_call | solution.py:527
  568.6 2.1 pad_maximum_fusion.refs_1_
  570.7 1.4 pad_maximum_fusion.1.refs_2_
  572.1 124.4 %attention_backward.1 = (bf16[2048,2048]{1,0:T(8,128)(2,1)}, bf16[512,4224]{1,0:T(8,128)(2,1)}, bf16[2048,3200]{1,0:T(8,128)(2,1)}, bf16[2048,768]{1,0:T(8,128)(...) custom-call(bf16[128,2048]{1,0:T(8,128)(2,1)} %bitcast.86, ...), custom_call_target="tpu_custom_call" | custom-call | tf_op jit(solution)/shard_map/attention_backward/pallas_call | solution.py:527
  696.5 137.9 %scatter_attention_assemble.1 = (f32[64,3200]{1,0:T(8,128)}, f32[64,768]{1,0:T(8,128)}, f32[16,4224]{1,0:T(8,128)}, f32[64,2048]{1,0:T(8,128)}, f32[1024,1408]{1...) custom-call(bf16[32,64,3200]{2,1,0:T(8,128)(2,1)} %bitcast.71, ...), custom_call_target="tpu_custom_call" | custom-call | tf_op jit(solution)/shard_map/scatter_attention_assemble/pallas_call | solution.py:527
  834.4 17.3 %finish.1 = (f32[64,3072]{1,0:T(8,128)}, f32[64,576]{1,0:T(8,128)}, f32[16,4096]{1,0:T(8,128)}, f32[2,64]{1,0:T(2,128)}, f32[1,16]{1,0:T(1,128)}, /*index=5*/f32...) custom-call(f32[64,3200]{1,0:T(8,128)} %get-tuple-element.176.refs_0, ...), custom_call_target="tpu_custom_call" | custom-call | tf_op jit(solution)/shard_map/finish/pallas_call | solution.py:1663
  851.7 1.3 slice_bitcast_fusion.2
  853.0 0.9 slice.43
  (8 shorter events, 0.0 us)
Async XLA Ops:
  477.3 91.3 %copy-start = (f32[64,2048]{1,0:T(8,128)S(1)}, f32[64,2048]{1,0:T(8,128)}, u32[]{:S(2)}) copy-start(f32[64,2048]{1,0:T(8,128)} %get-tuple-element.133) | copy-start | bytes 1572868
  477.3 93.4 %copy-start.2 = (f32[16,64]{1,0:T(8,128)S(1)}, f32[16,64]{1,0:T(8,128)}, u32[]{:S(2)}) copy-start(f32[16,64]{1,0:T(8,128)} %get-tuple-element.150) | copy-start | bytes 12292
  834.4 18.6 %copy-start.1 = (f32[128,2048]{1,0:T(8,128)S(1)}, f32[128,2048]{1,0:T(8,128)}, u32[]{:S(2)}) copy-start(f32[128,2048]{1,0:T(8,128)} %get-tuple-element.198) | copy-start | bytes 3145732
